TPU v7x, 128 devices: a whole 4x4x4 slice. The times are simulated.
128 devices in a mesh: obj: 8 (over z, core), pos: 16 (over y, x).
Axes of the slice: x: 4, y: 4, z: 4, core: 2. Of those that a mesh axis runs over, the one named last changes fastest.
Arguments:
- object_field: float32 [2, 4096, 8192], P(None, 'obj', 'pos'), may hold values from -5 to 5
- probe: float32 [2, 512, 512], replicated, may hold values from -5 to 5
- amplitudes: float32 [128, 512, 512], P(('obj', 'pos')), may hold values from 0.1 to 3
- offsets: int32 [128, 2], P(('obj', 'pos')), may hold values from 0 to 7680, as said below
Outputs:
- new_object: float32 [2, 4096, 8192], P(None, 'obj', 'pos')
- new_probe: float32 [2, 512, 512], replicated
Inputs may be any that keep to these rules, and one draw needn't show every extreme that they name: `offsets`: position k's patch starts in the tile of device k // 1 of obj+pos: its row lies in [o * 512, (o + 1) * 512) and its column in [p * 512, (p + 1) * 512) with o = k // 16 and p = (k) % 16, except that row is at most 3584 and column at most 7680, so every patch lies inside the object.
All inputs are finite; a program needn't handle non-finite values.
Results may differ from a plain program's by a relative error of at most 0.012.
The roundings to bfloat16 on the way count: a program that leaves them out, or rounds other values in their place, can miss the bound.
Values sent between devices are 32-bit elements; how exact they have to be, the bound alone decides.
No kernel may reach another device: no remote copies, remote signals or barrier semaphores. Data moves between devices by JAX's collectives and lax.ppermute only.
A program may use at most 128 MiB of HBM per device.

v0:
```python
import math

import jax
import jax.numpy as jnp
from jax import lax
from jax.sharding import PartitionSpec as P


def shifted(value, axis, steps):
    count = lax.axis_size(axis)
    leading, last = (max(0, -steps), min(count, count - steps))
    return lax.ppermute(value, axis, [(source, source + steps) for source in range(leading, last)])


def dft_tables(size):
    idx = jnp.arange(size, dtype=jnp.int32)
    turns = idx[:, None] * idx[None, :] % size
    angle = turns.astype(jnp.float32) * (2.0 * math.pi / size)
    scale = 1.0 / math.sqrt(size)
    return (
        (jnp.cos(angle) * scale).astype(jnp.bfloat16),
        (-jnp.sin(angle) * scale).astype(jnp.bfloat16),
    )


def right_mul(frames, table):
    return jnp.einsum("prc,ck->prk", frames, table, preferred_element_type=jnp.float32)


def left_mul(table, frames):
    return jnp.einsum("jr,prc->pjc", table, frames, preferred_element_type=jnp.float32)


def fourier_step(patch_real, patch_imag, probe_real, probe_imag, amps, table_re, table_im):
    psi_re = (probe_real * patch_real - probe_imag * patch_imag).astype(jnp.bfloat16)
    psi_im = (probe_real * patch_imag + probe_imag * patch_real).astype(jnp.bfloat16)
    half_re = (right_mul(psi_re, table_re) - right_mul(psi_im, table_im)).astype(jnp.bfloat16)
    half_im = (right_mul(psi_re, table_im) + right_mul(psi_im, table_re)).astype(jnp.bfloat16)
    spec_re = left_mul(table_re, half_re) - left_mul(table_im, half_im)
    spec_im = left_mul(table_re, half_im) + left_mul(table_im, half_re)
    magnitude = jnp.sqrt(spec_re * spec_re + spec_im * spec_im)
    factor = amps / jnp.maximum(magnitude, 0.25) - 1.0
    change_re = (factor * spec_re).astype(jnp.bfloat16)
    change_im = (factor * spec_im).astype(jnp.bfloat16)
    back_re = (left_mul(table_re, change_re) + left_mul(table_im, change_im)).astype(jnp.bfloat16)
    back_im = (left_mul(table_re, change_im) - left_mul(table_im, change_re)).astype(jnp.bfloat16)
    err_re = right_mul(back_re, table_re) + right_mul(back_im, table_im)
    err_im = right_mul(back_im, table_re) - right_mul(back_re, table_im)
    return (err_re, err_im)


def paint(canvas, corners, weights, power):
    frame = power.shape[0]

    def place(step, board):
        row = corners[step, 0]
        col = corners[step, 1]
        block = lax.dynamic_slice(board, (row, col), (frame, frame)) + weights[step] * power
        return lax.dynamic_update_slice(board, block, (row, col))

    return lax.fori_loop(0, corners.shape[0], place, canvas)


def body(object_field, probe, amplitudes, offsets):
    tile = object_field.shape[1]
    frame = probe.shape[1]
    count = offsets.shape[0]
    row_index = lax.axis_index("obj")
    col_index = lax.axis_index("pos")
    below = shifted(object_field, "obj", -1)
    taller = jnp.concatenate([object_field, below], axis=1)
    beside = shifted(taller, "pos", -1)
    extended = jnp.concatenate([taller, beside], axis=2)
    anchor = jnp.stack([row_index * tile, col_index * tile])
    local = offsets - anchor[None, :]

    def cut(corner):
        return lax.dynamic_slice(extended, (jnp.int32(0), corner[0], corner[1]), (2, frame, frame))

    patches = jax.vmap(cut)(local)
    patch_real = patches[:, 0]
    patch_imag = patches[:, 1]
    probe_real = probe[0]
    probe_imag = probe[1]
    power = probe_real * probe_real + probe_imag * probe_imag
    table_re, table_im = dft_tables(frame)
    err_re, err_im = fourier_step(
        patch_real, patch_imag, probe_real, probe_imag, amplitudes, table_re, table_im
    )
    grad_re = probe_real * err_re + probe_imag * err_im
    grad_im = probe_real * err_im - probe_imag * err_re
    span = tile + frame

    def place_grad(step, board):
        row = local[step, 0]
        col = local[step, 1]
        zero = jnp.int32(0)
        block = lax.dynamic_slice(board, (zero, row, col), (2, frame, frame))
        block = block + jnp.stack([grad_re[step], grad_im[step]])
        return lax.dynamic_update_slice(board, block, (zero, row, col))

    numer = lax.fori_loop(0, count, place_grad, jnp.zeros((2, span, span), jnp.float32))
    light = paint(
        jnp.zeros((span, span), jnp.float32), local, jnp.ones((count,), jnp.float32), power
    )
    moved_numer, moved_light = shifted((numer[:, :, tile:], light[:, tile:]), "pos", 1)
    numer = numer.at[:, :, :frame].add(moved_numer)
    light = light.at[:, :frame].add(moved_light)
    down_numer, down_light = shifted((numer[:, tile:, :tile], light[tile:, :tile]), "obj", 1)
    numer_tile = numer[:, :tile, :tile].at[:, :frame, :].add(down_numer)
    light_tile = light[:tile, :tile].at[:frame, :].add(down_light)
    new_object = object_field + numer_tile / (light_tile + 1.0)
    probe_numer = jnp.stack(
        [
            jnp.sum(patch_real * err_re + patch_imag * err_im, axis=0),
            jnp.sum(patch_real * err_im - patch_imag * err_re, axis=0),
        ]
    )
    probe_light = jnp.sum(patch_real * patch_real + patch_imag * patch_imag, axis=0)
    total_positions = count * lax.axis_size("obj") * lax.axis_size("pos")
    beta = 0.5 * math.sqrt(total_positions)
    total_numer, total_light = lax.psum((probe_numer, probe_light), ("obj", "pos"))
    new_probe = probe + beta * total_numer / (total_light + 1.0)
    return (new_object, new_probe)


def solution(mesh):
    in_specs = (P(None, "obj", "pos"), P(), P(("obj", "pos"), None, None), P(("obj", "pos"), None))
    out_specs = (P(None, "obj", "pos"), P())
    return jax.shard_map(body, mesh=mesh, in_specs=in_specs, out_specs=out_specs, check_vma=False)
```

profile of v0, /device:TPU:1, one launch (start us, length us, event | category | flops | bytes accessed | tf_op | source)
XLA Modules:
  0.0 443.0 jit_solution(11327608872810559209)
XLA Ops:
  13.6 22.8 %collective-permute-done = f32[2,512,512]{2,1,0:T(8,128)S(1)} collective-permute-done((f32[2,512,512]{2,1,0:T(8,128)}, f32[2,512,512]{2,1,0:T(8,128)S(1)}, u32[]{:S(2)}, u32[]{:S(2)}) %collective-permute-start) | collective-permute-done | bytes 2097184 | tf_op jit(solution)/shard_map/ppermute | solution.py:12
  49.4 62.0 %collective-permute-done.1 = f32[2,1024,512]{2,1,0:T(8,128)} collective-permute-done((f32[2,1024,512]{2,1,0:T(8,128)}, f32[2,1024,512]{2,1,0:T(8,128)}, u32[]{:S(2)}, u32[]{:S(2)}) %collective-permute-start.1) | collective-permute-done | bytes 4194336 | tf_op jit(solution)/shard_map/ppermute | solution.py:12
  115.8 5.4 %fusion.43 = f32[512,512]{1,0:T(8,128)S(1)} fusion(bf16[512,512]{1,0:T(8,128)(2,1)S(1)} %get-tuple-element.117), kind=kOutput, calls=%fused_computation.84 | convolution fusion | flops 272891904 | bytes 1572864 | tf_op jit(solution)/shard_map/prc,ck->prk/dot_general | solution.py:27
  121.2 4.9 %fusion.42 = f32[512,512]{1,0:T(8,128)S(1)} fusion(bf16[512,512]{1,0:T(8,128)(2,1)S(1)} %get-tuple-element.117), kind=kOutput, calls=%fused_computation.83 | convolution fusion | flops 272629760 | bytes 1572864 | tf_op jit(solution)/shard_map/prc,ck->prk/dot_general | solution.py:27
  126.1 5.0 %fusion.7 = bf16[512,512]{1,0:T(8,128)(2,1)S(1)} fusion(f32[512,512]{1,0:T(8,128)S(1)} %fusion.43, bf16[512,512]{1,0:T(8,128)(2,1)S(1)} %get-tuple-element.116), kind=kOutput, calls=%fused_computation.26 | convolution fusion | flops 273154048 | bytes 2097152 | tf_op jit(solution)/shard_map/prc,ck->prk/dot_general | solution.py:27
  131.1 5.0 %fusion.6 = bf16[512,512]{1,0:T(8,128)(2,1)S(1)} fusion(f32[512,512]{1,0:T(8,128)S(1)} %fusion.42, bf16[512,512]{1,0:T(8,128)(2,1)S(1)} %get-tuple-element.116), kind=kOutput, calls=%fused_computation.25 | convolution fusion | flops 273416192 | bytes 2097152 | tf_op jit(solution)/shard_map/prc,ck->prk/dot_general | solution.py:27
  136.1 5.0 %fusion.41 = f32[512,512]{1,0:T(8,128)S(1)} fusion(bf16[512,512]{1,0:T(8,128)(2,1)S(1)} %fusion.6), kind=kOutput, calls=%fused_computation.82 | convolution fusion | flops 272629760 | bytes 1572864 | tf_op jit(solution)/shard_map/jr,prc->pjc/dot_general | solution.py:31
  141.2 5.0 %fusion.40 = f32[512,512]{1,0:T(8,128)S(1)} fusion(bf16[512,512]{1,0:T(8,128)(2,1)S(1)} %fusion.7), kind=kOutput, calls=%fused_computation.81 | convolution fusion | flops 272629760 | bytes 1572864 | tf_op jit(solution)/shard_map/jr,prc->pjc/dot_general | solution.py:31
  146.2 5.4 %fusion.4 = f32[1,512,512]{1,2,0:T(8,128)S(1)} fusion(f32[512,512]{1,0:T(8,128)S(1)} %fusion.40, bf16[512,512]{1,0:T(8,128)(2,1)S(1)} %fusion.6), kind=kOutput, calls=%fused_computation.20 | convolution fusion | flops 273154048 | bytes 2621440 | tf_op jit(solution)/shard_map/jr,prc->pjc/dot_general | solution.py:31
  151.6 5.3 %multiply_convert_fusion.1 = (bf16[1,512,512]{1,2,0:T(8,128)(2,1)S(1)}, bf16[1,512,512]{1,2,0:T(8,128)(2,1)S(1)}) fusion(f32[1,512,512]{1,2,0:T(8,128)S(1)} %copy-done.13, f32[1,512,512]{1,2,0:T(8,128)S(1)} %fusion.4, f32[512,512]{1,0:T(8,128)S(1)} %fusion.41, bf16[512,512]{1,0:T(8,128)(2,1)S(1)} %fusion.7), kind=kOutput, calls=%fused_computation.63 | convolution fusion | flops 275775488 | bytes 4718592 | tf_op jit(solution)/shard_map/jr,prc->pjc/dot_general | solution.py:31
  156.8 4.9 %fusion.36 = f32[512,512]{1,0:T(8,128)S(1)} fusion(bf16[1,512,512]{1,2,0:T(8,128)(2,1)S(1)} %get-tuple-element.118), kind=kOutput, calls=%fused_computation.76 | convolution fusion | flops 272629760 | bytes 1572864 | tf_op jit(solution)/shard_map/jr,prc->pjc/dot_general | solution.py:31
  166.6 5.0 %fusion.11 = bf16[512,512]{0,1:T(8,128)(2,1)S(1)} fusion(f32[512,512]{1,0:T(8,128)S(1)} %fusion.36, bf16[1,512,512]{1,2,0:T(8,128)(2,1)S(1)} %get-tuple-element.119), kind=kOutput, calls=%fused_computation.30 | convolution fusion | flops 273416192 | bytes 2097152 | tf_op jit(solution)/shard_map/jr,prc->pjc/dot_general | solution.py:31
  171.6 5.0 %fusion.10 = bf16[512,512]{0,1:T(8,128)(2,1)S(1)} fusion(f32[512,512]{1,0:T(8,128)S(1)} %fusion.32, bf16[1,512,512]{1,2,0:T(8,128)(2,1)S(1)} %get-tuple-element.118), kind=kOutput, calls=%fused_computation.29 | convolution fusion | flops 273416192 | bytes 2097152 | tf_op jit(solution)/shard_map/jr,prc->pjc/dot_general | solution.py:31
  176.6 5.2 %fusion.38 = f32[512,512]{1,0:T(8,128)S(1)} fusion(bf16[512,512]{0,1:T(8,128)(2,1)S(1)} %fusion.10), kind=kOutput, calls=%fused_computation.79 | convolution fusion | flops 272629760 | bytes 1572864 | tf_op jit(solution)/shard_map/prc,ck->prk/dot_general | solution.py:27
  181.9 5.0 %fusion.39 = f32[512,512]{1,0:T(8,128)S(1)} fusion(bf16[512,512]{0,1:T(8,128)(2,1)S(1)} %fusion.11), kind=kOutput, calls=%fused_computation.80 | convolution fusion | flops 272629760 | bytes 1572864 | tf_op jit(solution)/shard_map/prc,ck->prk/dot_general | solution.py:27
  186.9 5.2 %convolution_subtract_fusion = f32[512,512]{1,0:T(8,128)S(1)} fusion(f32[512,512]{1,0:T(8,128)S(1)} %fusion.38, bf16[512,512]{0,1:T(8,128)(2,1)S(1)} %fusion.11), kind=kOutput, calls=%fused_computation.15 | convolution fusion | flops 273154048 | bytes 2621440 | tf_op jit(solution)/shard_map/prc,ck->prk/dot_general | solution.py:27
  192.1 5.2 %convolution_add_fusion = f32[512,512]{1,0:T(8,128)S(1)} fusion(f32[512,512]{1,0:T(8,128)S(1)} %fusion.39, bf16[512,512]{0,1:T(8,128)(2,1)S(1)} %fusion.10), kind=kOutput, calls=%fused_computation.16 | convolution fusion | flops 273154048 | bytes 2621440 | tf_op jit(solution)/shard_map/prc,ck->prk/dot_general | solution.py:27
  204.6 14.9 %dynamic_update_slice.8 = f32[2,1024,1024]{2,1,0:T(8,128)} dynamic-update-slice(f32[2,1024,1024]{2,1,0:T(8,128)} %broadcast_in_dim.19, f32[2,512,512]{2,1,0:T(8,128)} %pad_maximum_fusion, s32[]{:T(128)} %constant.174.clone.1, s32[]{:T(128)S(6)} %select_n.70, s32[]{:T(128)S(6)} %select_n.71) | dynamic-update-slice | bytes 4194308 | tf_op jit(solution)/shard_map/while/body/eval_jaxpr/dynamic_update_slice | solution.py:100
  224.1 5.2 %collective-permute-start.2 = (f32[2,1024,512]{2,1,0:T(8,128)}, f32[2,1024,512]{2,1,0:T(8,128)}, u32[]{:S(2)}, u32[]{:S(2)}) collective-permute-start(f32[2,1024,512]{2,1,0:T(8,128)} %slice.152), channel_id=1, source_target_pairs={{0,1},{1,2},{2,3},{3,4},{4,5},{5,6},{6,7},{7,8},{8,9},{9,10},{10,1... | collective-permute-start | bytes 12582920 | tf_op jit(solution)/shard_map/ppermute | solution.py:12
  231.8 8.3 %dynamic_update_slice.9 = f32[1024,1024]{1,0:T(8,128)} dynamic-update-slice(f32[1024,1024]{1,0:T(8,128)} %broadcast_in_dim.23, f32[512,512]{1,0:T(8,128)} %get-tuple-element.121, s32[]{:T(128)S(6)} %select_n.70, s32[]{:T(128)S(6)} %select_n.71) | dynamic-update-slice | bytes 2097156 | tf_op jit(solution)/shard_map/while/body/eval_jaxpr/dynamic_update_slice | solution.py:59
  249.1 74.9 %collective-permute-done.2 = f32[2,1024,512]{2,1,0:T(8,128)} collective-permute-done((f32[2,1024,512]{2,1,0:T(8,128)}, f32[2,1024,512]{2,1,0:T(8,128)}, u32[]{:S(2)}, u32[]{:S(2)}) %collective-permute-start.2) | collective-permute-done | bytes 4194336 | tf_op jit(solution)/shard_map/ppermute | solution.py:12
  331.7 23.7 %collective-permute-start.3 = (f32[2,512,512]{2,1,0:T(8,128)}, f32[2,512,512]{2,1,0:T(8,128)}, u32[]{:S(2)}, u32[]{:S(2)}) collective-permute-start(f32[2,512,512]{2,1,0:T(8,128)} %slice.154), channel_id=1, source_target_pairs={{0,16},{16,32},{32,48},{48,64},{64,80},{80,96},{96,112},{1,17},{17... | collective-permute-start | bytes 6291464 | tf_op jit(solution)/shard_map/ppermute | solution.py:12
  361.4 37.8 %collective-permute-start.5 = (f32[512,512]{1,0:T(8,128)}, f32[512,512]{1,0:T(8,128)S(1)}, u32[]{:S(2)}, u32[]{:S(2)}) collective-permute-start(f32[512,512]{1,0:T(8,128)} %slice.158), channel_id=1, source_target_pairs={{0,16},{16,32},{32,48},{48,64},{64,80},{80,96},{96,112},{1,17},{17... | collective-permute-start | bytes 3145736 | tf_op jit(solution)/shard_map/ppermute | solution.py:12
  399.2 26.7 %all-reduce.3.cloned.1.call-done = (f32[2,512,512]{2,1,0:T(8,128)}, f32[512,512]{1,0:T(8,128)}) async-done(((f32[2,512,512]{2,1,0:T(8,128)}, f32[512,512]{1,0:T(8,128)}), (f32[2,512,512]{2,1,0:T(8,128)}, f32[512,512]{1,0:T(8,128)})) %all-reduce.3.cloned.1.call-update) | async-done | bytes 3145744 | tf_op jit(solution)/shard_map/psum | solution.py:122
  (63 shorter events, 67.6 us)
Async XLA Ops:
  7.2 418.7 %all-reduce.3.cloned.1.call-start = ((), (), s32[]{:S(2)}) async-start(), calls=%async_computation | async-start | bytes 6291456 | tf_op jit(solution)/shard_map/psum | solution.py:122
  7.2 29.3 %collective-permute-start = (f32[2,512,512]{2,1,0:T(8,128)}, f32[2,512,512]{2,1,0:T(8,128)S(1)}, u32[]{:S(2)}, u32[]{:S(2)}) collective-permute-start(f32[2,512,512]{2,1,0:T(8,128)} %param.16), channel_id=1, source_target_pairs={{16,0},{32,16},{48,32},{64,48},{80,64},{96,80},{112,96},{17,1},{33... | collective-permute-start | bytes 6291464 | tf_op jit(solution)/shard_map/ppermute | solution.py:12
  13.6 25.7 %copy-start.14 = (s32[1,2]{1,0:T(1,128)S(1)}, s32[1,2]{1,0:T(1,128)}, u32[]{:S(2)}) copy-start(s32[1,2]{1,0:T(1,128)} %param.19) | copy-start | bytes 28
  13.6 31.8 %copy-start.12 = (f32[1,512,512]{2,1,0:T(8,128)S(1)}, f32[1,512,512]{2,1,0:T(8,128)}, u32[]{:S(2)}) copy-start(f32[1,512,512]{2,1,0:T(8,128)} %param.18) | copy-start | bytes 3145732
  38.0 73.4 %collective-permute-start.1 = (f32[2,1024,512]{2,1,0:T(8,128)}, f32[2,1024,512]{2,1,0:T(8,128)}, u32[]{:S(2)}, u32[]{:S(2)}) collective-permute-start(f32[2,1024,512]{2,1,0:T(8,128)} %constant_dynamic-update-slice_fusion), channel_id=1, source_target_pairs={{1,0},{2,1},{3,2},{4,3},{5,4},{6,5},{7,6},{8,7},{9,8},{10,9},{11,1... | collective-permute-start | bytes 12582920 | tf_op jit(solution)/shard_map/ppermute | solution.py:12
  111.4 3.1 copy-start
  114.5 1.3 copy-start.1
  146.2 5.4 %copy-start.13 = (f32[1,512,512]{1,2,0:T(8,128)S(1)}, f32[1,512,512]{1,2,0:T(8,128)}, u32[]{:S(2)}) copy-start(f32[1,512,512]{1,2,0:T(8,128)} %copy.6) | copy-start | bytes 3145732
  197.3 1.5 copy-start.9
  224.1 100.0 %collective-permute-start.2 = (f32[2,1024,512]{2,1,0:T(8,128)}, f32[2,1024,512]{2,1,0:T(8,128)}, u32[]{:S(2)}, u32[]{:S(2)}) collective-permute-start(f32[2,1024,512]{2,1,0:T(8,128)} %slice.152), channel_id=1, source_target_pairs={{0,1},{1,2},{2,3},{3,4},{4,5},{5,6},{6,7},{7,8},{8,9},{9,10},{10,1... | collective-permute-start | bytes 12582920 | tf_op jit(solution)/shard_map/ppermute | solution.py:12
  240.0 5.9 %copy-start.2 = (f32[1,2,512,512]{3,2,1,0:T(8,128)S(1)}, f32[1,2,512,512]{3,2,1,0:T(8,128)}, u32[]{:S(2)}) copy-start(f32[1,2,512,512]{3,2,1,0:T(8,128)} %copy-done.1) | copy-start | bytes 6291460
  240.0 5.9 %copy-start.10 = (f32[512,512]{1,0:T(8,128)S(1)}, f32[512,512]{1,0:T(8,128)}, u32[]{:S(2)}) copy-start(f32[512,512]{1,0:T(8,128)} %copy-done.9) | copy-start | bytes 3145732
  243.3 112.9 %collective-permute-start.4 = (f32[1024,512]{1,0:T(8,128)}, f32[1024,512]{1,0:T(8,128)}, u32[]{:S(2)}, u32[]{:S(2)}) collective-permute-start(f32[1024,512]{1,0:T(8,128)} %slice.156), channel_id=1, source_target_pairs={{0,1},{1,2},{2,3},{3,4},{4,5},{5,6},{6,7},{7,8},{8,9},{9,10},{10,1... | collective-permute-start | bytes 6291464 | tf_op jit(solution)/shard_map/ppermute | solution.py:12
  328.6 3.1 copy-start.3
  328.6 27.5 %copy-start.5 = (f32[1024,1024]{1,0:T(8,128)S(1)}, f32[1024,1024]{1,0:T(8,128)}, u32[]{:S(2)}) copy-start(f32[1024,1024]{1,0:T(8,128)} %dynamic_update_slice.9) | copy-start | bytes 12582916
  331.7 98.2 %collective-permute-start.3 = (f32[2,512,512]{2,1,0:T(8,128)}, f32[2,512,512]{2,1,0:T(8,128)}, u32[]{:S(2)}, u32[]{:S(2)}) collective-permute-start(f32[2,512,512]{2,1,0:T(8,128)} %slice.154), channel_id=1, source_target_pairs={{0,16},{16,32},{32,48},{48,64},{64,80},{80,96},{96,112},{1,17},{17... | collective-permute-start | bytes 6291464 | tf_op jit(solution)/shard_map/ppermute | solution.py:12
  358.9 1.4 copy-start.6
  361.4 68.3 %collective-permute-start.5 = (f32[512,512]{1,0:T(8,128)}, f32[512,512]{1,0:T(8,128)S(1)}, u32[]{:S(2)}, u32[]{:S(2)}) collective-permute-start(f32[512,512]{1,0:T(8,128)} %slice.158), channel_id=1, source_target_pairs={{0,16},{16,32},{32,48},{48,64},{64,80},{80,96},{96,112},{1,17},{17... | collective-permute-start | bytes 3145736 | tf_op jit(solution)/shard_map/ppermute | solution.py:12
  425.9 1.9 copy-start.11
  427.8 2.0 copy-start.7
  427.8 3.6 copy-start.4
  429.7 2.4 copy-start.8
Sparse Core Ops, SparseCore 0:
  249.3 176.5 all-reduce.2
where the time goes:
time: 447 us; the launch traced here: 443 us
  waiting for transfers between devices  187 us (42%)
  matrix products  81.4 us (18%)
  starting transfers between devices  74 us (17%)
  local copies, waits for them, and re-layouts  53.3 us (12%)
  other arithmetic  25.2 us (6%)
  between operations  22.6 us (5%)
    ppermute x6, waiting for transfers between devices, shifted(): lax.ppermute(value, axis, [(source, source + steps) for source in range(l...  160 us
    ppermute x6, starting transfers between devices, shifted(): lax.ppermute(value, axis, [(source, source + steps) for source in range(l...  74 us
    dot_general x8, matrix products, right_mul(): jnp.einsum('prc,ck->prk', frames, table, preferred_element_type=jnp.float32)  41 us
    dot_general x8, matrix products, left_mul(): jnp.einsum('jr,prc->pjc', table, frames, preferred_element_type=jnp.float32)  40.4 us
    psum x1, waiting for transfers between devices, body(): lax.psum((probe_numer, probe_light), ('obj', 'pos'))  26.7 us
    dynamic_update_slice x1, local copies, waits for them, and re-layouts, place_grad(): return lax.dynamic_update_slice(board, block, (zero, row, col))  14.9 us
    unnamed x32, local copies, waits for them, and re-layouts  10.7 us
  transfers between devices with their start and end apart: 7, of which 4 were waited for; matrix products, arithmetic and copies ran while one was open for 8% of the time, Pallas kernels for 0%

commit v1 on v0

v1 whole, which is shorter than its diff:
```python
import functools
import math

import jax
import jax.numpy as jnp
import numpy as np
from jax import lax
from jax.experimental import pallas as pl
from jax.experimental.pallas import tpu as pltpu
from jax.sharding import PartitionSpec as P

F = 512
CHUNKS = 4
R = F // CHUNKS
Y = X = Z = 4
HALF, QUARTER, SIXTEENTH = F // 2, F // 8, F // 32
F32, BF16 = jnp.float32, jnp.bfloat16
VMEM = pl.BlockSpec(memory_space=pltpu.VMEM)
SMEM = pl.BlockSpec(memory_space=pltpu.SMEM)

ROW, COL, ROW_T, COL_T, CORE, AT_Y, AT_Z, TOUCH = 0, 1, 2, 3, 4, 5, 6, 7


def dft_tables():
    idx = np.arange(F)
    angle = (idx[:, None] * idx[None, :] % F) * (2.0 * math.pi / F)
    scale = 1.0 / math.sqrt(F)
    return (
        jnp.asarray((np.cos(angle) * scale).astype(np.float32)).astype(BF16),
        jnp.asarray((-np.sin(angle) * scale).astype(np.float32)).astype(BF16),
    )


def call(kernel, out_shapes, args, specs=None, scratch=(), limit=48, **params):
    return pl.pallas_call(
        kernel,
        out_shape=[jax.ShapeDtypeStruct(s, d) for s, d in out_shapes],
        in_specs=specs or [SMEM] + [VMEM] * (len(args) - 1),
        out_specs=[VMEM] * len(out_shapes),
        scratch_shapes=list(scratch),
        compiler_params=pltpu.CompilerParams(vmem_limit_bytes=limit * 2**20, **params),
    )(*args)


def iota(shape, dim):
    return lax.broadcasted_iota(jnp.int32, shape, dim)


def back_by(shift):
    return jnp.bitwise_and(F - shift, F - 1)


def prep_kernel(s, wr, wi, probe, cf, rf, rb, cb, turned):
    r, c = s[ROW], s[COL]
    w_re, w_im = wr[...].astype(F32), wi[...].astype(F32)
    for out, axis, shift, sign in ((cf, 0, c, 1), (rf, 1, r, -1), (rb, 0, r, 1), (cb, 1, c, -1)):
        re = pltpu.roll(w_re, shift, axis).astype(BF16)
        im = (pltpu.roll(w_im, shift, axis) * sign).astype(BF16)
        out[:F, :F] = re
        out[F:, F:] = re
        out[:F, F:] = im
        out[F:, :F] = -im
    for k in range(2):
        turned[k] = pltpu.roll(pltpu.roll(probe[k], r, 0), c, 1)


def corner(s, which):
    return s[TOUCH + 2 * which], s[TOUCH + 2 * which + 1]


def touch_mask(which, r, c):
    row, col = iota((F, F), 0), iota((F, F), 1)
    inside_rows = row >= r if which < 2 else row < r
    inside_cols = col >= c if which % 2 == 0 else col < c
    return jnp.logical_and(inside_rows, inside_cols)


def probe_light_kernel(s, obj, keep, send):
    value = obj[0] * obj[0] + obj[1] * obj[1]
    total = jnp.zeros((F, F), F32)
    for which in range(4):
        r, c = corner(s, which)
        part = jnp.where(touch_mask(which, r, c), value, 0.0)
        total += pltpu.roll(pltpu.roll(part, back_by(c), 1), back_by(r + s[CORE] * HALF), 0)
    keep[...] = total[:HALF]
    send[...] = total[HALF:]


def light_kernel(s, probe, out):
    power = probe[0] * probe[0] + probe[1] * probe[1]
    total = jnp.zeros((F, F), F32)
    for which in range(4):
        r, c = corner(s, which)
        part = pltpu.roll(pltpu.roll(power, r, 0), c, 1)
        total += jnp.where(touch_mask(which, r, c), part, 0.0)
    out[...] = total


def half_kernel(first, s, obj, below, beside, turned, cf, patch, half):
    r, c, odd = s[ROW], s[COL], s[CORE] == 1
    row = iota((R, F), 0) + first
    col = iota((R, F), 1)
    low, high = jnp.where(odd, 0, c), jnp.where(odd, c, F)
    here = jnp.logical_and(col >= low, col < high)
    m = [jnp.where(here, jnp.where(row >= r, obj[k], below[k]), beside[k]) for k in range(2)]
    for k in range(2):
        patch[k] = m[k]
    psi_re = (turned[0] * m[0] - turned[1] * m[1]).astype(BF16)
    psi_im = (turned[0] * m[1] + turned[1] * m[0]).astype(BF16)
    out = jnp.dot(jnp.concatenate([psi_re, psi_im], axis=1), cf[...], preferred_element_type=F32)
    half[0] = out[:, :F].astype(BF16)
    half[1] = out[:, F:].astype(BF16)


def fourier_kernel(s, *refs):
    halves, patches = refs[:CHUNKS], refs[CHUNKS : 2 * CHUNKS]
    rf, rb, cb, amps, amps_moved, turned = refs[2 * CHUNKS : 2 * CHUNKS + 6]
    grads = refs[2 * CHUNKS + 6 : 3 * CHUNKS + 6]
    keep, send, stack, change, back, numer = refs[3 * CHUNKS + 6 :]
    r, c, odd = s[ROW], s[COL], s[CORE] == 1
    for i in range(CHUNKS):
        for k in range(2):
            stack[k * F + i * R : k * F + (i + 1) * R] = halves[i][k]
    wide = 256
    for j in range(0, F, wide):
        at = slice(j, j + wide)
        spec = jnp.dot(rf[...], stack[:, at], preferred_element_type=F32)
        re, im = spec[:F], spec[F:]
        a = jnp.where(odd, amps_moved[0, :, at], amps[0, :, at])
        factor = a / jnp.maximum(jnp.sqrt(re * re + im * im), 0.25) - 1.0
        change[:F, at] = (factor * re).astype(BF16)
        change[F:, at] = (factor * im).astype(BF16)
    for j in range(0, F, wide):
        at = slice(j, j + wide)
        out = jnp.dot(rb[...], change[:, at], preferred_element_type=F32)
        back[:, j : j + wide] = out[:F].astype(BF16)
        back[:, F + j : F + j + wide] = out[F:].astype(BF16)
    for i in range(CHUNKS):
        at = slice(i * R, (i + 1) * R)
        err = jnp.dot(back[at], cb[...], preferred_element_type=F32)
        re, im = err[:, :F], err[:, F:]
        p_re, p_im = turned[0, at], turned[1, at]
        grads[i][0] = p_re * re + p_im * im
        grads[i][1] = p_re * im - p_im * re
        m_re, m_im = patches[i][0], patches[i][1]
        numer[0, at] = pltpu.roll(m_re * re + m_im * im, back_by(c), 1)
        numer[1, at] = pltpu.roll(m_re * im - m_im * re, back_by(c), 1)
    for k in range(2):
        turned_back = pltpu.roll(numer[k], back_by(r + s[CORE] * HALF), 0)
        keep[k] = turned_back[:HALF]
        send[k] = turned_back[HALF:]


def split_kernel(axis, parts, rows, s, *refs):
    ins, outs, held = refs[: sum(parts)], refs[sum(parts) : -1], refs[-1]
    at, first = 0, 0
    for count in parts:
        total = ins[at][...]
        for ref in ins[at + 1 : at + count]:
            total = total + ref[...]
        planes = total.shape[0] if total.ndim == 3 else 1
        held[first : first + planes] = total.reshape((planes,) + total.shape[-2:])
        at, first = at + count, first + planes
    for j in range(4):
        block = jnp.bitwise_and(s[axis] + j, 3)
        outs[j][...] = held[:, pl.ds(pl.multiple_of(block * rows, rows), rows), :]


def join_kernel(axis, rows, s, *refs):
    for j in range(4):
        block = jnp.bitwise_and(s[axis] - j, 3)
        refs[4][:, pl.ds(pl.multiple_of(block * rows, rows), rows), :] = refs[j][...]


def update_kernel(beta, s, a, b, c, d, probe, out):
    total = a[...] + b[...] + c[...] + d[...]
    out[...] = probe[...] + beta * total[:2] / (total[2:3] + 1.0)


def turn(value, along, steps):
    if along == "z":
        return lax.ppermute(value, "obj", [(o, (o + 2 * steps) % (2 * Z)) for o in range(2 * Z)])
    pairs = []
    for y in range(Y):
        for x in range(X):
            to = (y, (x + steps) % X) if along == "x" else ((y + steps) % Y, x)
            pairs.append((y * X + x, to[0] * X + to[1]))
    return lax.ppermute(value, "pos", pairs)


def swap(value):
    return lax.ppermute(value, "obj", [(o, o ^ 1) for o in range(2 * Z)])


def shifted(value, steps):
    n = 2 * Z
    return lax.ppermute(value, "obj", [(o, o + steps) for o in range(n) if 0 <= o + steps < n])


def x_pairs(odd_only=False):
    n = Y * X
    pairs = [(o * n + p, o * n + (p + 1) % n) for o in range(1, 2 * Z, 2) for p in range(n)]
    if not odd_only:
        pairs += [(o * n + p, o * n + p - 1) for o in range(0, 2 * Z, 2) for p in range(1, n)]
    return pairs


def toward(value, odd_only=False):
    return lax.ppermute(value, ("obj", "pos"), x_pairs(odd_only))


def homeward(value):
    return lax.ppermute(value, ("obj", "pos"), [(b, a) for a, b in x_pairs()])


def body(object_field, probe, amplitudes, offsets):
    row_index = lax.axis_index("obj")
    col_index = lax.axis_index("pos")
    core, z = row_index % 2, row_index // 2
    y = col_index // X
    own = offsets[0] - jnp.stack([row_index * F, col_index * F])
    n = Y * X
    left = lax.ppermute(own, "pos", [(p, (p + 1) % n) for p in range(n)])
    above = shifted(jnp.concatenate([own, left]), 1)
    odd = core == 1
    mine, target = jnp.where(odd, left, own), jnp.where(odd, own, left)
    s = jnp.concatenate([mine, target, jnp.stack([core, y, z]), own, left, above]).astype(jnp.int32)

    col = jnp.arange(F, dtype=jnp.int32)[None, :]
    here = (col >= jnp.where(odd, 0, mine[1])) & (col < jnp.where(odd, mine[1], F))
    there = (col >= jnp.where(odd, target[1], 0)) & (col < jnp.where(odd, F, target[1]))
    rows = [jnp.arange(i * R, (i + 1) * R, dtype=jnp.int32)[:, None] for i in range(CHUNKS)]

    tiles = [object_field[:, i * R : (i + 1) * R] for i in range(CHUNKS)]
    below = [shifted(t, -1) for t in tiles]
    amps_moved = toward(amplitudes, odd_only=True)
    beside = [
        toward(jnp.where(rows[i] >= target[0], tiles[i], below[i])) for i in range(CHUNKS)
    ]

    wr, wi = dft_tables()
    square = ((2 * F, 2 * F), BF16)
    cf, rf, rb, cb, turned = call(
        prep_kernel, [square] * 4 + [((2, F, F), F32)], (s, wr, wi, probe)
    )
    pl_keep, pl_send = call(probe_light_kernel, [((HALF, F), F32)] * 2, (s, object_field))
    pl_got = swap(pl_send)
    pl_blocks = call(
        functools.partial(split_kernel, AT_Y, (2,), QUARTER),
        [((1, QUARTER, F), F32)] * 4,
        (s, pl_keep, pl_got),
        scratch=[pltpu.VMEM((1, HALF, F), F32)],
    )
    pl_parts = [pl_blocks[0]] + [turn(pl_blocks[j], "y", j) for j in (1, 2, 3)]

    patches, halves = [], []
    for i in range(CHUNKS):
        chunk = pl.BlockSpec((2, R, F), lambda g, i=i: (0, i, 0))
        whole = pl.BlockSpec((2, R, F), lambda g: (0, 0, 0))
        table = pl.BlockSpec((2 * F, 2 * F), lambda g: (0, 0))
        patch, half = pl.pallas_call(
            functools.partial(half_kernel, i * R),
            grid=(1,),
            out_shape=[
                jax.ShapeDtypeStruct((2, R, F), F32),
                jax.ShapeDtypeStruct((2, R, F), BF16),
            ],
            in_specs=[SMEM, chunk, whole, whole, chunk, table],
            out_specs=[whole, whole],
            compiler_params=pltpu.CompilerParams(vmem_limit_bytes=40 * 2**20),
        )(s, object_field, below[i], beside[i], turned, cf)
        patches.append(patch)
        halves.append(half)

    *grads, pn_keep, pn_send = call(
        fourier_kernel,
        [((2, R, F), F32)] * CHUNKS + [((2, HALF, F), F32)] * 2,
        (s, *halves, *patches, rf, rb, cb, amplitudes, amps_moved, turned),
        scratch=[
            pltpu.VMEM((2 * F, F), BF16),
            pltpu.VMEM((2 * F, F), BF16),
            pltpu.VMEM((F, 2 * F), BF16),
            pltpu.VMEM((2, F, F), F32),
        ],
    )

    (light,) = call(light_kernel, [((F, F), F32)], (s, probe))
    moved = [homeward(g) for g in grads]
    down = []
    for i in range(CHUNKS):
        mine_down = jnp.where(here & (rows[i] < mine[0]), grads[i], 0.0)
        moved_down = jnp.where(there & (rows[i] < target[0]), moved[i], 0.0)
        down.append(shifted(mine_down + moved_down, 1))

    pn_got = swap(pn_send)
    pn_blocks = call(
        functools.partial(split_kernel, AT_Y, (2,), QUARTER),
        [((2, QUARTER, F), F32)] * 4,
        (s, pn_keep, pn_got),
        scratch=[pltpu.VMEM((2, HALF, F), F32)],
    )
    pn_parts = [pn_blocks[0]] + [turn(pn_blocks[j], "y", j) for j in (1, 2, 3)]
    blocks = call(
        functools.partial(split_kernel, AT_Z, (4, 4), SIXTEENTH),
        [((3, SIXTEENTH, F), F32)] * 4,
        (s, *pn_parts, *pl_parts),
        scratch=[pltpu.VMEM((3, QUARTER, F), F32)],
    )
    parts = [blocks[0]] + [turn(blocks[j], "z", j) for j in (1, 2, 3)]
    share = parts[0] + parts[1] + parts[2] + parts[3]
    shares = [share] + [turn(share, "x", j) for j in (1, 2, 3)]
    beta = 0.5 * math.sqrt(Y * X * 2 * Z)
    start = core * HALF + y * QUARTER + z * SIXTEENTH
    probe_rows = lax.dynamic_slice(probe, (0, start, 0), (2, SIXTEENTH, F))
    (fresh,) = call(
        functools.partial(update_kernel, beta),
        [((2, SIXTEENTH, F), F32)],
        (s, *shares, probe_rows),
    )
    for along, at, size in (("z", AT_Z, SIXTEENTH), ("y", AT_Y, QUARTER)):
        pieces = [fresh] + [turn(fresh, along, j) for j in (1, 2, 3)]
        (fresh,) = call(
            functools.partial(join_kernel, at, size), [((2, 4 * size, F), F32)], (s, *pieces)
        )
    other = swap(fresh)
    new_probe = jnp.concatenate(
        [jnp.where(odd, other, fresh), jnp.where(odd, fresh, other)], axis=1
    )

    new_tiles = []
    for i in range(CHUNKS):
        numer = (
            jnp.where(here & (rows[i] >= mine[0]), grads[i], 0.0)
            + jnp.where(there & (rows[i] >= target[0]), moved[i], 0.0)
            + down[i]
        )
        new_tiles.append(tiles[i] + numer / (light[i * R : (i + 1) * R] + 1.0))
    return (jnp.concatenate(new_tiles, axis=1), new_probe)


def solution(mesh):
    in_specs = (P(None, "obj", "pos"), P(), P(("obj", "pos"), None, None), P(("obj", "pos"), None))
    out_specs = (P(None, "obj", "pos"), P())
    return jax.shard_map(body, mesh=mesh, in_specs=in_specs, out_specs=out_specs, check_vma=False)
```

time: 447 us -> 210 us (0.47)
  waiting for transfers between devices: 187 us -> 42 us
  matrix products: 81.4 us -> 0 us
  local copies, waits for them, and re-layouts: 53.3 us -> 11.8 us
  Pallas kernels: 0 us -> 40.2 us
  between operations: 22.6 us -> 3.98 us
  starting transfers between devices: 74 us -> 91 us
  other arithmetic: 25.2 us -> 20.1 us
    ppermute x6 -> x40, waiting for transfers between devices: 160 us -> 42 us  [the longest x9 21.1 us: shifted(): lax.ppermute(value, 'obj', [(o, o + steps) for o in range(n) if 0 <= o +...]
    dot_general x16 -> x0, matrix products: 81.4 us -> none  [the longest x8 41 us: right_mul(): jnp.einsum('prc,ck->prk', frames, table, preferred_element_type=jnp.float32)]
    pallas_call x0 -> x14, Pallas kernels: none -> 40.2 us  [the longest x10 33.4 us: call(): pl.pallas_call(kernel, out_shape=[jax.ShapeDtypeStruct(s, d) for s, d in...]
    psum x1 -> x0, waiting for transfers between devices: 26.7 us -> none  [body(): lax.psum((probe_numer, probe_light), ('obj', 'pos'))]
    dynamic_update_slice x2 -> x0, local copies, waits for them, and re-layouts: 23.2 us -> none  [the longest x1 14.9 us: place_grad(): return lax.dynamic_update_slice(board, block, (zero, row, col))]
    ppermute x6 -> x40, starting transfers between devices: 74 us -> 91 us  [the longest x4 24.7 us: homeward(): return lax.ppermute(value, ('obj', 'pos'), [(b, a) for a, b in x_pairs()])]
    add x7 -> x8, other arithmetic: 15.1 us -> 4.33 us  [the longest x3 2.56 us: body(): new_tiles.append(tiles[i] + numer / (light[i * R:(i + 1) * R] + 1.0))]
    another operation x5 -> x0, other arithmetic: 7.02 us -> none
  transfers between devices with their start and end apart: 7 -> 40, of which waited for: 4 -> 10; matrix products, arithmetic and copies ran while one was open for 8% -> 11% of each run, Pallas kernels for 0% -> 14%
where the time goes in v1:
time: 210 us; the launch traced here: 209 us
  starting transfers between devices  91 us (43%)
  waiting for transfers between devices  42 us (20%)
  Pallas kernels  40.2 us (19%)
  other arithmetic  20.1 us (10%)
  local copies, waits for them, and re-layouts  11.8 us (6%)
  between operations  3.98 us (2%)
    pallas_call x10, Pallas kernels, call(): pl.pallas_call(kernel, out_shape=[jax.ShapeDtypeStruct(s, d) for s, d in...  33.4 us
    ppermute x4, starting transfers between devices, homeward(): return lax.ppermute(value, ('obj', 'pos'), [(b, a) for a, b in x_pairs()])  24.7 us
    ppermute x9, starting transfers between devices, shifted(): lax.ppermute(value, 'obj', [(o, o + steps) for o in range(n) if 0 <= o +...  21.9 us
    ppermute x9, waiting for transfers between devices, shifted(): lax.ppermute(value, 'obj', [(o, o + steps) for o in range(n) if 0 <= o +...  21.1 us
    ppermute x12, starting transfers between devices, turn(): return lax.ppermute(value, 'pos', pairs)  16.6 us
    ppermute x12, waiting for transfers between devices, turn(): return lax.ppermute(value, 'pos', pairs)  16.4 us
    ppermute x5, starting transfers between devices, toward(): return lax.ppermute(value, ('obj', 'pos'), x_pairs(odd_only))  15.3 us
    ppermute x6, starting transfers between devices, turn(): lax.ppermute(value, 'obj', [(o, (o + 2 * steps) % (2 * Z)) for o in range...  9.22 us
  transfers between devices with their start and end apart: 40, of which 10 were waited for; matrix products, arithmetic and copies ran while one was open for 11% of the time, Pallas kernels for 14%

profile of v1, /device:TPU:1, one launch (start us, length us, event | category | flops | bytes accessed | tf_op | source)
XLA Modules:
  0.0 209.1 jit_solution(8013652092031334628)
XLA Ops:
  3.4 2.9 %fusion.14 = (f32[2,128,512]{2,1,0:T(8,128)}, f32[2,128,512]{2,1,0:T(8,128)}, f32[2,128,512]{2,1,0:T(8,128)}, f32[2,128,512]{2,1,0:T(8,128)}) fusion(f32[2,512,512]{2,1,0:T(8,128)} %obj.9), kind=kLoop, calls=%fused_computation.67 | loop fusion | bytes 4194304 | tf_op jit(solution)/shard_map/slice | solution.py:234
  6.3 2.9 %collective-permute-start.2 = (f32[2,128,512]{2,1,0:T(8,128)}, f32[2,128,512]{2,1,0:T(8,128)S(1)}, u32[]{:S(2)}, u32[]{:S(2)}) collective-permute-start(f32[2,128,512]{2,1,0:T(8,128)} %get-tuple-element.81), channel_id=1, source_target_pairs={{16,0},{32,16},{48,32},{64,48},{80,64},{96,80},{112,96},{17,1},{33... | collective-permute-start | bytes 1572872 | tf_op jit(solution)/shard_map/ppermute | solution.py:197
  15.0 3.1 %collective-permute-start.10 = (f32[1,512,512]{2,1,0:T(8,128)}, f32[1,512,512]{2,1,0:T(8,128)}, u32[]{:S(2)}, u32[]{:S(2)}) collective-permute-start(f32[1,512,512]{2,1,0:T(8,128)} %refs_11_.1), channel_id=1, source_target_pairs={{16,17},{17,18},{18,19},{19,20},{20,21},{21,22},{22,23},{23,24},{2... | collective-permute-start | bytes 3145736 | tf_op jit(solution)/shard_map/ppermute | solution.py:209
  20.2 3.2 %collective-permute-done.4.below = f32[2,128,512]{2,1,0:T(8,128)S(1)} collective-permute-done((f32[2,128,512]{2,1,0:T(8,128)}, f32[2,128,512]{2,1,0:T(8,128)S(1)}, u32[]{:S(2)}, u32[]{:S(2)}) %collective-permute-start.4) | collective-permute-done | bytes 524320 | tf_op jit(solution)/shard_map/ppermute | solution.py:197
  23.4 6.0 %collective-permute-done.6.below = f32[2,128,512]{2,1,0:T(8,128)} collective-permute-done((f32[2,128,512]{2,1,0:T(8,128)}, f32[2,128,512]{2,1,0:T(8,128)}, u32[]{:S(2)}, u32[]{:S(2)}) %collective-permute-start.6) | collective-permute-done | bytes 524320 | tf_op jit(solution)/shard_map/ppermute | solution.py:197
  29.4 5.3 %collective-permute-done.8.below = f32[2,128,512]{2,1,0:T(8,128)} collective-permute-done((f32[2,128,512]{2,1,0:T(8,128)}, f32[2,128,512]{2,1,0:T(8,128)}, u32[]{:S(2)}, u32[]{:S(2)}) %collective-permute-start.8) | collective-permute-done | bytes 524320 | tf_op jit(solution)/shard_map/ppermute | solution.py:197
  37.6 3.1 %collective-permute-start.9 = (f32[2,128,512]{2,1,0:T(8,128)}, f32[2,128,512]{2,1,0:T(8,128)}, u32[]{:S(2)}, u32[]{:S(2)}) collective-permute-start(f32[2,128,512]{2,1,0:T(8,128)} %get-tuple-element.74), channel_id=1, source_target_pairs={{16,17},{17,18},{18,19},{19,20},{20,21},{21,22},{22,23},{23,24},{2... | collective-permute-start | bytes 1572872 | tf_op jit(solution)/shard_map/ppermute | solution.py:209
  45.4 3.1 %collective-permute-start.5 = (f32[2,128,512]{2,1,0:T(8,128)}, f32[2,128,512]{2,1,0:T(8,128)}, u32[]{:S(2)}, u32[]{:S(2)}) collective-permute-start(f32[2,128,512]{2,1,0:T(8,128)} %get-tuple-element.76), channel_id=1, source_target_pairs={{16,17},{17,18},{18,19},{19,20},{20,21},{21,22},{22,23},{23,24},{2... | collective-permute-start | bytes 1572872 | tf_op jit(solution)/shard_map/ppermute | solution.py:209
  48.6 3.1 %collective-permute-start.3 = (f32[2,128,512]{2,1,0:T(8,128)}, f32[2,128,512]{2,1,0:T(8,128)}, u32[]{:S(2)}, u32[]{:S(2)}) collective-permute-start(f32[2,128,512]{2,1,0:T(8,128)} %get-tuple-element.75), channel_id=1, source_target_pairs={{16,17},{17,18},{18,19},{19,20},{20,21},{21,22},{22,23},{23,24},{2... | collective-permute-start | bytes 1572872 | tf_op jit(solution)/shard_map/ppermute | solution.py:209
  54.8 8.3 %shard_map.77 = (bf16[1024,1024]{1,0:T(8,128)(2,1)S(1)}, bf16[1024,1024]{1,0:T(8,128)(2,1)S(1)}, bf16[1024,1024]{1,0:T(8,128)(2,1)}, bf16[1024,1024]{1,0:T(8,128)(2,1)}, f32[2,512,512]{2,1,0:T(8,128)}) custom-call(s32[15]{0:T(128)S(1)} %concatenate.13.s, bf16[512,512]{1,0:T(8,128)(2,1)S(1)} %copy-done.7, bf16[512,512]{1,0:T(8,128)(2,1)S(1)} %copy-done.8, ...), custom_call_target="tpu_custom_call" | custom-call | tf_op jit(solution)/shard_map/pallas_call | solution.py:35
  72.4 10.8 %shard_map.82 = (f32[2,128,512]{2,1,0:T(8,128)S(1)}, f32[2,128,512]{2,1,0:T(8,128)}, f32[2,128,512]{2,1,0:T(8,128)S(1)}, f32[2,128,512]{2,1,0:T(8,128)S(1)}, f32...) custom-call(s32[15]{0:T(128)S(1)} %concatenate.13.s, bf16[2,128,512]{2,1,0:T(8,128)(2,1)S(1)} %get-tuple-element.37.refs_0_, ...), custom_call_target="tpu_custom_call" | custom-call | tf_op jit(solution)/shard_map/pallas_call | solution.py:35
  87.8 4.8 %shard_map.85 = (f32[256,512]{1,0:T(8,128)S(1)}, f32[256,512]{1,0:T(8,128)S(1)}) custom-call(s32[15]{0:T(128)S(1)} %concatenate.13.s, f32[2,512,512]{2,1,0:T(8,128)S(1)} %copy-done), custom_call_target="tpu_custom_call" | custom-call | tf_op jit(solution)/shard_map/pallas_call | solution.py:35
  98.5 2.9 %collective-permute-start.25 = (f32[1,64,512]{2,1,0:T(8,128)}, f32[1,64,512]{2,1,0:T(8,128)}, u32[]{:S(2)}, u32[]{:S(2)}) collective-permute-start(f32[1,64,512]{2,1,0:T(8,128)} %get-tuple-element.62), channel_id=1, source_target_pairs={{0,8},{1,9},{2,10},{3,11},{4,12},{5,13},{6,14},{7,15},{8,0},{9,1},... | collective-permute-start | bytes 393224 | tf_op jit(solution)/shard_map/ppermute | solution.py:188
  101.4 3.6 %collective-permute-start.13 = (f32[2,128,512]{2,1,0:T(8,128)}, f32[2,128,512]{2,1,0:T(8,128)}, u32[]{:S(2)}, u32[]{:S(2)}) collective-permute-start(f32[2,128,512]{2,1,0:T(8,128)} %get-tuple-element.49), channel_id=1, source_target_pairs={{17,16},{18,17},{19,18},{20,19},{21,20},{22,21},{23,22},{24,23},{2... | collective-permute-start | bytes 1572872 | tf_op jit(solution)/shard_map/ppermute | solution.py:213
  116.2 5.4 %collective-permute-start.11 = (f32[2,128,512]{2,1,0:T(8,128)}, f32[2,128,512]{2,1,0:T(8,128)S(1)}, u32[]{:S(2)}, u32[]{:S(2)}) collective-permute-start(f32[2,128,512]{2,1,0:T(8,128)} %copy-done.3), channel_id=1, source_target_pairs={{17,16},{18,17},{19,18},{20,19},{21,20},{22,21},{23,22},{24,23},{2... | collective-permute-start | bytes 1572872 | tf_op jit(solution)/shard_map/ppermute | solution.py:213
  122.6 3.9 %shard_map.83 = f32[512,512]{1,0:T(8,128)S(1)} custom-call(s32[15]{0:T(128)S(1)} %concatenate.13.s, f32[2,512,512]{2,1,0:T(8,128)S(1)} %copy-done.2), custom_call_target="tpu_custom_call" | custom-call | tf_op jit(solution)/shard_map/pallas_call | solution.py:35
  126.5 3.3 %collective-permute-start.17 = (f32[2,128,512]{2,1,0:T(8,128)S(1)}, f32[2,128,512]{2,1,0:T(8,128)S(1)}, u32[]{:S(2)}, u32[]{:S(2)}) collective-permute-start(f32[2,128,512]{2,1,0:T(8,128)S(1)} %get-tuple-element.51), channel_id=1, source_target_pairs={{17,16},{18,17},{19,18},{20,19},{21,20},{22,21},{23,22},{24,23},{2... | collective-permute-start | bytes 1572872 | tf_op jit(solution)/shard_map/ppermute | solution.py:213
  140.4 12.4 %collective-permute-start.15 = (f32[2,128,512]{2,1,0:T(8,128)S(1)}, f32[2,128,512]{2,1,0:T(8,128)S(1)}, u32[]{:S(2)}, u32[]{:S(2)}) collective-permute-start(f32[2,128,512]{2,1,0:T(8,128)S(1)} %get-tuple-element.50), channel_id=1, source_target_pairs={{17,16},{18,17},{19,18},{20,19},{21,20},{22,21},{23,22},{24,23},{2... | collective-permute-start | bytes 1572872 | tf_op jit(solution)/shard_map/ppermute | solution.py:213
  155.7 4.0 %collective-permute-done.30.b = f32[3,16,512]{2,1,0:T(8,128)S(1)} collective-permute-done((f32[3,16,512]{2,1,0:T(8,128)S(1)}, f32[3,16,512]{2,1,0:T(8,128)S(1)}, u32[]{:S(2)}, u32[]{:S(2)}) %collective-permute-start.30) | collective-permute-done | bytes 98336 | tf_op jit(solution)/shard_map/ppermute | solution.py:188
  159.7 3.8 %collective-permute-start.14 = (f32[2,128,512]{2,1,0:T(8,128)S(1)}, f32[2,128,512]{2,1,0:T(8,128)S(1)}, u32[]{:S(2)}, u32[]{:S(2)}) collective-permute-start(f32[2,128,512]{2,1,0:T(8,128)S(1)} %select_add_fusion.2), channel_id=1, source_target_pairs={{0,16},{16,32},{32,48},{48,64},{64,80},{80,96},{96,112},{1,17},{17... | collective-permute-start | bytes 1572872 | tf_op jit(solution)/shard_map/ppermute | solution.py:197
  167.8 3.9 %collective-permute-done.33.refs_1_ = f32[2,16,512]{2,1,0:T(8,128)S(1)} collective-permute-done((f32[2,16,512]{2,1,0:T(8,128)S(1)}, f32[2,16,512]{2,1,0:T(8,128)S(1)}, u32[]{:S(2)}, u32[]{:S(2)}) %collective-permute-start.33) | collective-permute-done | bytes 65568 | tf_op jit(solution)/shard_map/ppermute | solution.py:182
  179.8 10.0 %collective-permute-done.36.refs_1_ = f32[2,64,512]{2,1,0:T(8,128)S(1)} collective-permute-done((f32[2,64,512]{2,1,0:T(8,128)S(1)}, f32[2,64,512]{2,1,0:T(8,128)S(1)}, u32[]{:S(2)}, u32[]{:S(2)}) %collective-permute-start.36) | collective-permute-done | bytes 262176 | tf_op jit(solution)/shard_map/ppermute | solution.py:188
  189.8 3.8 %collective-permute-start.18 = (f32[2,128,512]{2,1,0:T(8,128)S(1)}, f32[2,128,512]{2,1,0:T(8,128)S(1)}, u32[]{:S(2)}, u32[]{:S(2)}) collective-permute-start(f32[2,128,512]{2,1,0:T(8,128)S(1)} %select_add_fusion), channel_id=1, source_target_pairs={{0,16},{16,32},{32,48},{48,64},{64,80},{80,96},{96,112},{1,17},{17... | collective-permute-start | bytes 1572872 | tf_op jit(solution)/shard_map/ppermute | solution.py:197
  199.7 5.6 %collective-permute-done.16 = f32[2,128,512]{2,1,0:T(8,128)S(1)} collective-permute-done((f32[2,128,512]{2,1,0:T(8,128)S(1)}, f32[2,128,512]{2,1,0:T(8,128)S(1)}, u32[]{:S(2)}, u32[]{:S(2)}) %collective-permute-start.16) | collective-permute-done | bytes 524320 | tf_op jit(solution)/shard_map/ppermute | solution.py:197
  (144 shorter events, 85.9 us)
Async XLA Ops:
  11.1 18.3 %collective-permute-start.6 = (f32[2,128,512]{2,1,0:T(8,128)}, f32[2,128,512]{2,1,0:T(8,128)}, u32[]{:S(2)}, u32[]{:S(2)}) collective-permute-start(f32[2,128,512]{2,1,0:T(8,128)} %get-tuple-element.79), channel_id=1, source_target_pairs={{16,0},{32,16},{48,32},{64,48},{80,64},{96,80},{112,96},{17,1},{33... | collective-permute-start | bytes 1572872 | tf_op jit(solution)/shard_map/ppermute | solution.py:197
  13.0 21.7 %collective-permute-start.8 = (f32[2,128,512]{2,1,0:T(8,128)}, f32[2,128,512]{2,1,0:T(8,128)}, u32[]{:S(2)}, u32[]{:S(2)}) collective-permute-start(f32[2,128,512]{2,1,0:T(8,128)} %get-tuple-element.78), channel_id=1, source_target_pairs={{16,0},{32,16},{48,32},{64,48},{80,64},{96,80},{112,96},{17,1},{33... | collective-permute-start | bytes 1572872 | tf_op jit(solution)/shard_map/ppermute | solution.py:197
  15.0 57.4 %collective-permute-start.10 = (f32[1,512,512]{2,1,0:T(8,128)}, f32[1,512,512]{2,1,0:T(8,128)}, u32[]{:S(2)}, u32[]{:S(2)}) collective-permute-start(f32[1,512,512]{2,1,0:T(8,128)} %refs_11_.1), channel_id=1, source_target_pairs={{16,17},{17,18},{18,19},{19,20},{20,21},{21,22},{22,23},{23,24},{2... | collective-permute-start | bytes 3145736 | tf_op jit(solution)/shard_map/ppermute | solution.py:209
  37.6 25.6 %collective-permute-start.9 = (f32[2,128,512]{2,1,0:T(8,128)}, f32[2,128,512]{2,1,0:T(8,128)}, u32[]{:S(2)}, u32[]{:S(2)}) collective-permute-start(f32[2,128,512]{2,1,0:T(8,128)} %get-tuple-element.74), channel_id=1, source_target_pairs={{16,17},{17,18},{18,19},{19,20},{20,21},{21,22},{22,23},{23,24},{2... | collective-permute-start | bytes 1572872 | tf_op jit(solution)/shard_map/ppermute | solution.py:209
  42.6 24.6 %collective-permute-start.7 = (f32[2,128,512]{2,1,0:T(8,128)}, f32[2,128,512]{2,1,0:T(8,128)}, u32[]{:S(2)}, u32[]{:S(2)}) collective-permute-start(f32[2,128,512]{2,1,0:T(8,128)} %get-tuple-element.77), channel_id=1, source_target_pairs={{16,17},{17,18},{18,19},{19,20},{20,21},{21,22},{22,23},{23,24},{2... | collective-permute-start | bytes 1572872 | tf_op jit(solution)/shard_map/ppermute | solution.py:209
  45.4 23.6 %collective-permute-start.5 = (f32[2,128,512]{2,1,0:T(8,128)}, f32[2,128,512]{2,1,0:T(8,128)}, u32[]{:S(2)}, u32[]{:S(2)}) collective-permute-start(f32[2,128,512]{2,1,0:T(8,128)} %get-tuple-element.76), channel_id=1, source_target_pairs={{16,17},{17,18},{18,19},{19,20},{20,21},{21,22},{22,23},{23,24},{2... | collective-permute-start | bytes 1572872 | tf_op jit(solution)/shard_map/ppermute | solution.py:209
  48.6 22.1 %collective-permute-start.3 = (f32[2,128,512]{2,1,0:T(8,128)}, f32[2,128,512]{2,1,0:T(8,128)}, u32[]{:S(2)}, u32[]{:S(2)}) collective-permute-start(f32[2,128,512]{2,1,0:T(8,128)} %get-tuple-element.75), channel_id=1, source_target_pairs={{16,17},{17,18},{18,19},{19,20},{20,21},{21,22},{22,23},{23,24},{2... | collective-permute-start | bytes 1572872 | tf_op jit(solution)/shard_map/ppermute | solution.py:209
  83.9 25.1 %collective-permute-start.19 = (f32[2,256,512]{2,1,0:T(8,128)}, f32[2,256,512]{2,1,0:T(8,128)}, u32[]{:S(2)}, u32[]{:S(2)}) collective-permute-start(f32[2,256,512]{2,1,0:T(8,128)} %get-tuple-element.53), channel_id=1, source_target_pairs={{0,16},{16,0},{32,48},{48,32},{64,80},{80,64},{96,112},{112,96},{1... | collective-permute-start | bytes 3145736 | tf_op jit(solution)/shard_map/ppermute | solution.py:192
  96.8 16.4 %collective-permute-start.24 = (f32[1,64,512]{2,1,0:T(8,128)}, f32[1,64,512]{2,1,0:T(8,128)S(1)}, u32[]{:S(2)}, u32[]{:S(2)}) collective-permute-start(f32[1,64,512]{2,1,0:T(8,128)} %get-tuple-element.61), channel_id=1, source_target_pairs={{0,4},{1,5},{2,6},{3,7},{4,8},{5,9},{6,10},{7,11},{8,12},{9,13},{1... | collective-permute-start | bytes 393224 | tf_op jit(solution)/shard_map/ppermute | solution.py:188
  98.5 15.7 %collective-permute-start.25 = (f32[1,64,512]{2,1,0:T(8,128)}, f32[1,64,512]{2,1,0:T(8,128)}, u32[]{:S(2)}, u32[]{:S(2)}) collective-permute-start(f32[1,64,512]{2,1,0:T(8,128)} %get-tuple-element.62), channel_id=1, source_target_pairs={{0,8},{1,9},{2,10},{3,11},{4,12},{5,13},{6,14},{7,15},{8,0},{9,1},... | collective-permute-start | bytes 393224 | tf_op jit(solution)/shard_map/ppermute | solution.py:188
  101.4 35.6 %collective-permute-start.13 = (f32[2,128,512]{2,1,0:T(8,128)}, f32[2,128,512]{2,1,0:T(8,128)}, u32[]{:S(2)}, u32[]{:S(2)}) collective-permute-start(f32[2,128,512]{2,1,0:T(8,128)} %get-tuple-element.49), channel_id=1, source_target_pairs={{17,16},{18,17},{19,18},{20,19},{21,20},{22,21},{23,22},{24,23},{2... | collective-permute-start | bytes 1572872 | tf_op jit(solution)/shard_map/ppermute | solution.py:213
  111.8 14.7 %collective-permute-start.20 = (f32[2,64,512]{2,1,0:T(8,128)S(1)}, f32[2,64,512]{2,1,0:T(8,128)S(1)}, u32[]{:S(2)}, u32[]{:S(2)}) collective-permute-start(f32[2,64,512]{2,1,0:T(8,128)S(1)} %get-tuple-element.55), channel_id=1, source_target_pairs={{0,4},{1,5},{2,6},{3,7},{4,8},{5,9},{6,10},{7,11},{8,12},{9,13},{1... | collective-permute-start | bytes 786440 | tf_op jit(solution)/shard_map/ppermute | solution.py:188
  113.2 19.0 %collective-permute-start.21 = (f32[2,64,512]{2,1,0:T(8,128)S(1)}, f32[2,64,512]{2,1,0:T(8,128)S(1)}, u32[]{:S(2)}, u32[]{:S(2)}) collective-permute-start(f32[2,64,512]{2,1,0:T(8,128)S(1)} %get-tuple-element.56), channel_id=1, source_target_pairs={{0,8},{1,9},{2,10},{3,11},{4,12},{5,13},{6,14},{7,15},{8,0},{9,1},... | collective-permute-start | bytes 786440 | tf_op jit(solution)/shard_map/ppermute | solution.py:188
  114.2 18.0 %collective-permute-start.22 = (f32[2,64,512]{2,1,0:T(8,128)S(1)}, f32[2,64,512]{2,1,0:T(8,128)S(1)}, u32[]{:S(2)}, u32[]{:S(2)}) collective-permute-start(f32[2,64,512]{2,1,0:T(8,128)S(1)} %get-tuple-element.57), channel_id=1, source_target_pairs={{0,12},{1,13},{2,14},{3,15},{4,0},{5,1},{6,2},{7,3},{8,4},{9,5},{1... | collective-permute-start | bytes 786440 | tf_op jit(solution)/shard_map/ppermute | solution.py:188
  116.2 36.8 %collective-permute-start.11 = (f32[2,128,512]{2,1,0:T(8,128)}, f32[2,128,512]{2,1,0:T(8,128)S(1)}, u32[]{:S(2)}, u32[]{:S(2)}) collective-permute-start(f32[2,128,512]{2,1,0:T(8,128)} %copy-done.3), channel_id=1, source_target_pairs={{17,16},{18,17},{19,18},{20,19},{21,20},{22,21},{23,22},{24,23},{2... | collective-permute-start | bytes 1572872 | tf_op jit(solution)/shard_map/ppermute | solution.py:213
  126.5 39.1 %collective-permute-start.17 = (f32[2,128,512]{2,1,0:T(8,128)S(1)}, f32[2,128,512]{2,1,0:T(8,128)S(1)}, u32[]{:S(2)}, u32[]{:S(2)}) collective-permute-start(f32[2,128,512]{2,1,0:T(8,128)S(1)} %get-tuple-element.51), channel_id=1, source_target_pairs={{17,16},{18,17},{19,18},{20,19},{21,20},{22,21},{23,22},{24,23},{2... | collective-permute-start | bytes 1572872 | tf_op jit(solution)/shard_map/ppermute | solution.py:213
  135.3 17.5 %collective-permute-start.28 = (f32[3,16,512]{2,1,0:T(8,128)S(1)}, f32[3,16,512]{2,1,0:T(8,128)S(1)}, u32[]{:S(2)}, u32[]{:S(2)}) collective-permute-start(f32[3,16,512]{2,1,0:T(8,128)S(1)} %get-tuple-element.66), channel_id=1, source_target_pairs={{0,64},{16,80},{32,96},{48,112},{64,0},{80,16},{96,32},{112,48},{1... | collective-permute-start | bytes 294920 | tf_op jit(solution)/shard_map/ppermute | solution.py:182
  137.0 15.7 %collective-permute-start.29 = (f32[3,16,512]{2,1,0:T(8,128)S(1)}, f32[3,16,512]{2,1,0:T(8,128)S(1)}, u32[]{:S(2)}, u32[]{:S(2)}) collective-permute-start(f32[3,16,512]{2,1,0:T(8,128)S(1)} %get-tuple-element.67), channel_id=1, source_target_pairs={{0,96},{16,112},{32,0},{48,16},{64,32},{80,48},{96,64},{112,80},{1... | collective-permute-start | bytes 294920 | tf_op jit(solution)/shard_map/ppermute | solution.py:182
  140.4 36.8 %collective-permute-start.15 = (f32[2,128,512]{2,1,0:T(8,128)S(1)}, f32[2,128,512]{2,1,0:T(8,128)S(1)}, u32[]{:S(2)}, u32[]{:S(2)}) collective-permute-start(f32[2,128,512]{2,1,0:T(8,128)S(1)} %get-tuple-element.50), channel_id=1, source_target_pairs={{17,16},{18,17},{19,18},{20,19},{21,20},{22,21},{23,22},{24,23},{2... | collective-permute-start | bytes 1572872 | tf_op jit(solution)/shard_map/ppermute | solution.py:213
  159.7 37.1 %collective-permute-start.14 = (f32[2,128,512]{2,1,0:T(8,128)S(1)}, f32[2,128,512]{2,1,0:T(8,128)S(1)}, u32[]{:S(2)}, u32[]{:S(2)}) collective-permute-start(f32[2,128,512]{2,1,0:T(8,128)S(1)} %select_add_fusion.2), channel_id=1, source_target_pairs={{0,16},{16,32},{32,48},{48,64},{64,80},{80,96},{96,112},{1,17},{17... | collective-permute-start | bytes 1572872 | tf_op jit(solution)/shard_map/ppermute | solution.py:197
  171.7 25.1 %collective-permute-start.12 = (f32[2,128,512]{2,1,0:T(8,128)S(1)}, f32[2,128,512]{2,1,0:T(8,128)S(1)}, u32[]{:S(2)}, u32[]{:S(2)}) collective-permute-start(f32[2,128,512]{2,1,0:T(8,128)S(1)} %select_add_fusion.3), channel_id=1, source_target_pairs={{0,16},{16,32},{32,48},{48,64},{64,80},{80,96},{96,112},{1,17},{17... | collective-permute-start | bytes 1572872 | tf_op jit(solution)/shard_map/ppermute | solution.py:197
  174.8 14.9 %collective-permute-start.36 = (f32[2,64,512]{2,1,0:T(8,128)S(1)}, f32[2,64,512]{2,1,0:T(8,128)S(1)}, u32[]{:S(2)}, u32[]{:S(2)}) collective-permute-start(f32[2,64,512]{2,1,0:T(8,128)S(1)} %shard_map.89.refs_0_), channel_id=1, source_target_pairs={{0,4},{1,5},{2,6},{3,7},{4,8},{5,9},{6,10},{7,11},{8,12},{9,13},{1... | collective-permute-start | bytes 786440 | tf_op jit(solution)/shard_map/ppermute | solution.py:188
  177.2 16.4 %collective-permute-start.37 = (f32[2,64,512]{2,1,0:T(8,128)S(1)}, f32[2,64,512]{2,1,0:T(8,128)S(1)}, u32[]{:S(2)}, u32[]{:S(2)}) collective-permute-start(f32[2,64,512]{2,1,0:T(8,128)S(1)} %shard_map.89.refs_0_), channel_id=1, source_target_pairs={{0,8},{1,9},{2,10},{3,11},{4,12},{5,13},{6,14},{7,15},{8,0},{9,1},... | collective-permute-start | bytes 786440 | tf_op jit(solution)/shard_map/ppermute | solution.py:188
  177.2 18.3 %collective-permute-start.38 = (f32[2,64,512]{2,1,0:T(8,128)S(1)}, f32[2,64,512]{2,1,0:T(8,128)S(1)}, u32[]{:S(2)}, u32[]{:S(2)}) collective-permute-start(f32[2,64,512]{2,1,0:T(8,128)S(1)} %shard_map.89.refs_0_), channel_id=1, source_target_pairs={{0,12},{1,13},{2,14},{3,15},{4,0},{5,1},{6,2},{7,3},{8,4},{9,5},{1... | collective-permute-start | bytes 786440 | tf_op jit(solution)/shard_map/ppermute | solution.py:188
  (37 other events, 444.9 us)

commit v2 on v1

v2 whole, which is shorter than its diff:
```python
import functools
import math

import jax
import jax.numpy as jnp
import numpy as np
from jax import lax
from jax.experimental import pallas as pl
from jax.experimental.pallas import tpu as pltpu
from jax.sharding import PartitionSpec as P

F = 512
BOUNDS = (0, 192, 352, 512)
SPANS = tuple(zip(BOUNDS[:-1], BOUNDS[1:]))
CHUNKS = len(SPANS)
Y = X = Z = 4
HALF = F // 2
QUARTER, BLOCK = HALF // Z, HALF // Z // Y
F32, BF16 = jnp.float32, jnp.bfloat16
VMEM = pl.BlockSpec(memory_space=pltpu.VMEM)
SMEM = pl.BlockSpec(memory_space=pltpu.SMEM)
ANY = pl.BlockSpec(memory_space=pl.ANY)

ROW, COL, ROW_T, COL_T, CORE, AT_Z, AT_Y, TOUCH = range(8)


def dft_tables():
    idx = np.arange(F)
    angle = (idx[:, None] * idx[None, :] % F) * (2.0 * math.pi / F)
    scale = 1.0 / math.sqrt(F)
    return (
        jnp.asarray((np.cos(angle) * scale).astype(np.float32)).astype(BF16),
        jnp.asarray((-np.sin(angle) * scale).astype(np.float32)).astype(BF16),
    )


def call(kernel, out_shapes, args, after=(), scratch=(), limit=8, space=VMEM, us=0):
    used = len(args)

    def run(*refs):
        kernel(*refs[:used], *refs[used + len(after) :])

    return pl.pallas_call(
        run,
        out_shape=[jax.ShapeDtypeStruct(s, d) for s, d in out_shapes],
        in_specs=[SMEM] + [space] * (used - 1) + [ANY] * len(after),
        out_specs=[VMEM] * len(out_shapes),
        scratch_shapes=list(scratch),
        cost_estimate=pl.CostEstimate(
            flops=1, bytes_accessed=1 + us * 3_500_000, transcendentals=0
        ),
        compiler_params=pltpu.CompilerParams(vmem_limit_bytes=limit * 2**20),
    )(*args, *after)


def iota(shape, dim):
    return lax.broadcasted_iota(jnp.int32, shape, dim)


def back_by(shift):
    return jnp.bitwise_and(F - shift, F - 1)


def prep_kernel(s, wr, wi, probe, col_table, row_table, row_table_t, turned, block):
    r, c = s[ROW], s[COL]
    for k, w in enumerate((wr, wi)):
        w = w[...].astype(F32)
        col_table[k] = pltpu.roll(w, c, 0).astype(BF16)
        row_table[k] = pltpu.roll(w, r, 0).astype(BF16)
        row_table_t[k] = pltpu.roll(w, r, 1).astype(BF16)
        turned[k] = pltpu.roll(pltpu.roll(probe[k], r, 0), c, 1)
    first = s[CORE] * HALF + s[AT_Z] * QUARTER + s[AT_Y] * BLOCK
    block[...] = probe[:, pl.ds(pl.multiple_of(first, BLOCK), BLOCK), :]


def corner(s, which):
    return s[TOUCH + 2 * which], s[TOUCH + 2 * which + 1]


def touch_mask(which, r, c):
    row, col = iota((F, F), 0), iota((F, F), 1)
    inside_rows = row >= r if which < 2 else row < r
    inside_cols = col >= c if which % 2 == 0 else col < c
    return jnp.logical_and(inside_rows, inside_cols)


def probe_light_kernel(s, obj, keep, send):
    value = obj[0] * obj[0] + obj[1] * obj[1]
    total = jnp.zeros((F, F), F32)
    for which in range(4):
        r, c = corner(s, which)
        part = jnp.where(touch_mask(which, r, c), value, 0.0)
        total += pltpu.roll(pltpu.roll(part, back_by(c), 1), back_by(r + s[CORE] * HALF), 0)
    keep[0] = total[:HALF]
    send[0] = total[HALF:]


def light_kernel(s, probe, out):
    power = probe[0] * probe[0] + probe[1] * probe[1]
    total = jnp.zeros((F, F), F32)
    for which in range(4):
        r, c = corner(s, which)
        part = pltpu.roll(pltpu.roll(power, r, 0), c, 1)
        total += jnp.where(touch_mask(which, r, c), part, 0.0)
    out[...] = total


def cut_kernel(s, obj, *refs):
    copies = [
        pltpu.make_async_copy(obj.at[:, first:last], refs[i], refs[CHUNKS].at[i])
        for i, (first, last) in enumerate(SPANS)
    ]
    for copy in copies:
        copy.start()
    for copy in copies:
        copy.wait()


def column_mask(shape, col_at, odd, own):
    col = iota(shape, 1)
    return jnp.logical_xor(col >= col_at, odd if own else jnp.logical_not(odd))


def lend_kernel(span, s, obj, below, out):
    first, last = span
    row = iota((last - first, F), 0) + first
    for k in range(2):
        out[k] = jnp.where(row >= s[ROW_T], obj[k, first:last], below[k])


def half_kernel(span, s, obj, below, beside, turned, table, patch, half):
    first, last = span
    shape = (last - first, F)
    row = iota(shape, 0) + first
    here = column_mask(shape, s[COL], s[CORE] == 1, True)
    m = [
        jnp.where(here, jnp.where(row >= s[ROW], obj[k, first:last], below[k]), beside[k])
        for k in range(2)
    ]
    for k in range(2):
        patch[k] = m[k]
    p_re, p_im = turned[0, first:last], turned[1, first:last]
    psi_re = (p_re * m[0] - p_im * m[1]).astype(BF16)
    psi_im = (p_re * m[1] + p_im * m[0]).astype(BF16)
    psi = jnp.concatenate([psi_re, psi_im], axis=0)
    by_re = jnp.dot(psi, table[0], preferred_element_type=F32)
    by_im = jnp.dot(psi, table[1], preferred_element_type=F32)
    n = last - first
    half[0] = (by_re[:n] - by_im[n:]).astype(BF16)
    half[1] = (by_re[n:] + by_im[:n]).astype(BF16)


def dot_t(a, b):
    return lax.dot_general(a, b, (((1,), (1,)), ((), ())), preferred_element_type=F32)


def fourier_kernel(s, *refs):
    halves, patches = refs[:CHUNKS], refs[CHUNKS : 2 * CHUNKS]
    col_table, row_table, row_table_t, amps, amps_moved = refs[2 * CHUNKS : 2 * CHUNKS + 5]
    err, keep, send, stack, change, back, numer = refs[2 * CHUNKS + 5 :]
    r, c, odd = s[ROW], s[COL], s[CORE] == 1
    for i, (first, last) in enumerate(SPANS):
        for k in range(2):
            stack[first:last, k * F : (k + 1) * F] = halves[i][k]
    wide = 256
    for j in range(0, F, wide):
        at = slice(j, j + wide)
        cols = jnp.concatenate([stack[:, at], stack[:, F + j : F + j + wide]], axis=1)
        by_re = jnp.dot(row_table_t[0], cols, preferred_element_type=F32)
        by_im = jnp.dot(row_table_t[1], cols, preferred_element_type=F32)
        re, im = by_re[:, :wide] - by_im[:, wide:], by_re[:, wide:] + by_im[:, :wide]
        a = jnp.where(odd, amps_moved[0, :, at], amps[0, :, at])
        factor = a / jnp.maximum(jnp.sqrt(re * re + im * im), 0.25) - 1.0
        change[:, :wide] = (factor * re).astype(BF16)
        change[:, wide:] = (factor * im).astype(BF16)
        by_re = jnp.dot(row_table[0], change[...], preferred_element_type=F32)
        by_im = jnp.dot(row_table[1], change[...], preferred_element_type=F32)
        back[0, :, at] = (by_re[:, :wide] + by_im[:, wide:]).astype(BF16)
        back[1, :, at] = (by_re[:, wide:] - by_im[:, :wide]).astype(BF16)
    tall = 128
    for j in range(0, F, tall):
        at = slice(j, j + tall)
        rows = jnp.concatenate([back[0, at], back[1, at]], axis=0)
        by_re, by_im = dot_t(rows, col_table[0]), dot_t(rows, col_table[1])
        re, im = by_re[:tall] + by_im[tall:], by_re[tall:] - by_im[:tall]
        err[0, at] = re
        err[1, at] = im
        for i, (first, last) in enumerate(SPANS):
            low, high = max(first, j), min(last, j + tall)
            if low < high:
                m_re, m_im = (patches[i][k, low - first : high - first] for k in range(2))
                e_re, e_im = re[low - j : high - j], im[low - j : high - j]
                numer[0, low:high] = pltpu.roll(m_re * e_re + m_im * e_im, back_by(c), 1)
                numer[1, low:high] = pltpu.roll(m_re * e_im - m_im * e_re, back_by(c), 1)
    for k in range(2):
        turned_back = pltpu.roll(numer[k], back_by(r + s[CORE] * HALF), 0)
        keep[k] = turned_back[:HALF]
        send[k] = turned_back[HALF:]


def grad_kernel(s, turned, err, grad):
    grad[0] = turned[0] * err[0] + turned[1] * err[1]
    grad[1] = turned[0] * err[1] - turned[1] * err[0]


def fallen_masks(s, below):
    row = iota((F, F), 0)
    odd = s[CORE] == 1
    rows = [row < s[at] if below else row >= s[at] for at in (ROW, ROW_T)]
    here = jnp.logical_and(column_mask((F, F), s[COL], odd, True), rows[0])
    there = jnp.logical_and(column_mask((F, F), s[COL_T], odd, False), rows[1])
    return here, there


def down_kernel(s, grad, moved, down):
    here, there = fallen_masks(s, True)
    for k in range(2):
        down[k] = jnp.where(here, grad[k], 0.0) + jnp.where(there, moved[k], 0.0)


def stay_kernel(s, obj, light, grad, moved, base, scale):
    here, there = fallen_masks(s, False)
    part = 1.0 / (light[...] + 1.0)
    scale[...] = part
    for k in range(2):
        stay = jnp.where(here, grad[k], 0.0) + jnp.where(there, moved[k], 0.0)
        base[k] = obj[k] + stay * part


def object_kernel(s, base, scale, fallen, out):
    for k in range(2):
        out[k] = base[k] + fallen[k] * scale[...]


def turn(value, along, steps):
    if along == "z":
        return lax.ppermute(value, "obj", [(o, (o + 2 * steps) % (2 * Z)) for o in range(2 * Z)])
    pairs = []
    for y in range(Y):
        for x in range(X):
            to = (y, (x + steps) % X) if along == "x" else ((y + steps) % Y, x)
            pairs.append((y * X + x, to[0] * X + to[1]))
    return lax.ppermute(value, "pos", pairs)


def exchange(blocks, along):
    return [blocks[0]] + [turn(blocks[j], along, j) for j in range(1, 4)]


def block_rows(at, j, size):
    return pl.ds(pl.multiple_of(jnp.bitwise_and(at + j, 3) * size, size), size)


def share_kernel(s, numer, numer_got, light, light_got, *outs):
    for j, out in enumerate(outs):
        rows = block_rows(s[AT_Z], j, QUARTER)
        out[:2] = numer[:, rows, :] + numer_got[:, rows, :]
        out[2:] = light[:, rows, :] + light_got[:, rows, :]


def sum_kernel(s, a, b, c, d, *outs):
    for j, out in enumerate(outs):
        rows = block_rows(s[AT_Y], j, BLOCK)
        out[...] = a[:, rows, :] + b[:, rows, :] + c[:, rows, :] + d[:, rows, :]


def add_kernel(s, a, b, c, d, out):
    out[...] = a[...] + b[...] + c[...] + d[...]


def update_kernel(beta, s, a, b, c, d, probe, out):
    total = a[...] + b[...] + c[...] + d[...]
    out[...] = probe[...] + beta * total[:2] / (total[2:3] + 1.0)


def join_kernel(axis, s, *refs):
    for j in range(4):
        refs[4][jnp.bitwise_and(s[axis] - j, 3)] = refs[j][...]


def pair_kernel(s, mine, other, out):
    for ref, half in ((mine, s[CORE]), (other, 1 - s[CORE])):
        for z in range(Z):
            for y in range(Y):
                first = pl.multiple_of(half * HALF + (z * QUARTER + y * BLOCK), BLOCK)
                out[:, pl.ds(first, BLOCK), :] = ref[z, y]


def swap(value):
    return lax.ppermute(value, "obj", [(o, o ^ 1) for o in range(2 * Z)])


def shifted(value, steps):
    n = 2 * Z
    return lax.ppermute(value, "obj", [(o, o + steps) for o in range(n) if 0 <= o + steps < n])


def x_pairs(odd_only=False):
    n = Y * X
    pairs = [(o * n + p, o * n + (p + 1) % n) for o in range(1, 2 * Z, 2) for p in range(n)]
    if not odd_only:
        pairs += [(o * n + p, o * n + p - 1) for o in range(0, 2 * Z, 2) for p in range(1, n)]
    return pairs


def toward(value, odd_only=False):
    return lax.ppermute(value, ("obj", "pos"), x_pairs(odd_only))


def homeward(value):
    return lax.ppermute(value, ("obj", "pos"), [(b, a) for a, b in x_pairs()])


def body(object_field, probe, amplitudes, offsets):
    row_index = lax.axis_index("obj")
    col_index = lax.axis_index("pos")
    core, z, y = row_index % 2, row_index // 2, col_index // X
    place_here = jnp.stack([core, z, y])
    own = offsets[0] - jnp.stack([row_index * F, col_index * F])
    n = Y * X
    left = lax.ppermute(own, "pos", [(p, (p + 1) % n) for p in range(n)])
    above = shifted(jnp.concatenate([own, left]), 1)
    odd = core == 1
    mine, target = jnp.where(odd, left, own), jnp.where(odd, own, left)
    s = jnp.concatenate([mine, target, place_here]).astype(jnp.int32)
    touch = jnp.concatenate([s, own, left, above]).astype(jnp.int32)

    shapes = [((2, last - first, F), F32) for first, last in SPANS]

    tiles = call(
        cut_kernel,
        shapes,
        (own, object_field),
        scratch=[pltpu.SemaphoreType.DMA((CHUNKS,))],
        space=ANY,
    )
    below = [shifted(tile, -1) for tile in tiles]
    amps_moved = toward(amplitudes, odd_only=True)
    lent, beside = [], []

    def lend(i, after):
        lent.extend(
            call(
                functools.partial(lend_kernel, SPANS[i]),
                [shapes[i]],
                (s, object_field, below[i]),
                after=after,
            )
        )
        beside.append(toward(lent[i]))

    lend(0, (amps_moved,))
    lend(1, (lent[0],))
    wr, wi = dft_tables()
    square = ((2, F, F), BF16)
    col_table, row_table, row_table_t, turned, probe_block = call(
        prep_kernel,
        [square] * 3 + [((2, F, F), F32), ((2, BLOCK, F), F32)],
        (s, wr, wi, probe),
        after=(lent[1],),
        limit=16,
    )
    lend(2, (turned,))
    seen, seen_send = call(
        probe_light_kernel,
        [((1, HALF, F), F32)] * 2,
        (touch, object_field),
        after=(lent[2],),
        limit=16,
        us=5,
    )

    patches, halves = [], []
    for i, span in enumerate(SPANS):
        patch, half = call(
            functools.partial(half_kernel, span),
            [shapes[i], (shapes[i][0], BF16)],
            (s, object_field, below[i], beside[i], turned, col_table),
            after=(lent[-1],),
            limit=16,
            us=0 if i == CHUNKS - 1 else 2,
        )
        patches.append(patch)
        halves.append(half)

    err, keep, send = call(
        fourier_kernel,
        [((2, F, F), F32)] + [((2, HALF, F), F32)] * 2,
        (s, *halves, *patches, col_table, row_table, row_table_t, amplitudes, amps_moved),
        after=(seen,),
        limit=24,
        scratch=[
            pltpu.VMEM((F, 2 * F), BF16),
            pltpu.VMEM((F, F), BF16),
            pltpu.VMEM((2, F, F), BF16),
            pltpu.VMEM((2, F, F), F32),
        ],
    )

    (grad,) = call(grad_kernel, [((2, F, F), F32)], (s, turned, err), us=3)
    moved = homeward(grad)
    (light,) = call(light_kernel, [((F, F), F32)], (touch, probe), after=(keep,), limit=16)
    quarter, block = ((3, QUARTER, F), F32), ((3, BLOCK, F), F32)
    parts = call(share_kernel, [quarter] * 4, (s, keep, swap(send), seen, swap(seen_send)))
    parts = call(sum_kernel, [block] * 4, (s, *exchange(parts, "z")), after=(light,))
    (down,) = call(down_kernel, [((2, F, F), F32)], (s, grad, moved), after=(parts[0],))
    fallen = shifted(down, 1)
    (share,) = call(add_kernel, [block], (s, *exchange(parts, "y")), after=(down,))
    beta = 0.5 * math.sqrt(2 * X * Y * Z)
    (fresh,) = call(
        functools.partial(update_kernel, beta),
        [((2, BLOCK, F), F32)],
        (s, *exchange([share] * 4, "x"), probe_block),
    )
    base, scale = call(
        stay_kernel,
        [((2, F, F), F32), ((F, F), F32)],
        (s, object_field, light, grad, moved),
        after=(share,),
    )
    (fresh,) = call(
        functools.partial(join_kernel, AT_Y),
        [((4,) + fresh.shape, F32)],
        (s, *exchange([fresh] * 4, "y")),
        after=(base,),
    )
    (new_object,) = call(object_kernel, [((2, F, F), F32)], (s, base, scale, fallen))
    (fresh,) = call(
        functools.partial(join_kernel, AT_Z),
        [((4,) + fresh.shape, F32)],
        (s, *exchange([fresh] * 4, "z")),
        after=(new_object,),
    )
    (new_probe,) = call(pair_kernel, [((2, F, F), F32)], (s, fresh, swap(fresh)))
    return (new_object, new_probe)


def solution(mesh):
    in_specs = (P(None, "obj", "pos"), P(), P(("obj", "pos"), None, None), P(("obj", "pos"), None))
    out_specs = (P(None, "obj", "pos"), P())
    return jax.shard_map(body, mesh=mesh, in_specs=in_specs, out_specs=out_specs, check_vma=False)
```

time: 210 us -> 155 us (0.74)
  starting transfers between devices: 91 us -> 53.1 us
  other arithmetic: 20.1 us -> 0.88 us
  local copies, waits for them, and re-layouts: 11.8 us -> 3.72 us
  waiting for transfers between devices: 42 us -> 49.8 us
  Pallas kernels: 40.2 us -> 45.5 us
  between operations: 3.98 us -> 1.06 us
    ppermute x4 -> x1, starting transfers between devices: 24.7 us -> 4.01 us  [homeward(): return lax.ppermute(value, ('obj', 'pos'), [(b, a) for a, b in x_pairs()])]
    ppermute x9 -> x5, waiting for transfers between devices: 21.1 us -> 4.14 us  [shifted(): lax.ppermute(value, 'obj', [(o, o + steps) for o in range(n) if 0 <= o +...]
    ppermute x6, waiting for transfers between devices: 4.56 us -> 20 us  [turn(): lax.ppermute(value, 'obj', [(o, (o + 2 * steps) % (2 * Z)) for o in range...]
    ppermute x9 -> x5, starting transfers between devices: 21.9 us -> 11.7 us  [shifted(): lax.ppermute(value, 'obj', [(o, o + steps) for o in range(n) if 0 <= o +...]
    ppermute x12 -> x9, starting transfers between devices: 16.6 us -> 10.7 us  [turn(): return lax.ppermute(value, 'pos', pairs)]
    pallas_call x14 -> x22, Pallas kernels: 40.2 us -> 45.5 us  [call(): pl.pallas_call(run, out_shape=[jax.ShapeDtypeStruct(s, d) for s, d in out...]
    ppermute x3, waiting for transfers between devices: 0.01 us -> 5.19 us  [swap(): return lax.ppermute(value, 'obj', [(o, o ^ 1) for o in range(2 * Z)])]
    ge x5 -> x0, other arithmetic: 4.97 us -> none  [the longest x3 3.75 us: body(): rows[i] >= mine[0]]
  transfers between devices with their start and end apart: 40 -> 29, of which waited for: 10 -> 19; matrix products, arithmetic and copies ran while one was open for 11% -> 1% of each run, Pallas kernels for 14% -> 21%
where the time goes in v2:
time: 155 us; the launch traced here: 154 us
  starting transfers between devices  53.1 us (34%)
  waiting for transfers between devices  49.8 us (32%)
  Pallas kernels  45.5 us (29%)
  local copies, waits for them, and re-layouts  3.72 us (2%)
    pallas_call x22, Pallas kernels, call(): pl.pallas_call(run, out_shape=[jax.ShapeDtypeStruct(s, d) for s, d in out...  45.5 us
    ppermute x6, waiting for transfers between devices, turn(): lax.ppermute(value, 'obj', [(o, (o + 2 * steps) % (2 * Z)) for o in range...  20 us
    ppermute x9, waiting for transfers between devices, turn(): return lax.ppermute(value, 'pos', pairs)  13.7 us
    ppermute x4, starting transfers between devices, toward(): return lax.ppermute(value, ('obj', 'pos'), x_pairs(odd_only))  13.3 us
    ppermute x5, starting transfers between devices, shifted(): lax.ppermute(value, 'obj', [(o, o + steps) for o in range(n) if 0 <= o +...  11.7 us
    ppermute x9, starting transfers between devices, turn(): return lax.ppermute(value, 'pos', pairs)  10.7 us
    ppermute x6, starting transfers between devices, turn(): lax.ppermute(value, 'obj', [(o, (o + 2 * steps) % (2 * Z)) for o in range...  9.41 us
    ppermute x3, waiting for transfers between devices, swap(): return lax.ppermute(value, 'obj', [(o, o ^ 1) for o in range(2 * Z)])  5.19 us
  transfers between devices with their start and end apart: 29, of which 19 were waited for; matrix products, arithmetic and copies ran while one was open for 1% of the time, Pallas kernels for 21%

profile of v2, /device:TPU:1, one launch (start us, length us, event | category | flops | bytes accessed | tf_op | source)
XLA Modules:
  0.0 154.1 jit_solution(6935201803110320815)
XLA Ops:
  0.6 4.0 %collective-permute-start.3 = (f32[1,512,512]{2,1,0:T(8,128)}, f32[1,512,512]{2,1,0:T(8,128)S(1)}, u32[]{:S(2)}, u32[]{:S(2)}) collective-permute-start(f32[1,512,512]{2,1,0:T(8,128)} %refs_10_.1), channel_id=1, source_target_pairs={{16,17},{17,18},{18,19},{19,20},{20,21},{21,22},{22,23},{23,24},{2... | collective-permute-start | bytes 3145736 | tf_op jit(solution)/shard_map/ppermute | solution.py:307
  16.2 4.6 %collective-permute-done = s32[2]{0:T(128)S(1)} collective-permute-done((s32[2]{0:T(128)S(1)}, s32[2]{0:T(128)S(1)}, u32[]{:S(2)}, u32[]{:S(2)}) %collective-permute-start) | collective-permute-done | bytes 40 | tf_op jit(solution)/shard_map/ppermute | solution.py:321
  22.8 2.5 %shard_map.78.refs_3_ = f32[2,192,512]{2,1,0:T(8,128)} custom-call(s32[7]{0:T(128)S(1)} %concatenate.10.refs_0_, f32[2,512,512]{2,1,0:T(8,128)S(1)} %copy-done.1, f32[2,192,512]{2,1,0:T(8,128)} %collective-permute-done.2.refs_2_, f32[1,512,512]{2,1,0:T(8,128)S(1)} %collective-permute-done.3.refs_3_.refs_11_), custom_call_target="tpu_custom_call" | custom-call | flops 1 | bytes 1 | tf_op jit(solution)/shard_map/pallas_call | solution.py:43
  25.3 3.4 %collective-permute-start.4 = (f32[2,192,512]{2,1,0:T(8,128)}, f32[2,192,512]{2,1,0:T(8,128)}, u32[]{:S(2)}, u32[]{:S(2)}) collective-permute-start(f32[2,192,512]{2,1,0:T(8,128)} %shard_map.78.refs_3_), channel_id=1, source_target_pairs={{16,17},{17,18},{18,19},{19,20},{20,21},{21,22},{22,23},{23,24},{2... | collective-permute-start | bytes 2359304 | tf_op jit(solution)/shard_map/ppermute | solution.py:307
  32.2 3.1 %collective-permute-start.7 = (f32[2,160,512]{2,1,0:T(8,128)}, f32[2,160,512]{2,1,0:T(8,128)}, u32[]{:S(2)}, u32[]{:S(2)}) collective-permute-start(f32[2,160,512]{2,1,0:T(8,128)} %shard_map.79.refs_4_), channel_id=1, source_target_pairs={{16,17},{17,18},{18,19},{19,20},{20,21},{21,22},{22,23},{23,24},{2... | collective-permute-start | bytes 1966088 | tf_op jit(solution)/shard_map/ppermute | solution.py:307
  35.3 4.5 %shard_map.80 = (bf16[2,512,512]{2,1,0:T(8,128)(2,1)S(1)}, bf16[2,512,512]{2,1,0:T(8,128)(2,1)S(1)}, bf16[2,512,512]{2,1,0:T(8,128)(2,1)S(1)}, f32[2,512,512]{2,1,0:T(8,128)S(1)}, f32[2,16,512]{2,1,0:T(8,128)S(1)}) custom-call(s32[7]{0:T(128)S(1)} %concatenate.10.refs_0_, bf16[512,512]{1,0:T(8,128)(2,1)S(1)} %copy-done.15, bf16[512,512]{1,0:T(8,128)(2,1)S(1)} %copy-done.14, ...), custom_call_target="tpu_custom_call" | custom-call | flops 1 | bytes 1 | tf_op jit(solution)/shard_map/pallas_call | solution.py:43
  39.9 2.5 %shard_map.81.refs_6_.refs_2_ = f32[2,160,512]{2,1,0:T(8,128)} custom-call(s32[7]{0:T(128)S(1)} %concatenate.10.refs_0_, f32[2,512,512]{2,1,0:T(8,128)S(1)} %copy-done.1, f32[2,160,512]{2,1,0:T(8,128)} %collective-permute-done.6.refs_2_, f32[2,512,512]{2,1,0:T(8,128)S(1)} %get-tuple-element.33.refs_3_.refs_4_.refs_1_), custom_call_target="tpu_custom_call" | custom-call | flops 1 | bytes 1 | tf_op jit(solution)/shard_map/pallas_call | solution.py:43
  42.4 2.8 %collective-permute-start.8 = (f32[2,160,512]{2,1,0:T(8,128)}, f32[2,160,512]{2,1,0:T(8,128)}, u32[]{:S(2)}, u32[]{:S(2)}) collective-permute-start(f32[2,160,512]{2,1,0:T(8,128)} %shard_map.81.refs_6_.refs_2_), channel_id=1, source_target_pairs={{16,17},{17,18},{18,19},{19,20},{20,21},{21,22},{22,23},{23,24},{2... | collective-permute-start | bytes 1966088 | tf_op jit(solution)/shard_map/ppermute | solution.py:307
  48.4 4.8 %shard_map.85 = (f32[1,256,512]{2,1,0:T(8,128)S(1)}, f32[1,256,512]{2,1,0:T(8,128)S(1)}) custom-call(s32[15]{0:T(128)S(1)} %concatenate.12.refs_0_, f32[2,512,512]{2,1,0:T(8,128)S(1)} %copy-done.1, f32[2,160,512]{2,1,0:T(8,128)} %shard_map.81.refs_6_.refs_2_), custom_call_target="tpu_custom_call" | custom-call | flops 1 | bytes 17500000 | tf_op jit(solution)/shard_map/pallas_call | solution.py:43
  59.3 2.3 %shard_map.82 = (f32[2,192,512]{2,1,0:T(8,128)S(1)}, bf16[2,192,512]{2,1,0:T(8,128)(2,1)S(1)}) custom-call(s32[7]{0:T(128)S(1)} %concatenate.10.refs_0_, f32[2,512,512]{2,1,0:T(8,128)S(1)} %copy-done.1, f32[2,192,512]{2,1,0:T(8,128)} %collective-permute-done.2.refs_2_, f32[2,192,512]{2,1,0:T(8,128)} %collective-permute-done.4.refs_3_, ...), custom_call_target="tpu_custom_call" | custom-call | flops 1 | bytes 7000001 | tf_op jit(solution)/shard_map/pallas_call | solution.py:43
  61.9 5.8 %shard_map.86 = (f32[2,512,512]{2,1,0:T(8,128)S(1)}, f32[2,256,512]{2,1,0:T(8,128)S(1)}, f32[2,256,512]{2,1,0:T(8,128)S(1)}) custom-call(s32[7]{0:T(128)S(1)} %concatenate.10.refs_0_, bf16[2,192,512]{2,1,0:T(8,128)(2,1)S(1)} %get-tuple-element.36.refs_1_, bf16[2,160,512]{2,1,0:T(8,128)(2,1)S(1)} %get-tuple-element.37.refs_2_, ...), custom_call_target="tpu_custom_call" | custom-call | flops 1 | bytes 1 | tf_op jit(solution)/shard_map/pallas_call | solution.py:43
  68.7 4.0 %collective-permute-start.9 = (f32[2,512,512]{2,1,0:T(8,128)S(1)}, f32[2,512,512]{2,1,0:T(8,128)S(1)}, u32[]{:S(2)}, u32[]{:S(2)}) collective-permute-start(f32[2,512,512]{2,1,0:T(8,128)S(1)} %shard_map.88.refs_1_.refs_3_), channel_id=1, source_target_pairs={{17,16},{18,17},{19,18},{20,19},{21,20},{22,21},{23,22},{24,23},{2... | collective-permute-start | bytes 6291464 | tf_op jit(solution)/shard_map/ppermute | solution.py:311
  73.3 2.9 %collective-permute-done.11.refs_4_ = f32[1,256,512]{2,1,0:T(8,128)S(1)} collective-permute-done((f32[1,256,512]{2,1,0:T(8,128)S(1)}, f32[1,256,512]{2,1,0:T(8,128)S(1)}, u32[]{:S(2)}, u32[]{:S(2)}) %collective-permute-start.11) | collective-permute-done | bytes 524320 | tf_op jit(solution)/shard_map/ppermute | solution.py:290
  82.9 3.9 %shard_map.87.refs_5_.refs_2_ = f32[512,512]{1,0:T(8,128)S(1)} custom-call(s32[15]{0:T(128)S(1)} %concatenate.12.refs_0_, f32[2,512,512]{2,1,0:T(8,128)S(1)} %copy-done.5, f32[2,256,512]{2,1,0:T(8,128)S(1)} %get-tuple-element.45.refs_2_.refs_1_), custom_call_target="tpu_custom_call" | custom-call | flops 1 | bytes 1 | tf_op jit(solution)/shard_map/pallas_call | solution.py:43
  89.0 9.4 %collective-permute-done.13.refs_3_ = f32[3,64,512]{2,1,0:T(8,128)S(1)} collective-permute-done((f32[3,64,512]{2,1,0:T(8,128)S(1)}, f32[3,64,512]{2,1,0:T(8,128)S(1)}, u32[]{:S(2)}, u32[]{:S(2)}) %collective-permute-start.13) | collective-permute-done | bytes 393248 | tf_op jit(solution)/shard_map/ppermute | solution.py:237
  100.1 3.9 %collective-permute-start.18 = (f32[2,512,512]{2,1,0:T(8,128)S(1)}, f32[2,512,512]{2,1,0:T(8,128)S(1)}, u32[]{:S(2)}, u32[]{:S(2)}) collective-permute-start(f32[2,512,512]{2,1,0:T(8,128)S(1)} %shard_map.91.refs_5_), channel_id=1, source_target_pairs={{0,16},{16,32},{32,48},{48,64},{64,80},{80,96},{96,112},{1,17},{17... | collective-permute-start | bytes 6291464 | tf_op jit(solution)/shard_map/ppermute | solution.py:295
  104.6 2.6 %collective-permute-start.16 = (f32[3,16,512]{2,1,0:T(8,128)S(1)}, f32[3,16,512]{2,1,0:T(8,128)S(1)}, u32[]{:S(2)}, u32[]{:S(2)}) collective-permute-start(f32[3,16,512]{2,1,0:T(8,128)S(1)} %get-tuple-element.55), channel_id=1, source_target_pairs={{0,8},{1,9},{2,10},{3,11},{4,12},{5,13},{6,14},{7,15},{8,0},{9,1},... | collective-permute-start | bytes 294920 | tf_op jit(solution)/shard_map/ppermute | solution.py:243
  116.7 3.1 %collective-permute-done.20.refs_3_ = f32[3,16,512]{2,1,0:T(8,128)S(1)} collective-permute-done((f32[3,16,512]{2,1,0:T(8,128)S(1)}, f32[3,16,512]{2,1,0:T(8,128)S(1)}, u32[]{:S(2)}, u32[]{:S(2)}) %collective-permute-start.20) | collective-permute-done | bytes 98336 | tf_op jit(solution)/shard_map/ppermute | solution.py:243
  119.8 2.3 %collective-permute-done.19.refs_2_ = f32[3,16,512]{2,1,0:T(8,128)S(1)} collective-permute-done((f32[3,16,512]{2,1,0:T(8,128)S(1)}, f32[3,16,512]{2,1,0:T(8,128)S(1)}, u32[]{:S(2)}, u32[]{:S(2)}) %collective-permute-start.19) | collective-permute-done | bytes 98336 | tf_op jit(solution)/shard_map/ppermute | solution.py:243
  122.6 2.9 %collective-permute-start.24 = (f32[2,16,512]{2,1,0:T(8,128)S(1)}, f32[2,16,512]{2,1,0:T(8,128)S(1)}, u32[]{:S(2)}, u32[]{:S(2)}) collective-permute-start(f32[2,16,512]{2,1,0:T(8,128)S(1)} %shard_map.95.refs_1_), channel_id=1, source_target_pairs={{0,12},{1,13},{2,14},{3,15},{4,0},{5,1},{6,2},{7,3},{8,4},{9,5},{1... | collective-permute-start | bytes 196616 | tf_op jit(solution)/shard_map/ppermute | solution.py:243
  127.9 2.4 %collective-permute-done.23.refs_3_ = f32[2,16,512]{2,1,0:T(8,128)S(1)} collective-permute-done((f32[2,16,512]{2,1,0:T(8,128)S(1)}, f32[2,16,512]{2,1,0:T(8,128)S(1)}, u32[]{:S(2)}, u32[]{:S(2)}) %collective-permute-start.23) | collective-permute-done | bytes 65568 | tf_op jit(solution)/shard_map/ppermute | solution.py:243
  131.5 2.6 %collective-permute-start.26 = (f32[4,2,16,512]{3,2,1,0:T(8,128)S(1)}, f32[4,2,16,512]{3,2,1,0:T(8,128)S(1)}, u32[]{:S(2)}, u32[]{:S(2)}) collective-permute-start(f32[4,2,16,512]{3,2,1,0:T(8,128)S(1)} %shard_map.96.refs_1_), channel_id=1, source_target_pairs={{0,64},{16,80},{32,96},{48,112},{64,0},{80,16},{96,32},{112,48},{1... | collective-permute-start | bytes 786440 | tf_op jit(solution)/shard_map/ppermute | solution.py:237
  138.4 7.1 %collective-permute-done.25.refs_2_ = f32[4,2,16,512]{3,2,1,0:T(8,128)S(1)} collective-permute-done((f32[4,2,16,512]{3,2,1,0:T(8,128)S(1)}, f32[4,2,16,512]{3,2,1,0:T(8,128)S(1)}, u32[]{:S(2)}, u32[]{:S(2)}) %collective-permute-start.25) | collective-permute-done | bytes 262176 | tf_op jit(solution)/shard_map/ppermute | solution.py:237
  149.7 2.3 %collective-permute-done.28.refs_2_ = f32[4,4,2,16,512]{4,3,2,1,0:T(8,128)S(1)} collective-permute-done((f32[4,4,2,16,512]{4,3,2,1,0:T(8,128)S(1)}, f32[4,4,2,16,512]{4,3,2,1,0:T(8,128)S(1)}, u32[]{:S(2)}, u32[]{:S(2)}) %collective-permute-start.28) | collective-permute-done | bytes 1048608 | tf_op jit(solution)/shard_map/ppermute | solution.py:290
  (95 shorter events, 63.5 us)
Async XLA Ops:
  0.6 22.1 %collective-permute-start.3 = (f32[1,512,512]{2,1,0:T(8,128)}, f32[1,512,512]{2,1,0:T(8,128)S(1)}, u32[]{:S(2)}, u32[]{:S(2)}) collective-permute-start(f32[1,512,512]{2,1,0:T(8,128)} %refs_10_.1), channel_id=1, source_target_pairs={{16,17},{17,18},{18,19},{19,20},{20,21},{21,22},{22,23},{23,24},{2... | collective-permute-start | bytes 3145736 | tf_op jit(solution)/shard_map/ppermute | solution.py:307
  9.1 13.6 %collective-permute-start.2 = (f32[2,192,512]{2,1,0:T(8,128)}, f32[2,192,512]{2,1,0:T(8,128)}, u32[]{:S(2)}, u32[]{:S(2)}) collective-permute-start(f32[2,192,512]{2,1,0:T(8,128)} %get-tuple-element.31), channel_id=1, source_target_pairs={{16,0},{32,16},{48,32},{64,48},{80,64},{96,80},{112,96},{17,1},{33... | collective-permute-start | bytes 2359304 | tf_op jit(solution)/shard_map/ppermute | solution.py:295
  11.1 19.0 %collective-permute-start.5 = (f32[2,160,512]{2,1,0:T(8,128)}, f32[2,160,512]{2,1,0:T(8,128)}, u32[]{:S(2)}, u32[]{:S(2)}) collective-permute-start(f32[2,160,512]{2,1,0:T(8,128)} %get-tuple-element.32), channel_id=1, source_target_pairs={{16,0},{32,16},{48,32},{64,48},{80,64},{96,80},{112,96},{17,1},{33... | collective-permute-start | bytes 1966088 | tf_op jit(solution)/shard_map/ppermute | solution.py:295
  13.0 26.9 %collective-permute-start.6 = (f32[2,160,512]{2,1,0:T(8,128)}, f32[2,160,512]{2,1,0:T(8,128)}, u32[]{:S(2)}, u32[]{:S(2)}) collective-permute-start(f32[2,160,512]{2,1,0:T(8,128)} %get-tuple-element.35), channel_id=1, source_target_pairs={{16,0},{32,16},{48,32},{64,48},{80,64},{96,80},{112,96},{17,1},{33... | collective-permute-start | bytes 1966088 | tf_op jit(solution)/shard_map/ppermute | solution.py:295
  14.9 5.9 %collective-permute-start = (s32[2]{0:T(128)S(1)}, s32[2]{0:T(128)S(1)}, u32[]{:S(2)}, u32[]{:S(2)}) collective-permute-start(s32[2]{0:T(128)S(1)} %add_subtract_fusion.refs_0_), channel_id=1, source_target_pairs={{0,1},{1,2},{2,3},{3,4},{4,5},{5,6},{6,7},{7,8},{8,9},{9,10},{10,1... | collective-permute-start | bytes 32 | tf_op jit(solution)/shard_map/ppermute | solution.py:321
  25.3 34.0 %collective-permute-start.4 = (f32[2,192,512]{2,1,0:T(8,128)}, f32[2,192,512]{2,1,0:T(8,128)}, u32[]{:S(2)}, u32[]{:S(2)}) collective-permute-start(f32[2,192,512]{2,1,0:T(8,128)} %shard_map.78.refs_3_), channel_id=1, source_target_pairs={{16,17},{17,18},{18,19},{19,20},{20,21},{21,22},{22,23},{23,24},{2... | collective-permute-start | bytes 2359304 | tf_op jit(solution)/shard_map/ppermute | solution.py:307
  32.2 21.0 %collective-permute-start.7 = (f32[2,160,512]{2,1,0:T(8,128)}, f32[2,160,512]{2,1,0:T(8,128)}, u32[]{:S(2)}, u32[]{:S(2)}) collective-permute-start(f32[2,160,512]{2,1,0:T(8,128)} %shard_map.79.refs_4_), channel_id=1, source_target_pairs={{16,17},{17,18},{18,19},{19,20},{20,21},{21,22},{22,23},{23,24},{2... | collective-permute-start | bytes 1966088 | tf_op jit(solution)/shard_map/ppermute | solution.py:307
  42.4 15.0 %collective-permute-start.8 = (f32[2,160,512]{2,1,0:T(8,128)}, f32[2,160,512]{2,1,0:T(8,128)}, u32[]{:S(2)}, u32[]{:S(2)}) collective-permute-start(f32[2,160,512]{2,1,0:T(8,128)} %shard_map.81.refs_6_.refs_2_), channel_id=1, source_target_pairs={{16,17},{17,18},{18,19},{19,20},{20,21},{21,22},{22,23},{23,24},{2... | collective-permute-start | bytes 1966088 | tf_op jit(solution)/shard_map/ppermute | solution.py:307
  68.7 30.3 %collective-permute-start.9 = (f32[2,512,512]{2,1,0:T(8,128)S(1)}, f32[2,512,512]{2,1,0:T(8,128)S(1)}, u32[]{:S(2)}, u32[]{:S(2)}) collective-permute-start(f32[2,512,512]{2,1,0:T(8,128)S(1)} %shard_map.88.refs_1_.refs_3_), channel_id=1, source_target_pairs={{17,16},{18,17},{19,18},{20,19},{21,20},{22,21},{23,22},{24,23},{2... | collective-permute-start | bytes 6291464 | tf_op jit(solution)/shard_map/ppermute | solution.py:311
  76.9 12.1 %collective-permute-start.12 = (f32[3,64,512]{2,1,0:T(8,128)S(1)}, f32[3,64,512]{2,1,0:T(8,128)S(1)}, u32[]{:S(2)}, u32[]{:S(2)}) collective-permute-start(f32[3,64,512]{2,1,0:T(8,128)S(1)} %get-tuple-element.50), channel_id=1, source_target_pairs={{0,32},{16,48},{32,64},{48,80},{64,96},{80,112},{96,0},{112,16},{1... | collective-permute-start | bytes 1179656 | tf_op jit(solution)/shard_map/ppermute | solution.py:237
  78.9 19.5 %collective-permute-start.13 = (f32[3,64,512]{2,1,0:T(8,128)S(1)}, f32[3,64,512]{2,1,0:T(8,128)S(1)}, u32[]{:S(2)}, u32[]{:S(2)}) collective-permute-start(f32[3,64,512]{2,1,0:T(8,128)S(1)} %get-tuple-element.51), channel_id=1, source_target_pairs={{0,64},{16,80},{32,96},{48,112},{64,0},{80,16},{96,32},{112,48},{1... | collective-permute-start | bytes 1179656 | tf_op jit(solution)/shard_map/ppermute | solution.py:237
  80.9 17.5 %collective-permute-start.14 = (f32[3,64,512]{2,1,0:T(8,128)S(1)}, f32[3,64,512]{2,1,0:T(8,128)S(1)}, u32[]{:S(2)}, u32[]{:S(2)}) collective-permute-start(f32[3,64,512]{2,1,0:T(8,128)S(1)} %get-tuple-element.52), channel_id=1, source_target_pairs={{0,96},{16,112},{32,0},{48,16},{64,32},{80,48},{96,64},{112,80},{1... | collective-permute-start | bytes 1179656 | tf_op jit(solution)/shard_map/ppermute | solution.py:237
  100.1 34.8 %collective-permute-start.18 = (f32[2,512,512]{2,1,0:T(8,128)S(1)}, f32[2,512,512]{2,1,0:T(8,128)S(1)}, u32[]{:S(2)}, u32[]{:S(2)}) collective-permute-start(f32[2,512,512]{2,1,0:T(8,128)S(1)} %shard_map.91.refs_5_), channel_id=1, source_target_pairs={{0,16},{16,32},{32,48},{48,64},{64,80},{80,96},{96,112},{1,17},{17... | collective-permute-start | bytes 6291464 | tf_op jit(solution)/shard_map/ppermute | solution.py:295
  104.0 5.6 %collective-permute-start.15 = (f32[3,16,512]{2,1,0:T(8,128)S(1)}, f32[3,16,512]{2,1,0:T(8,128)S(1)}, u32[]{:S(2)}, u32[]{:S(2)}) collective-permute-start(f32[3,16,512]{2,1,0:T(8,128)S(1)} %get-tuple-element.54), channel_id=1, source_target_pairs={{0,4},{1,5},{2,6},{3,7},{4,8},{5,9},{6,10},{7,11},{8,12},{9,13},{1... | collective-permute-start | bytes 294920 | tf_op jit(solution)/shard_map/ppermute | solution.py:243
  104.6 6.9 %collective-permute-start.16 = (f32[3,16,512]{2,1,0:T(8,128)S(1)}, f32[3,16,512]{2,1,0:T(8,128)S(1)}, u32[]{:S(2)}, u32[]{:S(2)}) collective-permute-start(f32[3,16,512]{2,1,0:T(8,128)S(1)} %get-tuple-element.55), channel_id=1, source_target_pairs={{0,8},{1,9},{2,10},{3,11},{4,12},{5,13},{6,14},{7,15},{8,0},{9,1},... | collective-permute-start | bytes 294920 | tf_op jit(solution)/shard_map/ppermute | solution.py:243
  107.3 4.7 %collective-permute-start.17 = (f32[3,16,512]{2,1,0:T(8,128)S(1)}, f32[3,16,512]{2,1,0:T(8,128)S(1)}, u32[]{:S(2)}, u32[]{:S(2)}) collective-permute-start(f32[3,16,512]{2,1,0:T(8,128)S(1)} %get-tuple-element.56), channel_id=1, source_target_pairs={{0,12},{1,13},{2,14},{3,15},{4,0},{5,1},{6,2},{7,3},{8,4},{9,5},{1... | collective-permute-start | bytes 294920 | tf_op jit(solution)/shard_map/ppermute | solution.py:243
  114.3 5.5 %collective-permute-start.20 = (f32[3,16,512]{2,1,0:T(8,128)S(1)}, f32[3,16,512]{2,1,0:T(8,128)S(1)}, u32[]{:S(2)}, u32[]{:S(2)}) collective-permute-start(f32[3,16,512]{2,1,0:T(8,128)S(1)} %shard_map.92.refs_5_.refs_1_), channel_id=1, source_target_pairs={{0,2},{1,3},{2,0},{3,1},{4,6},{5,7},{6,4},{7,5},{8,10},{9,11},{10,... | collective-permute-start | bytes 294920 | tf_op jit(solution)/shard_map/ppermute | solution.py:243
  114.3 7.7 %collective-permute-start.19 = (f32[3,16,512]{2,1,0:T(8,128)S(1)}, f32[3,16,512]{2,1,0:T(8,128)S(1)}, u32[]{:S(2)}, u32[]{:S(2)}) collective-permute-start(f32[3,16,512]{2,1,0:T(8,128)S(1)} %shard_map.92.refs_5_.refs_1_), channel_id=1, source_target_pairs={{0,1},{1,2},{2,3},{3,0},{4,5},{5,6},{6,7},{7,4},{8,9},{9,10},{10,1... | collective-permute-start | bytes 294920 | tf_op jit(solution)/shard_map/ppermute | solution.py:243
  122.6 5.2 %collective-permute-start.24 = (f32[2,16,512]{2,1,0:T(8,128)S(1)}, f32[2,16,512]{2,1,0:T(8,128)S(1)}, u32[]{:S(2)}, u32[]{:S(2)}) collective-permute-start(f32[2,16,512]{2,1,0:T(8,128)S(1)} %shard_map.95.refs_1_), channel_id=1, source_target_pairs={{0,12},{1,13},{2,14},{3,15},{4,0},{5,1},{6,2},{7,3},{8,4},{9,5},{1... | collective-permute-start | bytes 196616 | tf_op jit(solution)/shard_map/ppermute | solution.py:243
  125.6 4.7 %collective-permute-start.23 = (f32[2,16,512]{2,1,0:T(8,128)S(1)}, f32[2,16,512]{2,1,0:T(8,128)S(1)}, u32[]{:S(2)}, u32[]{:S(2)}) collective-permute-start(f32[2,16,512]{2,1,0:T(8,128)S(1)} %shard_map.95.refs_1_), channel_id=1, source_target_pairs={{0,8},{1,9},{2,10},{3,11},{4,12},{5,13},{6,14},{7,15},{8,0},{9,1},... | collective-permute-start | bytes 196616 | tf_op jit(solution)/shard_map/ppermute | solution.py:243
  126.2 4.7 %collective-permute-start.22 = (f32[2,16,512]{2,1,0:T(8,128)S(1)}, f32[2,16,512]{2,1,0:T(8,128)S(1)}, u32[]{:S(2)}, u32[]{:S(2)}) collective-permute-start(f32[2,16,512]{2,1,0:T(8,128)S(1)} %shard_map.95.refs_1_), channel_id=1, source_target_pairs={{0,4},{1,5},{2,6},{3,7},{4,8},{5,9},{6,10},{7,11},{8,12},{9,13},{1... | collective-permute-start | bytes 196616 | tf_op jit(solution)/shard_map/ppermute | solution.py:243
  131.4 5.6 %collective-permute-start.27 = (f32[4,2,16,512]{3,2,1,0:T(8,128)S(1)}, f32[4,2,16,512]{3,2,1,0:T(8,128)S(1)}, u32[]{:S(2)}, u32[]{:S(2)}) collective-permute-start(f32[4,2,16,512]{3,2,1,0:T(8,128)S(1)} %shard_map.96.refs_1_), channel_id=1, source_target_pairs={{0,96},{16,112},{32,0},{48,16},{64,32},{80,48},{96,64},{112,80},{1... | collective-permute-start | bytes 786440 | tf_op jit(solution)/shard_map/ppermute | solution.py:237
  131.5 6.9 %collective-permute-start.26 = (f32[4,2,16,512]{3,2,1,0:T(8,128)S(1)}, f32[4,2,16,512]{3,2,1,0:T(8,128)S(1)}, u32[]{:S(2)}, u32[]{:S(2)}) collective-permute-start(f32[4,2,16,512]{3,2,1,0:T(8,128)S(1)} %shard_map.96.refs_1_), channel_id=1, source_target_pairs={{0,64},{16,80},{32,96},{48,112},{64,0},{80,16},{96,32},{112,48},{1... | collective-permute-start | bytes 786440 | tf_op jit(solution)/shard_map/ppermute | solution.py:237
  134.1 11.3 %collective-permute-start.25 = (f32[4,2,16,512]{3,2,1,0:T(8,128)S(1)}, f32[4,2,16,512]{3,2,1,0:T(8,128)S(1)}, u32[]{:S(2)}, u32[]{:S(2)}) collective-permute-start(f32[4,2,16,512]{3,2,1,0:T(8,128)S(1)} %shard_map.96.refs_1_), channel_id=1, source_target_pairs={{0,32},{16,48},{32,64},{48,80},{64,96},{80,112},{96,0},{112,16},{1... | collective-permute-start | bytes 786440 | tf_op jit(solution)/shard_map/ppermute | solution.py:237
  (22 other events, 126.5 us)

commit v3 on v2

--- a/solution.py
+++ b/solution.py
@@ -10,9 +10,10 @@
 from jax.sharding import PartitionSpec as P
 
 F = 512
-BOUNDS = (0, 192, 352, 512)
+BOUNDS = (0, 256, 512)
 SPANS = tuple(zip(BOUNDS[:-1], BOUNDS[1:]))
 CHUNKS = len(SPANS)
+OUT_SPANS = ((0, 256), (256, 512))
 Y = X = Z = 4
 HALF = F // 2
 QUARTER, BLOCK = HALF // Z, HALF // Z // Y
@@ -34,7 +35,7 @@
     )
 
 
-def call(kernel, out_shapes, args, after=(), scratch=(), limit=8, space=VMEM, us=0):
+def call(kernel, out_shapes, args, after=(), scratch=(), limit=8, keep=pltpu.VMEM):
     used = len(args)
 
     def run(*refs):
@@ -42,13 +43,11 @@
 
     return pl.pallas_call(
         run,
-        out_shape=[jax.ShapeDtypeStruct(s, d) for s, d in out_shapes],
-        in_specs=[SMEM] + [space] * (used - 1) + [ANY] * len(after),
+        out_shape=[keep(s, d) for s, d in out_shapes],
+        in_specs=[SMEM] + [VMEM] * (used - 1) + [ANY] * len(after),
         out_specs=[VMEM] * len(out_shapes),
         scratch_shapes=list(scratch),
-        cost_estimate=pl.CostEstimate(
-            flops=1, bytes_accessed=1 + us * 3_500_000, transcendentals=0
-        ),
+        cost_estimate=pl.CostEstimate(flops=1, bytes_accessed=1, transcendentals=0),
         compiler_params=pltpu.CompilerParams(vmem_limit_bytes=limit * 2**20),
     )(*args, *after)
 
@@ -105,7 +104,7 @@
     out[...] = total
 
 
-def cut_kernel(s, obj, *refs):
+def cut_kernel(obj, *refs):
     copies = [
         pltpu.make_async_copy(obj.at[:, first:last], refs[i], refs[CHUNKS].at[i])
         for i, (first, last) in enumerate(SPANS)
@@ -116,25 +115,36 @@
         copy.wait()
 
 
+def cut(obj):
+    return pl.pallas_call(
+        cut_kernel,
+        out_shape=[pltpu.VMEM((2, last - first, F), F32) for first, last in SPANS],
+        in_specs=[ANY],
+        out_specs=[VMEM] * CHUNKS,
+        scratch_shapes=[pltpu.SemaphoreType.DMA((CHUNKS,))],
+        cost_estimate=pl.CostEstimate(flops=1, bytes_accessed=1, transcendentals=0),
+    )(pltpu.with_memory_space_constraint(obj, pltpu.HBM))
+
+
 def column_mask(shape, col_at, odd, own):
     col = iota(shape, 1)
     return jnp.logical_xor(col >= col_at, odd if own else jnp.logical_not(odd))
 
 
-def lend_kernel(span, s, obj, below, out):
+def lend_kernel(span, s, tile, below, out):
     first, last = span
     row = iota((last - first, F), 0) + first
     for k in range(2):
-        out[k] = jnp.where(row >= s[ROW_T], obj[k, first:last], below[k])
-
-
-def half_kernel(span, s, obj, below, beside, turned, table, patch, half):
+        out[k] = jnp.where(row >= s[ROW_T], tile[k], below[k])
+
+
+def half_kernel(span, s, tile, below, beside, turned, table, patch, half):
     first, last = span
     shape = (last - first, F)
     row = iota(shape, 0) + first
     here = column_mask(shape, s[COL], s[CORE] == 1, True)
     m = [
-        jnp.where(here, jnp.where(row >= s[ROW], obj[k, first:last], below[k]), beside[k])
+        jnp.where(here, jnp.where(row >= s[ROW], tile[k], below[k]), beside[k])
         for k in range(2)
     ]
     for k in range(2):
@@ -155,9 +165,9 @@
 
 
 def fourier_kernel(s, *refs):
-    halves, patches = refs[:CHUNKS], refs[CHUNKS : 2 * CHUNKS]
-    col_table, row_table, row_table_t, amps, amps_moved = refs[2 * CHUNKS : 2 * CHUNKS + 5]
-    err, keep, send, stack, change, back, numer = refs[2 * CHUNKS + 5 :]
+    halves, patches = (refs[i * CHUNKS : (i + 1) * CHUNKS] for i in range(2))
+    col_table, row_table, row_table_t, amps, amps_moved, turned = refs[2 * CHUNKS : 2 * CHUNKS + 6]
+    grads, (keep, send, stack, change, back, numer) = refs[2 * CHUNKS + 6 :][:2], refs[2 * CHUNKS + 8 :]
     r, c, odd = s[ROW], s[COL], s[CORE] == 1
     for i, (first, last) in enumerate(SPANS):
         for k in range(2):
@@ -183,8 +193,10 @@
         rows = jnp.concatenate([back[0, at], back[1, at]], axis=0)
         by_re, by_im = dot_t(rows, col_table[0]), dot_t(rows, col_table[1])
         re, im = by_re[:tall] + by_im[tall:], by_re[tall:] - by_im[:tall]
-        err[0, at] = re
-        err[1, at] = im
+        p_re, p_im = turned[0, at], turned[1, at]
+        grad, rows = next((g, slice(j - a, j - a + tall)) for g, (a, b) in zip(grads, OUT_SPANS) if j < b)
+        grad[0, rows] = p_re * re + p_im * im
+        grad[1, rows] = p_re * im - p_im * re
         for i, (first, last) in enumerate(SPANS):
             low, high = max(first, j), min(last, j + tall)
             if low < high:
@@ -198,38 +210,41 @@
         send[k] = turned_back[HALF:]
 
 
-def grad_kernel(s, turned, err, grad):
-    grad[0] = turned[0] * err[0] + turned[1] * err[1]
-    grad[1] = turned[0] * err[1] - turned[1] * err[0]
-
-
-def fallen_masks(s, below):
-    row = iota((F, F), 0)
+def fallen_masks(span, s, below):
+    shape = (span[1] - span[0], F)
+    row = iota(shape, 0) + span[0]
     odd = s[CORE] == 1
     rows = [row < s[at] if below else row >= s[at] for at in (ROW, ROW_T)]
-    here = jnp.logical_and(column_mask((F, F), s[COL], odd, True), rows[0])
-    there = jnp.logical_and(column_mask((F, F), s[COL_T], odd, False), rows[1])
+    here = jnp.logical_and(column_mask(shape, s[COL], odd, True), rows[0])
+    there = jnp.logical_and(column_mask(shape, s[COL_T], odd, False), rows[1])
     return here, there
 
 
-def down_kernel(s, grad, moved, down):
-    here, there = fallen_masks(s, True)
+def down_kernel(span, s, grad, moved, down):
+    here, there = fallen_masks(span, s, True)
     for k in range(2):
         down[k] = jnp.where(here, grad[k], 0.0) + jnp.where(there, moved[k], 0.0)
 
 
-def stay_kernel(s, obj, light, grad, moved, base, scale):
-    here, there = fallen_masks(s, False)
-    part = 1.0 / (light[...] + 1.0)
-    scale[...] = part
-    for k in range(2):
-        stay = jnp.where(here, grad[k], 0.0) + jnp.where(there, moved[k], 0.0)
-        base[k] = obj[k] + stay * part
-
-
-def object_kernel(s, base, scale, fallen, out):
-    for k in range(2):
-        out[k] = base[k] + fallen[k] * scale[...]
+def stay_kernel(s, obj, light, *refs):
+    grads, moved, (base, scale) = refs[:2], refs[2:4], refs[4:]
+    for i, span in enumerate(OUT_SPANS):
+        at = slice(*span)
+        here, there = fallen_masks(span, s, False)
+        part = 1.0 / (light[at] + 1.0)
+        scale[at] = part
+        for k in range(2):
+            stay = jnp.where(here, grads[i][k], 0.0) + jnp.where(there, moved[i][k], 0.0)
+            base[k, at] = obj[k, at] + stay * part
+
+
+def object_kernel(s, base, scale, *refs):
+    fallen, (out, ready) = refs[:2], refs[2:]
+    ready[...] = jnp.zeros(ready.shape, F32)
+    for i, span in enumerate(OUT_SPANS):
+        at = slice(*span)
+        for k in range(2):
+            out[k, at] = base[k, at] + fallen[i][k] * scale[at]
 
 
 def turn(value, along, steps):
@@ -251,17 +266,19 @@
     return pl.ds(pl.multiple_of(jnp.bitwise_and(at + j, 3) * size, size), size)
 
 
-def share_kernel(s, numer, numer_got, light, light_got, *outs):
+def share_kernel(s, keep, got, *outs):
     for j, out in enumerate(outs):
         rows = block_rows(s[AT_Z], j, QUARTER)
-        out[:2] = numer[:, rows, :] + numer_got[:, rows, :]
-        out[2:] = light[:, rows, :] + light_got[:, rows, :]
-
-
-def sum_kernel(s, a, b, c, d, *outs):
+        out[...] = keep[:, rows, :] + got[:, rows, :]
+
+
+def sum_kernel(s, *refs):
+    numer, light, outs = refs[:4], refs[4:8], refs[8:]
     for j, out in enumerate(outs):
         rows = block_rows(s[AT_Y], j, BLOCK)
-        out[...] = a[:, rows, :] + b[:, rows, :] + c[:, rows, :] + d[:, rows, :]
+        for first, parts in ((0, numer), (2, light)):
+            a, b, c, d = [ref[:, rows, :] for ref in parts]
+            out[first : first + a.shape[0]] = a + b + c + d
 
 
 def add_kernel(s, a, b, c, d, out):
@@ -327,13 +344,7 @@
 
     shapes = [((2, last - first, F), F32) for first, last in SPANS]
 
-    tiles = call(
-        cut_kernel,
-        shapes,
-        (own, object_field),
-        scratch=[pltpu.SemaphoreType.DMA((CHUNKS,))],
-        space=ANY,
-    )
+    tiles = cut(object_field)
     below = [shifted(tile, -1) for tile in tiles]
     amps_moved = toward(amplitudes, odd_only=True)
     lent, beside = [], []
@@ -343,14 +354,22 @@
             call(
                 functools.partial(lend_kernel, SPANS[i]),
                 [shapes[i]],
-                (s, object_field, below[i]),
+                (s, tiles[i], below[i]),
                 after=after,
+                keep=jax.ShapeDtypeStruct,
             )
         )
         beside.append(toward(lent[i]))
 
     lend(0, (amps_moved,))
-    lend(1, (lent[0],))
+    seen, seen_send = call(
+        probe_light_kernel,
+        [((1, HALF, F), F32)] * 2,
+        (touch, object_field),
+        after=(lent[0],),
+        limit=16,
+    )
+    lend(1, (seen,))
     wr, wi = dft_tables()
     square = ((2, F, F), BF16)
     col_table, row_table, row_table_t, turned, probe_block = call(
@@ -359,35 +378,31 @@
         (s, wr, wi, probe),
         after=(lent[1],),
         limit=16,
-    )
-    lend(2, (turned,))
-    seen, seen_send = call(
-        probe_light_kernel,
-        [((1, HALF, F), F32)] * 2,
-        (touch, object_field),
-        after=(lent[2],),
-        limit=16,
-        us=5,
-    )
+        keep=jax.ShapeDtypeStruct,
+    )
+    seen = call(
+        share_kernel, [((1, QUARTER, F), F32)] * 4, (s, seen, swap(seen_send)), after=(turned,)
+    )
+    seen = exchange(seen, "z")
 
     patches, halves = [], []
     for i, span in enumerate(SPANS):
         patch, half = call(
             functools.partial(half_kernel, span),
             [shapes[i], (shapes[i][0], BF16)],
-            (s, object_field, below[i], beside[i], turned, col_table),
-            after=(lent[-1],),
+            (s, tiles[i], below[i], beside[i], turned, col_table),
+            after=(seen[0],) if i == 0 else (patches[-1], *seen),
             limit=16,
-            us=0 if i == CHUNKS - 1 else 2,
+            keep=jax.ShapeDtypeStruct,
         )
         patches.append(patch)
         halves.append(half)
 
-    err, keep, send = call(
+    half_tile = ((2, HALF, F), F32)
+    *grads, keep, send = call(
         fourier_kernel,
-        [((2, F, F), F32)] + [((2, HALF, F), F32)] * 2,
-        (s, *halves, *patches, col_table, row_table, row_table_t, amplitudes, amps_moved),
-        after=(seen,),
+        [half_tile] * 2 + [((2, HALF, F), F32)] * 2,
+        (s, *halves, *patches, col_table, row_table, row_table_t, amplitudes, amps_moved, turned),
         limit=24,
         scratch=[
             pltpu.VMEM((F, 2 * F), BF16),
@@ -397,25 +412,32 @@
         ],
     )
 
-    (grad,) = call(grad_kernel, [((2, F, F), F32)], (s, turned, err), us=3)
-    moved = homeward(grad)
-    (light,) = call(light_kernel, [((F, F), F32)], (touch, probe), after=(keep,), limit=16)
-    quarter, block = ((3, QUARTER, F), F32), ((3, BLOCK, F), F32)
-    parts = call(share_kernel, [quarter] * 4, (s, keep, swap(send), seen, swap(seen_send)))
-    parts = call(sum_kernel, [block] * 4, (s, *exchange(parts, "z")), after=(light,))
-    (down,) = call(down_kernel, [((2, F, F), F32)], (s, grad, moved), after=(parts[0],))
-    fallen = shifted(down, 1)
-    (share,) = call(add_kernel, [block], (s, *exchange(parts, "y")), after=(down,))
+    quarter, block = ((2, QUARTER, F), F32), ((3, BLOCK, F), F32)
+    parts = call(share_kernel, [quarter] * 4, (s, keep, swap(send)))
+    moved = [homeward(grad) for grad in grads]
+    (light,) = call(light_kernel, [((F, F), F32)], (touch, probe), after=(parts[0],), limit=16)
+    (down,) = call(
+        functools.partial(down_kernel, OUT_SPANS[0]), [half_tile], (s, grads[0], moved[0]), after=(light,)
+    )
+    fallen = [shifted(down, 1)]
+    parts = call(sum_kernel, [block] * 4, (s, *exchange(parts, "z"), *seen), after=(down,))
+    parts = exchange(parts, "y")
+    (down,) = call(
+        functools.partial(down_kernel, OUT_SPANS[1]), [half_tile], (s, grads[1], moved[1]), after=parts
+    )
+    fallen.append(shifted(down, 1))
+    (share,) = call(add_kernel, [block], (s, *parts))
     beta = 0.5 * math.sqrt(2 * X * Y * Z)
     (fresh,) = call(
         functools.partial(update_kernel, beta),
         [((2, BLOCK, F), F32)],
         (s, *exchange([share] * 4, "x"), probe_block),
+        after=(down,),
     )
     base, scale = call(
         stay_kernel,
         [((2, F, F), F32), ((F, F), F32)],
-        (s, object_field, light, grad, moved),
+        (s, object_field, light, *grads, *moved),
         after=(share,),
     )
     (fresh,) = call(
@@ -424,14 +446,16 @@
         (s, *exchange([fresh] * 4, "y")),
         after=(base,),
     )
-    (new_object,) = call(object_kernel, [((2, F, F), F32)], (s, base, scale, fallen))
+    new_object, ready = call(
+        object_kernel, [((2, F, F), F32), ((8, 128), F32)], (s, base, scale, *fallen), keep=pltpu.HBM
+    )
     (fresh,) = call(
         functools.partial(join_kernel, AT_Z),
         [((4,) + fresh.shape, F32)],
         (s, *exchange([fresh] * 4, "z")),
-        after=(new_object,),
-    )
-    (new_probe,) = call(pair_kernel, [((2, F, F), F32)], (s, fresh, swap(fresh)))
+        after=(ready,),
+    )
+    (new_probe,) = call(pair_kernel, [((2, F, F), F32)], (s, fresh, swap(fresh)), keep=pltpu.HBM)
     return (new_object, new_probe)
 
 

time: 155 us -> 147 us (0.948)
  waiting for transfers between devices: 49.8 us -> 44.1 us
  starting transfers between devices: 53.1 us -> 56.7 us
  local copies, waits for them, and re-layouts: 3.72 us -> 0.89 us
  Pallas kernels: 45.5 us -> 43.2 us
    ppermute x6 -> x9, starting transfers between devices: 9.41 us -> 14.4 us  [turn(): lax.ppermute(value, 'obj', [(o, (o + 2 * steps) % (2 * Z)) for o in range...]
    ppermute x1, waiting for transfers between devices: 4.58 us -> 8.5 us  [body(): left = lax.ppermute(own, 'pos', [(p, (p + 1) % n) for p in range(n)])]
    ppermute x1 -> x2, starting transfers between devices: 4.01 us -> 7.92 us  [homeward(): return lax.ppermute(value, ('obj', 'pos'), [(b, a) for a, b in x_pairs()])]
    ppermute x6 -> x9, waiting for transfers between devices: 20 us -> 16.2 us  [turn(): lax.ppermute(value, 'obj', [(o, (o + 2 * steps) % (2 * Z)) for o in range...]
    ppermute x4 -> x3, starting transfers between devices: 13.3 us -> 9.98 us  [toward(): return lax.ppermute(value, ('obj', 'pos'), x_pairs(odd_only))]
    ppermute x3, waiting for transfers between devices: 5.19 us -> 2.29 us  [swap(): return lax.ppermute(value, 'obj', [(o, o ^ 1) for o in range(2 * Z)])]
    unnamed x34 -> x14, local copies, waits for them, and re-layouts: 3.55 us -> 0.72 us
    ppermute x5, waiting for transfers between devices: 4.14 us -> 1.59 us  [shifted(): lax.ppermute(value, 'obj', [(o, o + steps) for o in range(n) if 0 <= o +...]
  transfers between devices with their start and end apart: 29 -> 32, of which waited for: 19 -> 16; matrix products, arithmetic and copies ran while one was open for 1% -> 0% of each run, Pallas kernels for 21% -> 21%
where the time goes in v3:
time: 147 us; the launch traced here: 146 us
  starting transfers between devices  56.7 us (39%)
  waiting for transfers between devices  44.1 us (30%)
  Pallas kernels  43.2 us (29%)
    pallas_call x20, Pallas kernels, call(): pl.pallas_call(run, out_shape=[keep(s, d) for s, d in out_shapes], in_spe...  40.7 us
    ppermute x9, waiting for transfers between devices, turn(): lax.ppermute(value, 'obj', [(o, (o + 2 * steps) % (2 * Z)) for o in range...  16.2 us
    ppermute x9, starting transfers between devices, turn(): lax.ppermute(value, 'obj', [(o, (o + 2 * steps) % (2 * Z)) for o in range...  14.4 us
    ppermute x9, waiting for transfers between devices, turn(): return lax.ppermute(value, 'pos', pairs)  14.1 us
    ppermute x5, starting transfers between devices, shifted(): lax.ppermute(value, 'obj', [(o, o + steps) for o in range(n) if 0 <= o +...  13.3 us
    ppermute x3, starting transfers between devices, toward(): return lax.ppermute(value, ('obj', 'pos'), x_pairs(odd_only))  9.98 us
    ppermute x1, waiting for transfers between devices, body(): left = lax.ppermute(own, 'pos', [(p, (p + 1) % n) for p in range(n)])  8.5 us
    ppermute x9, starting transfers between devices, turn(): return lax.ppermute(value, 'pos', pairs)  8.48 us
  transfers between devices with their start and end apart: 32, of which 16 were waited for; matrix products, arithmetic and copies ran while one was open for 0% of the time, Pallas kernels for 21%

profile of v3, /device:TPU:1, one launch (start us, length us, event | category | flops | bytes accessed | tf_op | source)
XLA Modules:
  0.0 146.1 jit_solution(16941573943720469593)
XLA Ops:
  0.6 4.0 %collective-permute-start.3 = (f32[1,512,512]{2,1,0:T(8,128)}, f32[1,512,512]{2,1,0:T(8,128)}, u32[]{:S(2)}, u32[]{:S(2)}) collective-permute-start(f32[1,512,512]{2,1,0:T(8,128)} %refs_8_.1), channel_id=1, source_target_pairs={{16,17},{17,18},{18,19},{19,20},{20,21},{21,22},{22,23},{23,24},{2... | collective-permute-start | bytes 3145736 | tf_op jit(solution)/shard_map/ppermute | solution.py:324
  4.6 2.5 %shard_map.77 = (f32[2,256,512]{2,1,0:T(8,128)S(1)}, f32[2,256,512]{2,1,0:T(8,128)}) custom-call(f32[2,512,512]{2,1,0:T(8,128)} %refs_1_.5), custom_call_target="tpu_custom_call" | custom-call | flops 1 | bytes 1 | tf_op jit(solution)/shard_map/pallas_call | solution.py:119
  12.3 8.5 %collective-permute-done = s32[2]{0:T(128)S(1)} collective-permute-done((s32[2]{0:T(128)S(1)}, s32[2]{0:T(128)S(1)}, u32[]{:S(2)}, u32[]{:S(2)}) %collective-permute-start) | collective-permute-done | bytes 40 | tf_op jit(solution)/shard_map/ppermute | solution.py:338
  23.4 2.5 %shard_map.78.refs_2_ = f32[2,256,512]{2,1,0:T(8,128)} custom-call(s32[7]{0:T(128)S(1)} %concatenate.10.refs_0_, f32[2,256,512]{2,1,0:T(8,128)S(1)} %get-tuple-element.35.refs_1_, f32[2,256,512]{2,1,0:T(8,128)} %collective-permute-done.2.refs_2_, f32[1,512,512]{2,1,0:T(8,128)} %collective-permute-done.3.refs_3_.refs_9_), custom_call_target="tpu_custom_call" | custom-call | flops 1 | bytes 1 | tf_op jit(solution)/shard_map/pallas_call | solution.py:44
  25.9 2.9 %collective-permute-start.4 = (f32[2,256,512]{2,1,0:T(8,128)}, f32[2,256,512]{2,1,0:T(8,128)}, u32[]{:S(2)}, u32[]{:S(2)}) collective-permute-start(f32[2,256,512]{2,1,0:T(8,128)} %shard_map.78.refs_2_), channel_id=1, source_target_pairs={{16,17},{17,18},{18,19},{19,20},{20,21},{21,22},{22,23},{23,24},{2... | collective-permute-start | bytes 3145736 | tf_op jit(solution)/shard_map/ppermute | solution.py:324
  28.9 4.8 %shard_map.79 = (f32[1,256,512]{2,1,0:T(8,128)S(1)}, f32[1,256,512]{2,1,0:T(8,128)S(1)}) custom-call(s32[15]{0:T(128)S(1)} %concatenate.12.refs_0_, f32[2,512,512]{2,1,0:T(8,128)S(1)} %copy-done, f32[2,256,512]{2,1,0:T(8,128)} %shard_map.78.refs_2_), custom_call_target="tpu_custom_call" | custom-call | flops 1 | bytes 1 | tf_op jit(solution)/shard_map/pallas_call | solution.py:44
  36.6 3.1 %collective-permute-start.7 = (f32[2,256,512]{2,1,0:T(8,128)S(1)}, f32[2,256,512]{2,1,0:T(8,128)S(1)}, u32[]{:S(2)}, u32[]{:S(2)}) collective-permute-start(f32[2,256,512]{2,1,0:T(8,128)S(1)} %shard_map.80.refs_4_), channel_id=1, source_target_pairs={{16,17},{17,18},{18,19},{19,20},{20,21},{21,22},{22,23},{23,24},{2... | collective-permute-start | bytes 3145736 | tf_op jit(solution)/shard_map/ppermute | solution.py:324
  39.8 4.5 %shard_map.81 = (bf16[2,512,512]{2,1,0:T(8,128)(2,1)S(1)}, bf16[2,512,512]{2,1,0:T(8,128)(2,1)S(1)}, bf16[2,512,512]{2,1,0:T(8,128)(2,1)S(1)}, f32[2,512,512]{2,1,0:T(8,128)S(1)}, f32[2,16,512]{2,1,0:T(8,128)S(1)}) custom-call(s32[7]{0:T(128)S(1)} %concatenate.10.refs_0_, bf16[512,512]{1,0:T(8,128)(2,1)S(1)} %copy-done.4, bf16[512,512]{1,0:T(8,128)(2,1)S(1)} %copy-done.3, ...), custom_call_target="tpu_custom_call" | custom-call | flops 1 | bytes 1 | tf_op jit(solution)/shard_map/pallas_call | solution.py:44
  50.7 2.5 %shard_map.83 = (f32[2,256,512]{2,1,0:T(8,128)S(1)}, bf16[2,256,512]{2,1,0:T(8,128)(2,1)S(1)}) custom-call(s32[7]{0:T(128)S(1)} %concatenate.10.refs_0_, f32[2,256,512]{2,1,0:T(8,128)S(1)} %get-tuple-element.35.refs_1_, f32[2,256,512]{2,1,0:T(8,128)} %collective-permute-done.2.refs_2_, f32[2,256,512]{2,1,0:T(8,128)} %collective-permute-done.4.refs_3_, ...), custom_call_target="tpu_custom_call" | custom-call | flops 1 | bytes 1 | tf_op jit(solution)/shard_map/pallas_call | solution.py:44
  56.2 2.6 %shard_map.84 = (f32[2,256,512]{2,1,0:T(8,128)S(1)}, bf16[2,256,512]{2,1,0:T(8,128)(2,1)S(1)}) custom-call(s32[7]{0:T(128)S(1)} %concatenate.10.refs_0_, f32[2,256,512]{2,1,0:T(8,128)} %get-tuple-element.36.refs_1_, f32[2,256,512]{2,1,0:T(8,128)} %collective-permute-done.5.refs_2_, f32[2,256,512]{2,1,0:T(8,128)S(1)} %collective-permute-done.7.refs_3_, ...), custom_call_target="tpu_custom_call" | custom-call | flops 1 | bytes 1 | tf_op jit(solution)/shard_map/pallas_call | solution.py:44
  58.8 6.9 %shard_map.85 = (f32[2,256,512]{2,1,0:T(8,128)S(1)}, f32[2,256,512]{2,1,0:T(8,128)S(1)}, f32[2,256,512]{2,1,0:T(8,128)S(1)}, f32[2,256,512]{2,1,0:T(8,128)S(1)}) custom-call(s32[7]{0:T(128)S(1)} %concatenate.10.refs_0_, bf16[2,256,512]{2,1,0:T(8,128)(2,1)S(1)} %get-tuple-element.42.refs_1_, bf16[2,256,512]{2,1,0:T(8,128)(2,1)S(1)} %get-tuple-element.47.refs_2_, ...), custom_call_target="tpu_custom_call" | custom-call | flops 1 | bytes 1 | tf_op jit(solution)/shard_map/pallas_call | solution.py:44
  65.8 5.5 %collective-permute-start.12 = (f32[2,256,512]{2,1,0:T(8,128)S(1)}, f32[2,256,512]{2,1,0:T(8,128)S(1)}, u32[]{:S(2)}, u32[]{:S(2)}) collective-permute-start(f32[2,256,512]{2,1,0:T(8,128)S(1)} %get-tuple-element.54.refs_1_.refs_3_), channel_id=1, source_target_pairs={{17,16},{18,17},{19,18},{20,19},{21,20},{22,21},{23,22},{24,23},{2... | collective-permute-start | bytes 3145736 | tf_op jit(solution)/shard_map/ppermute | solution.py:328
  71.3 2.4 %collective-permute-start.13 = (f32[2,256,512]{2,1,0:T(8,128)S(1)}, f32[2,256,512]{2,1,0:T(8,128)S(1)}, u32[]{:S(2)}, u32[]{:S(2)}) collective-permute-start(f32[2,256,512]{2,1,0:T(8,128)S(1)} %get-tuple-element.55.refs_4_.refs_1_), channel_id=1, source_target_pairs={{17,16},{18,17},{19,18},{20,19},{21,20},{22,21},{23,22},{24,23},{2... | collective-permute-start | bytes 3145736 | tf_op jit(solution)/shard_map/ppermute | solution.py:328
  75.4 2.3 %collective-permute-start.15 = (f32[2,64,512]{2,1,0:T(8,128)S(1)}, f32[2,64,512]{2,1,0:T(8,128)S(1)}, u32[]{:S(2)}, u32[]{:S(2)}) collective-permute-start(f32[2,64,512]{2,1,0:T(8,128)S(1)} %get-tuple-element.57), channel_id=1, source_target_pairs={{0,64},{16,80},{32,96},{48,112},{64,0},{80,16},{96,32},{112,48},{1... | collective-permute-start | bytes 786440 | tf_op jit(solution)/shard_map/ppermute | solution.py:252
  79.4 3.9 %shard_map.87.refs_3_.refs_2_ = f32[512,512]{1,0:T(8,128)S(1)} custom-call(s32[15]{0:T(128)S(1)} %concatenate.12.refs_0_, f32[2,512,512]{2,1,0:T(8,128)S(1)} %copy-done.1, f32[2,64,512]{2,1,0:T(8,128)S(1)} %get-tuple-element.53.refs_2_.refs_1_), custom_call_target="tpu_custom_call" | custom-call | flops 1 | bytes 1 | tf_op jit(solution)/shard_map/pallas_call | solution.py:44
  84.2 5.0 %collective-permute-done.15.refs_3_ = f32[2,64,512]{2,1,0:T(8,128)S(1)} collective-permute-done((f32[2,64,512]{2,1,0:T(8,128)S(1)}, f32[2,64,512]{2,1,0:T(8,128)S(1)}, u32[]{:S(2)}, u32[]{:S(2)}) %collective-permute-start.15) | collective-permute-done | bytes 262176 | tf_op jit(solution)/shard_map/ppermute | solution.py:252
  90.6 2.6 %collective-permute-start.18 = (f32[3,16,512]{2,1,0:T(8,128)S(1)}, f32[3,16,512]{2,1,0:T(8,128)S(1)}, u32[]{:S(2)}, u32[]{:S(2)}) collective-permute-start(f32[3,16,512]{2,1,0:T(8,128)S(1)} %get-tuple-element.61), channel_id=1, source_target_pairs={{0,8},{1,9},{2,10},{3,11},{4,12},{5,13},{6,14},{7,15},{8,0},{9,1},... | collective-permute-start | bytes 294920 | tf_op jit(solution)/shard_map/ppermute | solution.py:258
  94.4 4.3 %collective-permute-start.20 = (f32[2,256,512]{2,1,0:T(8,128)S(1)}, f32[2,256,512]{2,1,0:T(8,128)S(1)}, u32[]{:S(2)}, u32[]{:S(2)}) collective-permute-start(f32[2,256,512]{2,1,0:T(8,128)S(1)} %shard_map.88.refs_9_), channel_id=1, source_target_pairs={{0,16},{16,32},{32,48},{48,64},{64,80},{80,96},{96,112},{1,17},{17... | collective-permute-start | bytes 3145736 | tf_op jit(solution)/shard_map/ppermute | solution.py:312
  98.8 4.0 %collective-permute-done.18.refs_3_.refs_5_ = f32[3,16,512]{2,1,0:T(8,128)S(1)} collective-permute-done((f32[3,16,512]{2,1,0:T(8,128)S(1)}, f32[3,16,512]{2,1,0:T(8,128)S(1)}, u32[]{:S(2)}, u32[]{:S(2)}) %collective-permute-start.18) | collective-permute-done | bytes 98336 | tf_op jit(solution)/shard_map/ppermute | solution.py:258
  103.6 3.2 %collective-permute-start.21 = (f32[2,256,512]{2,1,0:T(8,128)S(1)}, f32[2,256,512]{2,1,0:T(8,128)S(1)}, u32[]{:S(2)}, u32[]{:S(2)}) collective-permute-start(f32[2,256,512]{2,1,0:T(8,128)S(1)} %shard_map.92.refs_6_), channel_id=1, source_target_pairs={{0,16},{16,32},{32,48},{48,64},{64,80},{80,96},{96,112},{1,17},{17... | collective-permute-start | bytes 3145736 | tf_op jit(solution)/shard_map/ppermute | solution.py:312
  108.9 3.3 %collective-permute-done.24.refs_4_ = f32[3,16,512]{2,1,0:T(8,128)S(1)} collective-permute-done((f32[3,16,512]{2,1,0:T(8,128)S(1)}, f32[3,16,512]{2,1,0:T(8,128)S(1)}, u32[]{:S(2)}, u32[]{:S(2)}) %collective-permute-start.24) | collective-permute-done | bytes 98336 | tf_op jit(solution)/shard_map/ppermute | solution.py:258
  113.4 2.3 %collective-permute-done.22.refs_2_ = f32[3,16,512]{2,1,0:T(8,128)S(1)} collective-permute-done((f32[3,16,512]{2,1,0:T(8,128)S(1)}, f32[3,16,512]{2,1,0:T(8,128)S(1)}, u32[]{:S(2)}, u32[]{:S(2)}) %collective-permute-start.22) | collective-permute-done | bytes 98336 | tf_op jit(solution)/shard_map/ppermute | solution.py:258
  124.0 3.6 %collective-permute-start.29 = (f32[4,2,16,512]{3,2,1,0:T(8,128)S(1)}, f32[4,2,16,512]{3,2,1,0:T(8,128)S(1)}, u32[]{:S(2)}, u32[]{:S(2)}) collective-permute-start(f32[4,2,16,512]{3,2,1,0:T(8,128)S(1)} %shard_map.95.refs_1_), channel_id=1, source_target_pairs={{0,64},{16,80},{32,96},{48,112},{64,0},{80,16},{96,32},{112,48},{1... | collective-permute-start | bytes 786440 | tf_op jit(solution)/shard_map/ppermute | solution.py:252
  132.3 7.0 %collective-permute-done.28.refs_2_ = f32[4,2,16,512]{3,2,1,0:T(8,128)S(1)} collective-permute-done((f32[4,2,16,512]{3,2,1,0:T(8,128)S(1)}, f32[4,2,16,512]{3,2,1,0:T(8,128)S(1)}, u32[]{:S(2)}, u32[]{:S(2)}) %collective-permute-start.28) | collective-permute-done | bytes 262176 | tf_op jit(solution)/shard_map/ppermute | solution.py:252
  (80 shorter events, 50.8 us)
Async XLA Ops:
  0.6 22.3 %collective-permute-start.3 = (f32[1,512,512]{2,1,0:T(8,128)}, f32[1,512,512]{2,1,0:T(8,128)}, u32[]{:S(2)}, u32[]{:S(2)}) collective-permute-start(f32[1,512,512]{2,1,0:T(8,128)} %refs_8_.1), channel_id=1, source_target_pairs={{16,17},{17,18},{18,19},{19,20},{20,21},{21,22},{22,23},{23,24},{2... | collective-permute-start | bytes 3145736 | tf_op jit(solution)/shard_map/ppermute | solution.py:324
  7.1 16.2 %collective-permute-start.2 = (f32[2,256,512]{2,1,0:T(8,128)S(1)}, f32[2,256,512]{2,1,0:T(8,128)}, u32[]{:S(2)}, u32[]{:S(2)}) collective-permute-start(f32[2,256,512]{2,1,0:T(8,128)S(1)} %get-tuple-element.35.refs_1_), channel_id=1, source_target_pairs={{16,0},{32,16},{48,32},{64,48},{80,64},{96,80},{112,96},{17,1},{33... | collective-permute-start | bytes 3145736 | tf_op jit(solution)/shard_map/ppermute | solution.py:312
  9.1 25.8 %collective-permute-start.5 = (f32[2,256,512]{2,1,0:T(8,128)}, f32[2,256,512]{2,1,0:T(8,128)}, u32[]{:S(2)}, u32[]{:S(2)}) collective-permute-start(f32[2,256,512]{2,1,0:T(8,128)} %get-tuple-element.36.refs_1_), channel_id=1, source_target_pairs={{16,0},{32,16},{48,32},{64,48},{80,64},{96,80},{112,96},{17,1},{33... | collective-permute-start | bytes 3145736 | tf_op jit(solution)/shard_map/ppermute | solution.py:312
  11.1 9.7 %collective-permute-start = (s32[2]{0:T(128)S(1)}, s32[2]{0:T(128)S(1)}, u32[]{:S(2)}, u32[]{:S(2)}) collective-permute-start(s32[2]{0:T(128)S(1)} %add_subtract_fusion), channel_id=1, source_target_pairs={{0,1},{1,2},{2,3},{3,4},{4,5},{5,6},{6,7},{7,8},{8,9},{9,10},{10,1... | collective-permute-start | bytes 32 | tf_op jit(solution)/shard_map/ppermute | solution.py:338
  20.9 7.9 %collective-permute-start.1 = (s32[4]{0:T(128)S(1)}, s32[4]{0:T(128)S(1)}, u32[]{:S(2)}, u32[]{:S(2)}) collective-permute-start(s32[4]{0:T(128)S(1)} %pad_add_fusion), channel_id=1, source_target_pairs={{0,16},{16,32},{32,48},{48,64},{64,80},{80,96},{96,112},{1,17},{17... | collective-permute-start | bytes 56 | tf_op jit(solution)/shard_map/ppermute | solution.py:312
  25.9 24.8 %collective-permute-start.4 = (f32[2,256,512]{2,1,0:T(8,128)}, f32[2,256,512]{2,1,0:T(8,128)}, u32[]{:S(2)}, u32[]{:S(2)}) collective-permute-start(f32[2,256,512]{2,1,0:T(8,128)} %shard_map.78.refs_2_), channel_id=1, source_target_pairs={{16,17},{17,18},{18,19},{19,20},{20,21},{21,22},{22,23},{23,24},{2... | collective-permute-start | bytes 3145736 | tf_op jit(solution)/shard_map/ppermute | solution.py:324
  36.6 19.6 %collective-permute-start.7 = (f32[2,256,512]{2,1,0:T(8,128)S(1)}, f32[2,256,512]{2,1,0:T(8,128)S(1)}, u32[]{:S(2)}, u32[]{:S(2)}) collective-permute-start(f32[2,256,512]{2,1,0:T(8,128)S(1)} %shard_map.80.refs_4_), channel_id=1, source_target_pairs={{16,17},{17,18},{18,19},{19,20},{20,21},{21,22},{22,23},{23,24},{2... | collective-permute-start | bytes 3145736 | tf_op jit(solution)/shard_map/ppermute | solution.py:324
  44.9 8.3 %collective-permute-start.8 = (f32[1,64,512]{2,1,0:T(8,128)S(1)}, f32[1,64,512]{2,1,0:T(8,128)S(1)}, u32[]{:S(2)}, u32[]{:S(2)}) collective-permute-start(f32[1,64,512]{2,1,0:T(8,128)S(1)} %get-tuple-element.44), channel_id=1, source_target_pairs={{0,32},{16,48},{32,64},{48,80},{64,96},{80,112},{96,0},{112,16},{1... | collective-permute-start | bytes 393224 | tf_op jit(solution)/shard_map/ppermute | solution.py:252
  46.6 8.2 %collective-permute-start.9 = (f32[1,64,512]{2,1,0:T(8,128)S(1)}, f32[1,64,512]{2,1,0:T(8,128)S(1)}, u32[]{:S(2)}, u32[]{:S(2)}) collective-permute-start(f32[1,64,512]{2,1,0:T(8,128)S(1)} %get-tuple-element.45), channel_id=1, source_target_pairs={{0,64},{16,80},{32,96},{48,112},{64,0},{80,16},{96,32},{112,48},{1... | collective-permute-start | bytes 393224 | tf_op jit(solution)/shard_map/ppermute | solution.py:252
  65.7 8.0 %collective-permute-start.11 = (f32[2,256,512]{2,1,0:T(8,128)S(1)}, f32[2,256,512]{2,1,0:T(8,128)S(1)}, u32[]{:S(2)}, u32[]{:S(2)}) collective-permute-start(f32[2,256,512]{2,1,0:T(8,128)S(1)} %get-tuple-element.52), channel_id=1, source_target_pairs={{0,16},{16,0},{32,48},{48,32},{64,80},{80,64},{96,112},{112,96},{1... | collective-permute-start | bytes 3145736 | tf_op jit(solution)/shard_map/ppermute | solution.py:307
  65.8 17.5 %collective-permute-start.12 = (f32[2,256,512]{2,1,0:T(8,128)S(1)}, f32[2,256,512]{2,1,0:T(8,128)S(1)}, u32[]{:S(2)}, u32[]{:S(2)}) collective-permute-start(f32[2,256,512]{2,1,0:T(8,128)S(1)} %get-tuple-element.54.refs_1_.refs_3_), channel_id=1, source_target_pairs={{17,16},{18,17},{19,18},{20,19},{21,20},{22,21},{23,22},{24,23},{2... | collective-permute-start | bytes 3145736 | tf_op jit(solution)/shard_map/ppermute | solution.py:328
  71.3 27.5 %collective-permute-start.13 = (f32[2,256,512]{2,1,0:T(8,128)S(1)}, f32[2,256,512]{2,1,0:T(8,128)S(1)}, u32[]{:S(2)}, u32[]{:S(2)}) collective-permute-start(f32[2,256,512]{2,1,0:T(8,128)S(1)} %get-tuple-element.55.refs_4_.refs_1_), channel_id=1, source_target_pairs={{17,16},{18,17},{19,18},{20,19},{21,20},{22,21},{23,22},{24,23},{2... | collective-permute-start | bytes 3145736 | tf_op jit(solution)/shard_map/ppermute | solution.py:328
  74.4 9.8 %collective-permute-start.14 = (f32[2,64,512]{2,1,0:T(8,128)S(1)}, f32[2,64,512]{2,1,0:T(8,128)S(1)}, u32[]{:S(2)}, u32[]{:S(2)}) collective-permute-start(f32[2,64,512]{2,1,0:T(8,128)S(1)} %get-tuple-element.56), channel_id=1, source_target_pairs={{0,32},{16,48},{32,64},{48,80},{64,96},{80,112},{96,0},{112,16},{1... | collective-permute-start | bytes 786440 | tf_op jit(solution)/shard_map/ppermute | solution.py:252
  75.4 13.7 %collective-permute-start.15 = (f32[2,64,512]{2,1,0:T(8,128)S(1)}, f32[2,64,512]{2,1,0:T(8,128)S(1)}, u32[]{:S(2)}, u32[]{:S(2)}) collective-permute-start(f32[2,64,512]{2,1,0:T(8,128)S(1)} %get-tuple-element.57), channel_id=1, source_target_pairs={{0,64},{16,80},{32,96},{48,112},{64,0},{80,16},{96,32},{112,48},{1... | collective-permute-start | bytes 786440 | tf_op jit(solution)/shard_map/ppermute | solution.py:252
  77.7 11.4 %collective-permute-start.16 = (f32[2,64,512]{2,1,0:T(8,128)S(1)}, f32[2,64,512]{2,1,0:T(8,128)S(1)}, u32[]{:S(2)}, u32[]{:S(2)}) collective-permute-start(f32[2,64,512]{2,1,0:T(8,128)S(1)} %get-tuple-element.58), channel_id=1, source_target_pairs={{0,96},{16,112},{32,0},{48,16},{64,32},{80,48},{96,64},{112,80},{1... | collective-permute-start | bytes 786440 | tf_op jit(solution)/shard_map/ppermute | solution.py:252
  89.7 9.1 %collective-permute-start.17 = (f32[3,16,512]{2,1,0:T(8,128)S(1)}, f32[3,16,512]{2,1,0:T(8,128)S(1)}, u32[]{:S(2)}, u32[]{:S(2)}) collective-permute-start(f32[3,16,512]{2,1,0:T(8,128)S(1)} %get-tuple-element.60), channel_id=1, source_target_pairs={{0,4},{1,5},{2,6},{3,7},{4,8},{5,9},{6,10},{7,11},{8,12},{9,13},{1... | collective-permute-start | bytes 294920 | tf_op jit(solution)/shard_map/ppermute | solution.py:258
  90.6 12.2 %collective-permute-start.18 = (f32[3,16,512]{2,1,0:T(8,128)S(1)}, f32[3,16,512]{2,1,0:T(8,128)S(1)}, u32[]{:S(2)}, u32[]{:S(2)}) collective-permute-start(f32[3,16,512]{2,1,0:T(8,128)S(1)} %get-tuple-element.61), channel_id=1, source_target_pairs={{0,8},{1,9},{2,10},{3,11},{4,12},{5,13},{6,14},{7,15},{8,0},{9,1},... | collective-permute-start | bytes 294920 | tf_op jit(solution)/shard_map/ppermute | solution.py:258
  93.2 9.6 %collective-permute-start.19 = (f32[3,16,512]{2,1,0:T(8,128)S(1)}, f32[3,16,512]{2,1,0:T(8,128)S(1)}, u32[]{:S(2)}, u32[]{:S(2)}) collective-permute-start(f32[3,16,512]{2,1,0:T(8,128)S(1)} %get-tuple-element.62), channel_id=1, source_target_pairs={{0,12},{1,13},{2,14},{3,15},{4,0},{5,1},{6,2},{7,3},{8,4},{9,5},{1... | collective-permute-start | bytes 294920 | tf_op jit(solution)/shard_map/ppermute | solution.py:258
  94.4 33.1 %collective-permute-start.20 = (f32[2,256,512]{2,1,0:T(8,128)S(1)}, f32[2,256,512]{2,1,0:T(8,128)S(1)}, u32[]{:S(2)}, u32[]{:S(2)}) collective-permute-start(f32[2,256,512]{2,1,0:T(8,128)S(1)} %shard_map.88.refs_9_), channel_id=1, source_target_pairs={{0,16},{16,32},{32,48},{48,64},{64,80},{80,96},{96,112},{1,17},{17... | collective-permute-start | bytes 3145736 | tf_op jit(solution)/shard_map/ppermute | solution.py:312
  103.6 24.0 %collective-permute-start.21 = (f32[2,256,512]{2,1,0:T(8,128)S(1)}, f32[2,256,512]{2,1,0:T(8,128)S(1)}, u32[]{:S(2)}, u32[]{:S(2)}) collective-permute-start(f32[2,256,512]{2,1,0:T(8,128)S(1)} %shard_map.92.refs_6_), channel_id=1, source_target_pairs={{0,16},{16,32},{32,48},{48,64},{64,80},{80,96},{96,112},{1,17},{17... | collective-permute-start | bytes 3145736 | tf_op jit(solution)/shard_map/ppermute | solution.py:312
  107.6 8.1 %collective-permute-start.22 = (f32[3,16,512]{2,1,0:T(8,128)S(1)}, f32[3,16,512]{2,1,0:T(8,128)S(1)}, u32[]{:S(2)}, u32[]{:S(2)}) collective-permute-start(f32[3,16,512]{2,1,0:T(8,128)S(1)} %shard_map.90.refs_7_.refs_1_), channel_id=1, source_target_pairs={{0,1},{1,2},{2,3},{3,0},{4,5},{5,6},{6,7},{7,4},{8,9},{9,10},{10,1... | collective-permute-start | bytes 294920 | tf_op jit(solution)/shard_map/ppermute | solution.py:258
  123.9 7.1 %collective-permute-start.30 = (f32[4,2,16,512]{3,2,1,0:T(8,128)S(1)}, f32[4,2,16,512]{3,2,1,0:T(8,128)S(1)}, u32[]{:S(2)}, u32[]{:S(2)}) collective-permute-start(f32[4,2,16,512]{3,2,1,0:T(8,128)S(1)} %shard_map.95.refs_1_), channel_id=1, source_target_pairs={{0,96},{16,112},{32,0},{48,16},{64,32},{80,48},{96,64},{112,80},{1... | collective-permute-start | bytes 786440 | tf_op jit(solution)/shard_map/ppermute | solution.py:252
  124.0 8.4 %collective-permute-start.29 = (f32[4,2,16,512]{3,2,1,0:T(8,128)S(1)}, f32[4,2,16,512]{3,2,1,0:T(8,128)S(1)}, u32[]{:S(2)}, u32[]{:S(2)}) collective-permute-start(f32[4,2,16,512]{3,2,1,0:T(8,128)S(1)} %shard_map.95.refs_1_), channel_id=1, source_target_pairs={{0,64},{16,80},{32,96},{48,112},{64,0},{80,16},{96,32},{112,48},{1... | collective-permute-start | bytes 786440 | tf_op jit(solution)/shard_map/ppermute | solution.py:252
  127.5 11.8 %collective-permute-start.28 = (f32[4,2,16,512]{3,2,1,0:T(8,128)S(1)}, f32[4,2,16,512]{3,2,1,0:T(8,128)S(1)}, u32[]{:S(2)}, u32[]{:S(2)}) collective-permute-start(f32[4,2,16,512]{3,2,1,0:T(8,128)S(1)} %shard_map.95.refs_1_), channel_id=1, source_target_pairs={{0,32},{16,48},{32,64},{48,80},{64,96},{80,112},{96,0},{112,16},{1... | collective-permute-start | bytes 786440 | tf_op jit(solution)/shard_map/ppermute | solution.py:252
  (15 other events, 76.6 us)

commit v4 on v3

--- a/solution.py
+++ b/solution.py
@@ -104,26 +104,20 @@
     out[...] = total
 
 
-def cut_kernel(obj, *refs):
-    copies = [
-        pltpu.make_async_copy(obj.at[:, first:last], refs[i], refs[CHUNKS].at[i])
-        for i, (first, last) in enumerate(SPANS)
-    ]
-    for copy in copies:
+def cut(obj, span, after=()):
+    def kernel(obj, *refs):
+        copy = pltpu.make_async_copy(obj.at[:, span[0] : span[1]], refs[-2], refs[-1])
         copy.start()
-    for copy in copies:
         copy.wait()
 
-
-def cut(obj):
     return pl.pallas_call(
-        cut_kernel,
-        out_shape=[pltpu.VMEM((2, last - first, F), F32) for first, last in SPANS],
-        in_specs=[ANY],
-        out_specs=[VMEM] * CHUNKS,
-        scratch_shapes=[pltpu.SemaphoreType.DMA((CHUNKS,))],
+        kernel,
+        out_shape=pltpu.VMEM((2, span[1] - span[0], F), F32),
+        in_specs=[ANY] * (1 + len(after)),
+        out_specs=VMEM,
+        scratch_shapes=[pltpu.SemaphoreType.DMA],
         cost_estimate=pl.CostEstimate(flops=1, bytes_accessed=1, transcendentals=0),
-    )(pltpu.with_memory_space_constraint(obj, pltpu.HBM))
+    )(pltpu.with_memory_space_constraint(obj, pltpu.HBM), *after)
 
 
 def column_mask(shape, col_at, odd, own):
@@ -344,7 +338,7 @@
 
     shapes = [((2, last - first, F), F32) for first, last in SPANS]
 
-    tiles = cut(object_field)
+    tiles = [cut(object_field, SPANS[0]), cut(object_field, SPANS[1], (left,))]
     below = [shifted(tile, -1) for tile in tiles]
     amps_moved = toward(amplitudes, odd_only=True)
     lent, beside = [], []
@@ -361,12 +355,12 @@
         )
         beside.append(toward(lent[i]))
 
-    lend(0, (amps_moved,))
+    lend(0, ())
     seen, seen_send = call(
         probe_light_kernel,
         [((1, HALF, F), F32)] * 2,
         (touch, object_field),
-        after=(lent[0],),
+        after=(lent[0], amps_moved),
         limit=16,
     )
     lend(1, (seen,))

time: 147 us -> 144 us (0.980)
  waiting for transfers between devices: 44.1 us -> 39.9 us
    ppermute x1, waiting for transfers between devices: 8.5 us -> 1.53 us  [body(): left = lax.ppermute(own, 'pos', [(p, (p + 1) % n) for p in range(n)])]
    ppermute x5, starting transfers between devices: 13.3 us -> 17.8 us  [shifted(): lax.ppermute(value, 'obj', [(o, o + steps) for o in range(n) if 0 <= o +...]
    ppermute x3, starting transfers between devices: 9.98 us -> 7.16 us  [toward(): return lax.ppermute(value, ('obj', 'pos'), x_pairs(odd_only))]
    ppermute x3, waiting for transfers between devices: 1.31 us -> 3.31 us  [toward(): return lax.ppermute(value, ('obj', 'pos'), x_pairs(odd_only))]
    ppermute x9, waiting for transfers between devices: 16.2 us -> 18 us  [turn(): lax.ppermute(value, 'obj', [(o, (o + 2 * steps) % (2 * Z)) for o in range...]
    ppermute x9, starting transfers between devices: 14.4 us -> 12.7 us  [turn(): lax.ppermute(value, 'obj', [(o, (o + 2 * steps) % (2 * Z)) for o in range...]
  transfers between devices with their start and end apart: 32 -> 32, of which waited for: 16 -> 18; matrix products, arithmetic and copies ran while one was open for 0% -> 1% of each run, Pallas kernels for 21% -> 21%
where the time goes in v4:
time: 144 us; the launch traced here: 143 us
  starting transfers between devices  55.6 us (39%)
  Pallas kernels  42.5 us (30%)
  waiting for transfers between devices  39.9 us (28%)
  local copies, waits for them, and re-layouts  2.34 us (2%)
    pallas_call x20, Pallas kernels, call(): pl.pallas_call(run, out_shape=[keep(s, d) for s, d in out_shapes], in_spe...  40.1 us
    ppermute x9, waiting for transfers between devices, turn(): lax.ppermute(value, 'obj', [(o, (o + 2 * steps) % (2 * Z)) for o in range...  18 us
    ppermute x5, starting transfers between devices, shifted(): lax.ppermute(value, 'obj', [(o, o + steps) for o in range(n) if 0 <= o +...  17.8 us
    ppermute x9, waiting for transfers between devices, turn(): return lax.ppermute(value, 'pos', pairs)  13.7 us
    ppermute x9, starting transfers between devices, turn(): lax.ppermute(value, 'obj', [(o, (o + 2 * steps) % (2 * Z)) for o in range...  12.7 us
    ppermute x9, starting transfers between devices, turn(): return lax.ppermute(value, 'pos', pairs)  8.93 us
    ppermute x3, starting transfers between devices, toward(): return lax.ppermute(value, ('obj', 'pos'), x_pairs(odd_only))  7.16 us
    ppermute x2, starting transfers between devices, homeward(): return lax.ppermute(value, ('obj', 'pos'), [(b, a) for a, b in x_pairs()])  6.59 us
  transfers between devices with their start and end apart: 32, of which 18 were waited for; matrix products, arithmetic and copies ran while one was open for 1% of the time, Pallas kernels for 21%

profile of v4, /device:TPU:1, one launch (start us, length us, event | category | flops | bytes accessed | tf_op | source)
XLA Modules:
  0.0 142.9 jit_solution(9484673291787175426)
XLA Ops:
  1.9 3.3 %collective-permute-start.2 = (f32[2,256,512]{2,1,0:T(8,128)S(1)}, f32[2,256,512]{2,1,0:T(8,128)}, u32[]{:S(2)}, u32[]{:S(2)}) collective-permute-start(f32[2,256,512]{2,1,0:T(8,128)S(1)} %shard_map.77.refs_1_), channel_id=1, source_target_pairs={{16,0},{32,16},{48,32},{64,48},{80,64},{96,80},{112,96},{17,1},{33... | collective-permute-start | bytes 3145736 | tf_op jit(solution)/shard_map/ppermute | solution.py:306
  6.6 3.1 %collective-permute-start.5 = (f32[1,512,512]{2,1,0:T(8,128)}, f32[1,512,512]{2,1,0:T(8,128)}, u32[]{:S(2)}, u32[]{:S(2)}) collective-permute-start(f32[1,512,512]{2,1,0:T(8,128)} %refs_8_.1), channel_id=1, source_target_pairs={{16,17},{17,18},{18,19},{19,20},{20,21},{21,22},{22,23},{23,24},{2... | collective-permute-start | bytes 3145736 | tf_op jit(solution)/shard_map/ppermute | solution.py:318
  14.0 2.3 %collective-permute-start.4 = (f32[2,256,512]{2,1,0:T(8,128)}, f32[2,256,512]{2,1,0:T(8,128)}, u32[]{:S(2)}, u32[]{:S(2)}) collective-permute-start(f32[2,256,512]{2,1,0:T(8,128)} %copy-done.1), channel_id=1, source_target_pairs={{16,0},{32,16},{48,32},{64,48},{80,64},{96,80},{112,96},{17,1},{33... | collective-permute-start | bytes 3145736 | tf_op jit(solution)/shard_map/ppermute | solution.py:306
  17.0 4.1 %collective-permute-start.1 = (s32[4]{0:T(128)S(1)}, s32[4]{0:T(128)S(1)}, u32[]{:S(2)}, u32[]{:S(2)}) collective-permute-start(s32[4]{0:T(128)S(1)} %pad_add_fusion), channel_id=1, source_target_pairs={{0,16},{16,32},{32,48},{48,64},{64,80},{80,96},{96,112},{1,17},{17... | collective-permute-start | bytes 56 | tf_op jit(solution)/shard_map/ppermute | solution.py:306
  21.9 2.3 %shard_map.78.refs_2_ = f32[2,256,512]{2,1,0:T(8,128)} custom-call(s32[7]{0:T(128)S(1)} %concatenate.10.refs_0_, f32[2,256,512]{2,1,0:T(8,128)S(1)} %shard_map.77.refs_1_, f32[2,256,512]{2,1,0:T(8,128)} %collective-permute-done.2.refs_2_), custom_call_target="tpu_custom_call" | custom-call | flops 1 | bytes 1 | tf_op jit(solution)/shard_map/pallas_call | solution.py:44
  26.2 4.8 %shard_map.80 = (f32[1,256,512]{2,1,0:T(8,128)S(1)}, f32[1,256,512]{2,1,0:T(8,128)S(1)}) custom-call(s32[15]{0:T(128)S(1)} %concatenate.12.refs_0_, f32[2,512,512]{2,1,0:T(8,128)S(1)} %copy-done, f32[2,256,512]{2,1,0:T(8,128)} %shard_map.78.refs_2_, f32[1,512,512]{2,1,0:T(8,128)} %collective-permute-done.5.refs_3_.refs_9_), custom_call_target="tpu_custom_call" | custom-call | flops 1 | bytes 1 | tf_op jit(solution)/shard_map/pallas_call | solution.py:44
  35.5 4.5 %shard_map.82 = (bf16[2,512,512]{2,1,0:T(8,128)(2,1)S(1)}, bf16[2,512,512]{2,1,0:T(8,128)(2,1)S(1)}, bf16[2,512,512]{2,1,0:T(8,128)(2,1)S(1)}, f32[2,512,512]{2,1,0:T(8,128)S(1)}, f32[2,16,512]{2,1,0:T(8,128)S(1)}) custom-call(s32[7]{0:T(128)S(1)} %concatenate.10.refs_0_, bf16[512,512]{1,0:T(8,128)(2,1)S(1)} %copy-done.5, bf16[512,512]{1,0:T(8,128)(2,1)S(1)} %copy-done.4, ...), custom_call_target="tpu_custom_call" | custom-call | flops 1 | bytes 1 | tf_op jit(solution)/shard_map/pallas_call | solution.py:44
  42.4 2.9 %collective-permute-start.9 = (f32[1,64,512]{2,1,0:T(8,128)S(1)}, f32[1,64,512]{2,1,0:T(8,128)S(1)}, u32[]{:S(2)}, u32[]{:S(2)}) collective-permute-start(f32[1,64,512]{2,1,0:T(8,128)S(1)} %get-tuple-element.41), channel_id=1, source_target_pairs={{0,64},{16,80},{32,96},{48,112},{64,0},{80,16},{96,32},{112,48},{1... | collective-permute-start | bytes 393224 | tf_op jit(solution)/shard_map/ppermute | solution.py:246
  46.1 2.5 %shard_map.84 = (f32[2,256,512]{2,1,0:T(8,128)S(1)}, bf16[2,256,512]{2,1,0:T(8,128)(2,1)S(1)}) custom-call(s32[7]{0:T(128)S(1)} %concatenate.10.refs_0_, f32[2,256,512]{2,1,0:T(8,128)S(1)} %shard_map.77.refs_1_, f32[2,256,512]{2,1,0:T(8,128)} %collective-permute-done.2.refs_2_, f32[2,256,512]{2,1,0:T(8,128)} %collective-permute-done.3.refs_3_, ...), custom_call_target="tpu_custom_call" | custom-call | flops 1 | bytes 1 | tf_op jit(solution)/shard_map/pallas_call | solution.py:44
  48.6 2.6 %collective-permute-done.9.refs_9_.refs_7_ = f32[1,64,512]{2,1,0:T(8,128)S(1)} collective-permute-done((f32[1,64,512]{2,1,0:T(8,128)S(1)}, f32[1,64,512]{2,1,0:T(8,128)S(1)}, u32[]{:S(2)}, u32[]{:S(2)}) %collective-permute-start.9) | collective-permute-done | bytes 131104 | tf_op jit(solution)/shard_map/ppermute | solution.py:246
  51.2 3.3 %collective-permute-done.7.refs_3_ = f32[2,256,512]{2,1,0:T(8,128)S(1)} collective-permute-done((f32[2,256,512]{2,1,0:T(8,128)S(1)}, f32[2,256,512]{2,1,0:T(8,128)S(1)}, u32[]{:S(2)}, u32[]{:S(2)}) %collective-permute-start.7) | collective-permute-done | bytes 1048608 | tf_op jit(solution)/shard_map/ppermute | solution.py:318
  56.7 7.1 %shard_map.86 = (f32[2,256,512]{2,1,0:T(8,128)S(1)}, f32[2,256,512]{2,1,0:T(8,128)S(1)}, f32[2,256,512]{2,1,0:T(8,128)S(1)}, f32[2,256,512]{2,1,0:T(8,128)S(1)}) custom-call(s32[7]{0:T(128)S(1)} %concatenate.10.refs_0_, bf16[2,256,512]{2,1,0:T(8,128)(2,1)S(1)} %get-tuple-element.38.refs_1_, bf16[2,256,512]{2,1,0:T(8,128)(2,1)S(1)} %get-tuple-element.43.refs_2_, ...), custom_call_target="tpu_custom_call" | custom-call | flops 1 | bytes 1 | tf_op jit(solution)/shard_map/pallas_call | solution.py:44
  63.8 4.7 %collective-permute-start.12 = (f32[2,256,512]{2,1,0:T(8,128)S(1)}, f32[2,256,512]{2,1,0:T(8,128)S(1)}, u32[]{:S(2)}, u32[]{:S(2)}) collective-permute-start(f32[2,256,512]{2,1,0:T(8,128)S(1)} %get-tuple-element.50.refs_1_.refs_3_), channel_id=1, source_target_pairs={{17,16},{18,17},{19,18},{20,19},{21,20},{22,21},{23,22},{24,23},{2... | collective-permute-start | bytes 3145736 | tf_op jit(solution)/shard_map/ppermute | solution.py:322
  75.9 3.9 %shard_map.88.refs_3_.refs_2_ = f32[512,512]{1,0:T(8,128)S(1)} custom-call(s32[15]{0:T(128)S(1)} %concatenate.12.refs_0_, f32[2,512,512]{2,1,0:T(8,128)S(1)} %copy-done.3, f32[2,64,512]{2,1,0:T(8,128)S(1)} %get-tuple-element.49.refs_2_.refs_1_), custom_call_target="tpu_custom_call" | custom-call | flops 1 | bytes 1 | tf_op jit(solution)/shard_map/pallas_call | solution.py:44
  81.1 4.5 %collective-permute-done.15.refs_3_ = f32[2,64,512]{2,1,0:T(8,128)S(1)} collective-permute-done((f32[2,64,512]{2,1,0:T(8,128)S(1)}, f32[2,64,512]{2,1,0:T(8,128)S(1)}, u32[]{:S(2)}, u32[]{:S(2)}) %collective-permute-start.15) | collective-permute-done | bytes 262176 | tf_op jit(solution)/shard_map/ppermute | solution.py:246
  87.4 2.6 %collective-permute-start.18 = (f32[3,16,512]{2,1,0:T(8,128)S(1)}, f32[3,16,512]{2,1,0:T(8,128)S(1)}, u32[]{:S(2)}, u32[]{:S(2)}) collective-permute-start(f32[3,16,512]{2,1,0:T(8,128)S(1)} %get-tuple-element.57), channel_id=1, source_target_pairs={{0,8},{1,9},{2,10},{3,11},{4,12},{5,13},{6,14},{7,15},{8,0},{9,1},... | collective-permute-start | bytes 294920 | tf_op jit(solution)/shard_map/ppermute | solution.py:252
  91.1 4.4 %collective-permute-start.20 = (f32[2,256,512]{2,1,0:T(8,128)S(1)}, f32[2,256,512]{2,1,0:T(8,128)S(1)}, u32[]{:S(2)}, u32[]{:S(2)}) collective-permute-start(f32[2,256,512]{2,1,0:T(8,128)S(1)} %shard_map.89.refs_9_), channel_id=1, source_target_pairs={{0,16},{16,32},{32,48},{48,64},{64,80},{80,96},{96,112},{1,17},{17... | collective-permute-start | bytes 3145736 | tf_op jit(solution)/shard_map/ppermute | solution.py:306
  95.5 3.0 %collective-permute-done.18.refs_3_.refs_5_ = f32[3,16,512]{2,1,0:T(8,128)S(1)} collective-permute-done((f32[3,16,512]{2,1,0:T(8,128)S(1)}, f32[3,16,512]{2,1,0:T(8,128)S(1)}, u32[]{:S(2)}, u32[]{:S(2)}) %collective-permute-start.18) | collective-permute-done | bytes 98336 | tf_op jit(solution)/shard_map/ppermute | solution.py:252
  99.3 3.6 %collective-permute-start.21 = (f32[2,256,512]{2,1,0:T(8,128)S(1)}, f32[2,256,512]{2,1,0:T(8,128)S(1)}, u32[]{:S(2)}, u32[]{:S(2)}) collective-permute-start(f32[2,256,512]{2,1,0:T(8,128)S(1)} %shard_map.93.refs_6_), channel_id=1, source_target_pairs={{0,16},{16,32},{32,48},{48,64},{64,80},{80,96},{96,112},{1,17},{17... | collective-permute-start | bytes 3145736 | tf_op jit(solution)/shard_map/ppermute | solution.py:306
  105.0 3.3 %collective-permute-done.24.refs_4_ = f32[3,16,512]{2,1,0:T(8,128)S(1)} collective-permute-done((f32[3,16,512]{2,1,0:T(8,128)S(1)}, f32[3,16,512]{2,1,0:T(8,128)S(1)}, u32[]{:S(2)}, u32[]{:S(2)}) %collective-permute-start.24) | collective-permute-done | bytes 98336 | tf_op jit(solution)/shard_map/ppermute | solution.py:252
  112.4 2.4 %collective-permute-start.27 = (f32[2,16,512]{2,1,0:T(8,128)S(1)}, f32[2,16,512]{2,1,0:T(8,128)S(1)}, u32[]{:S(2)}, u32[]{:S(2)}) collective-permute-start(f32[2,16,512]{2,1,0:T(8,128)S(1)} %shard_map.95.refs_1_), channel_id=1, source_target_pairs={{0,12},{1,13},{2,14},{3,15},{4,0},{5,1},{6,2},{7,3},{8,4},{9,5},{1... | collective-permute-start | bytes 196616 | tf_op jit(solution)/shard_map/ppermute | solution.py:252
  117.2 2.3 %collective-permute-done.26.refs_3_ = f32[2,16,512]{2,1,0:T(8,128)S(1)} collective-permute-done((f32[2,16,512]{2,1,0:T(8,128)S(1)}, f32[2,16,512]{2,1,0:T(8,128)S(1)}, u32[]{:S(2)}, u32[]{:S(2)}) %collective-permute-start.26) | collective-permute-done | bytes 65568 | tf_op jit(solution)/shard_map/ppermute | solution.py:252
  128.9 7.3 %collective-permute-done.28.refs_2_ = f32[4,2,16,512]{3,2,1,0:T(8,128)S(1)} collective-permute-done((f32[4,2,16,512]{3,2,1,0:T(8,128)S(1)}, f32[4,2,16,512]{3,2,1,0:T(8,128)S(1)}, u32[]{:S(2)}, u32[]{:S(2)}) %collective-permute-start.28) | collective-permute-done | bytes 262176 | tf_op jit(solution)/shard_map/ppermute | solution.py:246
  138.6 2.3 %collective-permute-done.31.refs_2_ = f32[4,4,2,16,512]{4,3,2,1,0:T(8,128)S(1)} collective-permute-done((f32[4,4,2,16,512]{4,3,2,1,0:T(8,128)S(1)}, f32[4,4,2,16,512]{4,3,2,1,0:T(8,128)S(1)}, u32[]{:S(2)}, u32[]{:S(2)}) %collective-permute-start.31) | collective-permute-done | bytes 1048608 | tf_op jit(solution)/shard_map/ppermute | solution.py:301
  (87 shorter events, 54.7 us)
Async XLA Ops:
  1.9 20.0 %collective-permute-start.2 = (f32[2,256,512]{2,1,0:T(8,128)S(1)}, f32[2,256,512]{2,1,0:T(8,128)}, u32[]{:S(2)}, u32[]{:S(2)}) collective-permute-start(f32[2,256,512]{2,1,0:T(8,128)S(1)} %shard_map.77.refs_1_), channel_id=1, source_target_pairs={{16,0},{32,16},{48,32},{64,48},{80,64},{96,80},{112,96},{17,1},{33... | collective-permute-start | bytes 3145736 | tf_op jit(solution)/shard_map/ppermute | solution.py:306
  6.6 19.6 %collective-permute-start.5 = (f32[1,512,512]{2,1,0:T(8,128)}, f32[1,512,512]{2,1,0:T(8,128)}, u32[]{:S(2)}, u32[]{:S(2)}) collective-permute-start(f32[1,512,512]{2,1,0:T(8,128)} %refs_8_.1), channel_id=1, source_target_pairs={{16,17},{17,18},{18,19},{19,20},{20,21},{21,22},{22,23},{23,24},{2... | collective-permute-start | bytes 3145736 | tf_op jit(solution)/shard_map/ppermute | solution.py:318
  14.0 17.7 %collective-permute-start.4 = (f32[2,256,512]{2,1,0:T(8,128)}, f32[2,256,512]{2,1,0:T(8,128)}, u32[]{:S(2)}, u32[]{:S(2)}) collective-permute-start(f32[2,256,512]{2,1,0:T(8,128)} %copy-done.1), channel_id=1, source_target_pairs={{16,0},{32,16},{48,32},{64,48},{80,64},{96,80},{112,96},{17,1},{33... | collective-permute-start | bytes 3145736 | tf_op jit(solution)/shard_map/ppermute | solution.py:306
  17.0 9.1 %collective-permute-start.1 = (s32[4]{0:T(128)S(1)}, s32[4]{0:T(128)S(1)}, u32[]{:S(2)}, u32[]{:S(2)}) collective-permute-start(s32[4]{0:T(128)S(1)} %pad_add_fusion), channel_id=1, source_target_pairs={{0,16},{16,32},{32,48},{48,64},{64,80},{80,96},{96,112},{1,17},{17... | collective-permute-start | bytes 56 | tf_op jit(solution)/shard_map/ppermute | solution.py:306
  24.2 21.9 %collective-permute-start.3 = (f32[2,256,512]{2,1,0:T(8,128)}, f32[2,256,512]{2,1,0:T(8,128)}, u32[]{:S(2)}, u32[]{:S(2)}) collective-permute-start(f32[2,256,512]{2,1,0:T(8,128)} %shard_map.78.refs_2_), channel_id=1, source_target_pairs={{16,17},{17,18},{18,19},{19,20},{20,21},{21,22},{22,23},{23,24},{2... | collective-permute-start | bytes 3145736 | tf_op jit(solution)/shard_map/ppermute | solution.py:318
  33.3 21.2 %collective-permute-start.7 = (f32[2,256,512]{2,1,0:T(8,128)S(1)}, f32[2,256,512]{2,1,0:T(8,128)S(1)}, u32[]{:S(2)}, u32[]{:S(2)}) collective-permute-start(f32[2,256,512]{2,1,0:T(8,128)S(1)} %shard_map.81.refs_4_), channel_id=1, source_target_pairs={{16,17},{17,18},{18,19},{19,20},{20,21},{21,22},{22,23},{23,24},{2... | collective-permute-start | bytes 3145736 | tf_op jit(solution)/shard_map/ppermute | solution.py:318
  40.7 7.9 %collective-permute-start.8 = (f32[1,64,512]{2,1,0:T(8,128)S(1)}, f32[1,64,512]{2,1,0:T(8,128)S(1)}, u32[]{:S(2)}, u32[]{:S(2)}) collective-permute-start(f32[1,64,512]{2,1,0:T(8,128)S(1)} %get-tuple-element.40), channel_id=1, source_target_pairs={{0,32},{16,48},{32,64},{48,80},{64,96},{80,112},{96,0},{112,16},{1... | collective-permute-start | bytes 393224 | tf_op jit(solution)/shard_map/ppermute | solution.py:246
  42.4 8.8 %collective-permute-start.9 = (f32[1,64,512]{2,1,0:T(8,128)S(1)}, f32[1,64,512]{2,1,0:T(8,128)S(1)}, u32[]{:S(2)}, u32[]{:S(2)}) collective-permute-start(f32[1,64,512]{2,1,0:T(8,128)S(1)} %get-tuple-element.41), channel_id=1, source_target_pairs={{0,64},{16,80},{32,96},{48,112},{64,0},{80,16},{96,32},{112,48},{1... | collective-permute-start | bytes 393224 | tf_op jit(solution)/shard_map/ppermute | solution.py:246
  63.7 6.7 %collective-permute-start.11 = (f32[2,256,512]{2,1,0:T(8,128)S(1)}, f32[2,256,512]{2,1,0:T(8,128)S(1)}, u32[]{:S(2)}, u32[]{:S(2)}) collective-permute-start(f32[2,256,512]{2,1,0:T(8,128)S(1)} %get-tuple-element.48), channel_id=1, source_target_pairs={{0,16},{16,0},{32,48},{48,32},{64,80},{80,64},{96,112},{112,96},{1... | collective-permute-start | bytes 3145736 | tf_op jit(solution)/shard_map/ppermute | solution.py:301
  63.8 16.4 %collective-permute-start.12 = (f32[2,256,512]{2,1,0:T(8,128)S(1)}, f32[2,256,512]{2,1,0:T(8,128)S(1)}, u32[]{:S(2)}, u32[]{:S(2)}) collective-permute-start(f32[2,256,512]{2,1,0:T(8,128)S(1)} %get-tuple-element.50.refs_1_.refs_3_), channel_id=1, source_target_pairs={{17,16},{18,17},{19,18},{20,19},{21,20},{22,21},{23,22},{24,23},{2... | collective-permute-start | bytes 3145736 | tf_op jit(solution)/shard_map/ppermute | solution.py:322
  68.5 26.9 %collective-permute-start.13 = (f32[2,256,512]{2,1,0:T(8,128)S(1)}, f32[2,256,512]{2,1,0:T(8,128)S(1)}, u32[]{:S(2)}, u32[]{:S(2)}) collective-permute-start(f32[2,256,512]{2,1,0:T(8,128)S(1)} %get-tuple-element.51.refs_4_.refs_1_), channel_id=1, source_target_pairs={{17,16},{18,17},{19,18},{20,19},{21,20},{22,21},{23,22},{24,23},{2... | collective-permute-start | bytes 3145736 | tf_op jit(solution)/shard_map/ppermute | solution.py:322
  71.1 9.9 %collective-permute-start.14 = (f32[2,64,512]{2,1,0:T(8,128)S(1)}, f32[2,64,512]{2,1,0:T(8,128)S(1)}, u32[]{:S(2)}, u32[]{:S(2)}) collective-permute-start(f32[2,64,512]{2,1,0:T(8,128)S(1)} %get-tuple-element.52), channel_id=1, source_target_pairs={{0,32},{16,48},{32,64},{48,80},{64,96},{80,112},{96,0},{112,16},{1... | collective-permute-start | bytes 786440 | tf_op jit(solution)/shard_map/ppermute | solution.py:246
  72.1 13.4 %collective-permute-start.15 = (f32[2,64,512]{2,1,0:T(8,128)S(1)}, f32[2,64,512]{2,1,0:T(8,128)S(1)}, u32[]{:S(2)}, u32[]{:S(2)}) collective-permute-start(f32[2,64,512]{2,1,0:T(8,128)S(1)} %get-tuple-element.53), channel_id=1, source_target_pairs={{0,64},{16,80},{32,96},{48,112},{64,0},{80,16},{96,32},{112,48},{1... | collective-permute-start | bytes 786440 | tf_op jit(solution)/shard_map/ppermute | solution.py:246
  74.3 11.8 %collective-permute-start.16 = (f32[2,64,512]{2,1,0:T(8,128)S(1)}, f32[2,64,512]{2,1,0:T(8,128)S(1)}, u32[]{:S(2)}, u32[]{:S(2)}) collective-permute-start(f32[2,64,512]{2,1,0:T(8,128)S(1)} %get-tuple-element.54), channel_id=1, source_target_pairs={{0,96},{16,112},{32,0},{48,16},{64,32},{80,48},{96,64},{112,80},{1... | collective-permute-start | bytes 786440 | tf_op jit(solution)/shard_map/ppermute | solution.py:246
  86.8 8.7 %collective-permute-start.17 = (f32[3,16,512]{2,1,0:T(8,128)S(1)}, f32[3,16,512]{2,1,0:T(8,128)S(1)}, u32[]{:S(2)}, u32[]{:S(2)}) collective-permute-start(f32[3,16,512]{2,1,0:T(8,128)S(1)} %get-tuple-element.56), channel_id=1, source_target_pairs={{0,4},{1,5},{2,6},{3,7},{4,8},{5,9},{6,10},{7,11},{8,12},{9,13},{1... | collective-permute-start | bytes 294920 | tf_op jit(solution)/shard_map/ppermute | solution.py:252
  87.4 11.1 %collective-permute-start.18 = (f32[3,16,512]{2,1,0:T(8,128)S(1)}, f32[3,16,512]{2,1,0:T(8,128)S(1)}, u32[]{:S(2)}, u32[]{:S(2)}) collective-permute-start(f32[3,16,512]{2,1,0:T(8,128)S(1)} %get-tuple-element.57), channel_id=1, source_target_pairs={{0,8},{1,9},{2,10},{3,11},{4,12},{5,13},{6,14},{7,15},{8,0},{9,1},... | collective-permute-start | bytes 294920 | tf_op jit(solution)/shard_map/ppermute | solution.py:252
  90.0 8.5 %collective-permute-start.19 = (f32[3,16,512]{2,1,0:T(8,128)S(1)}, f32[3,16,512]{2,1,0:T(8,128)S(1)}, u32[]{:S(2)}, u32[]{:S(2)}) collective-permute-start(f32[3,16,512]{2,1,0:T(8,128)S(1)} %get-tuple-element.58), channel_id=1, source_target_pairs={{0,12},{1,13},{2,14},{3,15},{4,0},{5,1},{6,2},{7,3},{8,4},{9,5},{1... | collective-permute-start | bytes 294920 | tf_op jit(solution)/shard_map/ppermute | solution.py:252
  91.1 32.7 %collective-permute-start.20 = (f32[2,256,512]{2,1,0:T(8,128)S(1)}, f32[2,256,512]{2,1,0:T(8,128)S(1)}, u32[]{:S(2)}, u32[]{:S(2)}) collective-permute-start(f32[2,256,512]{2,1,0:T(8,128)S(1)} %shard_map.89.refs_9_), channel_id=1, source_target_pairs={{0,16},{16,32},{32,48},{48,64},{64,80},{80,96},{96,112},{1,17},{17... | collective-permute-start | bytes 3145736 | tf_op jit(solution)/shard_map/ppermute | solution.py:306
  99.3 24.5 %collective-permute-start.21 = (f32[2,256,512]{2,1,0:T(8,128)S(1)}, f32[2,256,512]{2,1,0:T(8,128)S(1)}, u32[]{:S(2)}, u32[]{:S(2)}) collective-permute-start(f32[2,256,512]{2,1,0:T(8,128)S(1)} %shard_map.93.refs_6_), channel_id=1, source_target_pairs={{0,16},{16,32},{32,48},{48,64},{64,80},{80,96},{96,112},{1,17},{17... | collective-permute-start | bytes 3145736 | tf_op jit(solution)/shard_map/ppermute | solution.py:306
  103.5 6.0 %collective-permute-start.23 = (f32[3,16,512]{2,1,0:T(8,128)S(1)}, f32[3,16,512]{2,1,0:T(8,128)S(1)}, u32[]{:S(2)}, u32[]{:S(2)}) collective-permute-start(f32[3,16,512]{2,1,0:T(8,128)S(1)} %shard_map.91.refs_7_.refs_1_), channel_id=1, source_target_pairs={{0,2},{1,3},{2,0},{3,1},{4,6},{5,7},{6,4},{7,5},{8,10},{9,11},{10,... | collective-permute-start | bytes 294920 | tf_op jit(solution)/shard_map/ppermute | solution.py:252
  103.6 8.2 %collective-permute-start.22 = (f32[3,16,512]{2,1,0:T(8,128)S(1)}, f32[3,16,512]{2,1,0:T(8,128)S(1)}, u32[]{:S(2)}, u32[]{:S(2)}) collective-permute-start(f32[3,16,512]{2,1,0:T(8,128)S(1)} %shard_map.91.refs_7_.refs_1_), channel_id=1, source_target_pairs={{0,1},{1,2},{2,3},{3,0},{4,5},{5,6},{6,7},{7,4},{8,9},{9,10},{10,1... | collective-permute-start | bytes 294920 | tf_op jit(solution)/shard_map/ppermute | solution.py:252
  121.2 6.5 %collective-permute-start.30 = (f32[4,2,16,512]{3,2,1,0:T(8,128)S(1)}, f32[4,2,16,512]{3,2,1,0:T(8,128)S(1)}, u32[]{:S(2)}, u32[]{:S(2)}) collective-permute-start(f32[4,2,16,512]{3,2,1,0:T(8,128)S(1)} %shard_map.96.refs_1_), channel_id=1, source_target_pairs={{0,96},{16,112},{32,0},{48,16},{64,32},{80,48},{96,64},{112,80},{1... | collective-permute-start | bytes 786440 | tf_op jit(solution)/shard_map/ppermute | solution.py:246
  121.3 7.7 %collective-permute-start.29 = (f32[4,2,16,512]{3,2,1,0:T(8,128)S(1)}, f32[4,2,16,512]{3,2,1,0:T(8,128)S(1)}, u32[]{:S(2)}, u32[]{:S(2)}) collective-permute-start(f32[4,2,16,512]{3,2,1,0:T(8,128)S(1)} %shard_map.96.refs_1_), channel_id=1, source_target_pairs={{0,64},{16,80},{32,96},{48,112},{64,0},{80,16},{96,32},{112,48},{1... | collective-permute-start | bytes 786440 | tf_op jit(solution)/shard_map/ppermute | solution.py:246
  123.0 13.3 %collective-permute-start.28 = (f32[4,2,16,512]{3,2,1,0:T(8,128)S(1)}, f32[4,2,16,512]{3,2,1,0:T(8,128)S(1)}, u32[]{:S(2)}, u32[]{:S(2)}) collective-permute-start(f32[4,2,16,512]{3,2,1,0:T(8,128)S(1)} %shard_map.96.refs_1_), channel_id=1, source_target_pairs={{0,32},{16,48},{32,64},{48,80},{64,96},{80,112},{96,0},{112,16},{1... | collective-permute-start | bytes 786440 | tf_op jit(solution)/shard_map/ppermute | solution.py:246
  (18 other events, 90.0 us)

commit v5 on v4

--- a/solution.py
+++ b/solution.py
@@ -154,15 +154,19 @@
     half[1] = (by_re[n:] + by_im[:n]).astype(BF16)
 
 
+def pick_kernel(s, own, moved, out):
+    out[...] = jnp.where(s[CORE] == 1, moved[...], own[...])
+
+
 def dot_t(a, b):
     return lax.dot_general(a, b, (((1,), (1,)), ((), ())), preferred_element_type=F32)
 
 
 def fourier_kernel(s, *refs):
     halves, patches = (refs[i * CHUNKS : (i + 1) * CHUNKS] for i in range(2))
-    col_table, row_table, row_table_t, amps, amps_moved, turned = refs[2 * CHUNKS : 2 * CHUNKS + 6]
-    grads, (keep, send, stack, change, back, numer) = refs[2 * CHUNKS + 6 :][:2], refs[2 * CHUNKS + 8 :]
-    r, c, odd = s[ROW], s[COL], s[CORE] == 1
+    col_table, row_table, row_table_t, amps, turned = refs[2 * CHUNKS : 2 * CHUNKS + 5]
+    grads, (keep, send, stack, change, back, numer) = refs[2 * CHUNKS + 5 :][:2], refs[2 * CHUNKS + 7 :]
+    r, c = s[ROW], s[COL]
     for i, (first, last) in enumerate(SPANS):
         for k in range(2):
             stack[first:last, k * F : (k + 1) * F] = halves[i][k]
@@ -173,8 +177,7 @@
         by_re = jnp.dot(row_table_t[0], cols, preferred_element_type=F32)
         by_im = jnp.dot(row_table_t[1], cols, preferred_element_type=F32)
         re, im = by_re[:, :wide] - by_im[:, wide:], by_re[:, wide:] + by_im[:, :wide]
-        a = jnp.where(odd, amps_moved[0, :, at], amps[0, :, at])
-        factor = a / jnp.maximum(jnp.sqrt(re * re + im * im), 0.25) - 1.0
+        factor = amps[0, :, at] / jnp.maximum(jnp.sqrt(re * re + im * im), 0.25) - 1.0
         change[:, :wide] = (factor * re).astype(BF16)
         change[:, wide:] = (factor * im).astype(BF16)
         by_re = jnp.dot(row_table[0], change[...], preferred_element_type=F32)
@@ -348,7 +351,7 @@
             call(
                 functools.partial(lend_kernel, SPANS[i]),
                 [shapes[i]],
-                (s, tiles[i], below[i]),
+                (touch, tiles[i], below[i]),
                 after=after,
                 keep=jax.ShapeDtypeStruct,
             )
@@ -385,18 +388,25 @@
             functools.partial(half_kernel, span),
             [shapes[i], (shapes[i][0], BF16)],
             (s, tiles[i], below[i], beside[i], turned, col_table),
-            after=(seen[0],) if i == 0 else (patches[-1], *seen),
+            after=(seen[0],) if i == 0 else (patches[-1], *seen, amps),
             limit=16,
             keep=jax.ShapeDtypeStruct,
         )
         patches.append(patch)
         halves.append(half)
+        if i == 0:
+            (amps,) = call(
+                pick_kernel,
+                [((1, F, F), F32)],
+                (s, amplitudes, amps_moved),
+                after=(patch,),
+            )
 
     half_tile = ((2, HALF, F), F32)
     *grads, keep, send = call(
         fourier_kernel,
         [half_tile] * 2 + [((2, HALF, F), F32)] * 2,
-        (s, *halves, *patches, col_table, row_table, row_table_t, amplitudes, amps_moved, turned),
+        (s, *halves, *patches, col_table, row_table, row_table_t, amps, turned),
         limit=24,
         scratch=[
             pltpu.VMEM((F, 2 * F), BF16),

time: 144 us -> 150 us (1.042)
  local copies, waits for them, and re-layouts: 2.34 us -> 6.68 us
  Pallas kernels: 42.5 us -> 45.8 us
  waiting for transfers between devices: 39.9 us -> 36.7 us
  starting transfers between devices: 55.6 us -> 57.3 us
    unnamed x20 -> x26, local copies, waits for them, and re-layouts: 2.17 us -> 5.89 us
    ppermute x2, starting transfers between devices: 6.59 us -> 10 us  [homeward(): return lax.ppermute(value, ('obj', 'pos'), [(b, a) for a, b in x_pairs()])]
    ppermute x3, waiting for transfers between devices: 3.31 us -> 0.01 us  [toward(): return lax.ppermute(value, ('obj', 'pos'), x_pairs(odd_only))]
    pallas_call x20 -> x21, Pallas kernels: 40.1 us -> 43.3 us  [call(): pl.pallas_call(run, out_shape=[keep(s, d) for s, d in out_shapes], in_spe...]
    ppermute x9, starting transfers between devices: 8.93 us -> 7.31 us  [turn(): return lax.ppermute(value, 'pos', pairs)]
  transfers between devices with their start and end apart: 32 -> 32, of which waited for: 18 -> 15; matrix products, arithmetic and copies ran while one was open for 1% -> 2% of each run, Pallas kernels for 21% -> 23%
where the time goes in v5:
time: 150 us; the launch traced here: 149 us
  starting transfers between devices  57.3 us (38%)
  Pallas kernels  45.8 us (31%)
  waiting for transfers between devices  36.7 us (24%)
  local copies, waits for them, and re-layouts  6.68 us (4%)
    pallas_call x21, Pallas kernels, call(): pl.pallas_call(run, out_shape=[keep(s, d) for s, d in out_shapes], in_spe...  43.3 us
    ppermute x5, starting transfers between devices, shifted(): lax.ppermute(value, 'obj', [(o, o + steps) for o in range(n) if 0 <= o +...  17.5 us
    ppermute x9, waiting for transfers between devices, turn(): lax.ppermute(value, 'obj', [(o, (o + 2 * steps) % (2 * Z)) for o in range...  17.4 us
    ppermute x9, waiting for transfers between devices, turn(): return lax.ppermute(value, 'pos', pairs)  14.8 us
    ppermute x9, starting transfers between devices, turn(): lax.ppermute(value, 'obj', [(o, (o + 2 * steps) % (2 * Z)) for o in range...  12 us
    ppermute x2, starting transfers between devices, homeward(): return lax.ppermute(value, ('obj', 'pos'), [(b, a) for a, b in x_pairs()])  10 us
    ppermute x9, starting transfers between devices, turn(): return lax.ppermute(value, 'pos', pairs)  7.31 us
    ppermute x3, starting transfers between devices, toward(): return lax.ppermute(value, ('obj', 'pos'), x_pairs(odd_only))  7.06 us
  transfers between devices with their start and end apart: 32, of which 15 were waited for; matrix products, arithmetic and copies ran while one was open for 2% of the time, Pallas kernels for 23%

profile of v5, /device:TPU:1, one launch (start us, length us, event | category | flops | bytes accessed | tf_op | source)
XLA Modules:
  0.0 149.1 jit_solution(14170139673846941653)
XLA Ops:
  1.9 3.3 %collective-permute-start.2 = (f32[2,256,512]{2,1,0:T(8,128)S(1)}, f32[2,256,512]{2,1,0:T(8,128)}, u32[]{:S(2)}, u32[]{:S(2)}) collective-permute-start(f32[2,256,512]{2,1,0:T(8,128)S(1)} %shard_map.77.refs_1_), channel_id=1, source_target_pairs={{16,0},{32,16},{48,32},{64,48},{80,64},{96,80},{112,96},{17,1},{33... | collective-permute-start | bytes 3145736 | tf_op jit(solution)/shard_map/ppermute | solution.py:309
  6.6 3.1 %collective-permute-start.5 = (f32[1,512,512]{2,1,0:T(8,128)}, f32[1,512,512]{2,1,0:T(8,128)}, u32[]{:S(2)}, u32[]{:S(2)}) collective-permute-start(f32[1,512,512]{2,1,0:T(8,128)} %refs_1_.5), channel_id=1, source_target_pairs={{16,17},{17,18},{18,19},{19,20},{20,21},{21,22},{22,23},{23,24},{2... | collective-permute-start | bytes 3145736 | tf_op jit(solution)/shard_map/ppermute | solution.py:321
  14.0 2.3 %collective-permute-start.4 = (f32[2,256,512]{2,1,0:T(8,128)}, f32[2,256,512]{2,1,0:T(8,128)}, u32[]{:S(2)}, u32[]{:S(2)}) collective-permute-start(f32[2,256,512]{2,1,0:T(8,128)} %copy-done.1), channel_id=1, source_target_pairs={{16,0},{32,16},{48,32},{64,48},{80,64},{96,80},{112,96},{17,1},{33... | collective-permute-start | bytes 3145736 | tf_op jit(solution)/shard_map/ppermute | solution.py:309
  17.1 4.1 %collective-permute-start.1 = (s32[4]{0:T(128)S(1)}, s32[4]{0:T(128)S(1)}, u32[]{:S(2)}, u32[]{:S(2)}) collective-permute-start(s32[4]{0:T(128)S(1)} %pad_add_fusion), channel_id=1, source_target_pairs={{0,16},{16,32},{32,48},{48,64},{64,80},{80,96},{96,112},{1,17},{17... | collective-permute-start | bytes 56 | tf_op jit(solution)/shard_map/ppermute | solution.py:309
  22.7 2.3 %shard_map.78.refs_2_ = f32[2,256,512]{2,1,0:T(8,128)} custom-call(s32[15]{0:T(128)S(1)} %concatenate.12.refs_0_, f32[2,256,512]{2,1,0:T(8,128)S(1)} %shard_map.77.refs_1_, f32[2,256,512]{2,1,0:T(8,128)} %collective-permute-done.2.refs_2_), custom_call_target="tpu_custom_call" | custom-call | flops 1 | bytes 1 | tf_op jit(solution)/shard_map/pallas_call | solution.py:44
  27.1 5.5 %shard_map.80 = (f32[1,256,512]{2,1,0:T(8,128)S(1)}, f32[1,256,512]{2,1,0:T(8,128)}) custom-call(s32[15]{0:T(128)S(1)} %concatenate.12.refs_0_, f32[2,512,512]{2,1,0:T(8,128)S(1)} %copy-done, f32[2,256,512]{2,1,0:T(8,128)} %shard_map.78.refs_2_, f32[1,512,512]{2,1,0:T(8,128)} %collective-permute-done.5.refs_3_.refs_2_), custom_call_target="tpu_custom_call" | custom-call | flops 1 | bytes 1 | tf_op jit(solution)/shard_map/pallas_call | solution.py:44
  32.6 2.5 %shard_map.81.refs_4_ = f32[2,256,512]{2,1,0:T(8,128)} custom-call(s32[15]{0:T(128)S(1)} %concatenate.12.refs_0_, f32[2,256,512]{2,1,0:T(8,128)S(1)} %copy-done.2, f32[2,256,512]{2,1,0:T(8,128)} %collective-permute-done.4.refs_2_, f32[1,256,512]{2,1,0:T(8,128)S(1)} %get-tuple-element.33.refs_3_.refs_1_), custom_call_target="tpu_custom_call" | custom-call | flops 1 | bytes 1 | tf_op jit(solution)/shard_map/pallas_call | solution.py:44
  40.9 4.5 %shard_map.82 = (bf16[2,512,512]{2,1,0:T(8,128)(2,1)S(1)}, bf16[2,512,512]{2,1,0:T(8,128)(2,1)S(1)}, bf16[2,512,512]{2,1,0:T(8,128)(2,1)S(1)}, f32[2,512,512]{2,1,0:T(8,128)S(1)}, f32[2,16,512]{2,1,0:T(8,128)S(1)}) custom-call(s32[7]{0:T(128)S(1)} %concatenate.10.refs_0_, bf16[512,512]{1,0:T(8,128)(2,1)S(1)} %copy-done.9, bf16[512,512]{1,0:T(8,128)(2,1)S(1)} %copy-done.8, ...), custom_call_target="tpu_custom_call" | custom-call | flops 1 | bytes 1 | tf_op jit(solution)/shard_map/pallas_call | solution.py:44
  48.2 3.1 %collective-permute-start.9 = (f32[1,64,512]{2,1,0:T(8,128)S(1)}, f32[1,64,512]{2,1,0:T(8,128)S(1)}, u32[]{:S(2)}, u32[]{:S(2)}) collective-permute-start(f32[1,64,512]{2,1,0:T(8,128)S(1)} %get-tuple-element.41), channel_id=1, source_target_pairs={{0,64},{16,80},{32,96},{48,112},{64,0},{80,16},{96,32},{112,48},{1... | collective-permute-start | bytes 393224 | tf_op jit(solution)/shard_map/ppermute | solution.py:249
  52.0 2.4 %shard_map.84 = (f32[2,256,512]{2,1,0:T(8,128)S(1)}, bf16[2,256,512]{2,1,0:T(8,128)(2,1)S(1)}) custom-call(s32[7]{0:T(128)S(1)} %concatenate.10.refs_0_, f32[2,256,512]{2,1,0:T(8,128)S(1)} %shard_map.77.refs_1_, f32[2,256,512]{2,1,0:T(8,128)} %collective-permute-done.2.refs_2_, f32[2,256,512]{2,1,0:T(8,128)} %collective-permute-done.3.refs_3_, ...), custom_call_target="tpu_custom_call" | custom-call | flops 1 | bytes 1 | tf_op jit(solution)/shard_map/pallas_call | solution.py:44
  57.2 2.4 %shard_map.86 = (f32[2,256,512]{2,1,0:T(8,128)S(1)}, bf16[2,256,512]{2,1,0:T(8,128)(2,1)S(1)}) custom-call(s32[7]{0:T(128)S(1)} %concatenate.10.refs_0_, f32[2,256,512]{2,1,0:T(8,128)S(1)} %copy-done.3, f32[2,256,512]{2,1,0:T(8,128)} %collective-permute-done.4.refs_2_, f32[2,256,512]{2,1,0:T(8,128)} %collective-permute-done.7.refs_3_, ...), custom_call_target="tpu_custom_call" | custom-call | flops 1 | bytes 1 | tf_op jit(solution)/shard_map/pallas_call | solution.py:44
  59.7 5.9 %shard_map.87 = (f32[2,256,512]{2,1,0:T(8,128)S(1)}, f32[2,256,512]{2,1,0:T(8,128)S(1)}, f32[2,256,512]{2,1,0:T(8,128)S(1)}, f32[2,256,512]{2,1,0:T(8,128)S(1)}) custom-call(s32[7]{0:T(128)S(1)} %concatenate.10.refs_0_, bf16[2,256,512]{2,1,0:T(8,128)(2,1)S(1)} %get-tuple-element.38.refs_1_, bf16[2,256,512]{2,1,0:T(8,128)(2,1)S(1)} %get-tuple-element.43.refs_2_, ...), custom_call_target="tpu_custom_call" | custom-call | flops 1 | bytes 1 | tf_op jit(solution)/shard_map/pallas_call | solution.py:44
  67.0 7.7 %collective-permute-start.12 = (f32[2,256,512]{2,1,0:T(8,128)S(1)}, f32[2,256,512]{2,1,0:T(8,128)S(1)}, u32[]{:S(2)}, u32[]{:S(2)}) collective-permute-start(f32[2,256,512]{2,1,0:T(8,128)S(1)} %get-tuple-element.50.refs_1_.refs_3_), channel_id=1, source_target_pairs={{17,16},{18,17},{19,18},{20,19},{21,20},{22,21},{23,22},{24,23},{2... | collective-permute-start | bytes 3145736 | tf_op jit(solution)/shard_map/ppermute | solution.py:325
  74.7 2.4 %collective-permute-start.13 = (f32[2,256,512]{2,1,0:T(8,128)S(1)}, f32[2,256,512]{2,1,0:T(8,128)S(1)}, u32[]{:S(2)}, u32[]{:S(2)}) collective-permute-start(f32[2,256,512]{2,1,0:T(8,128)S(1)} %get-tuple-element.51.refs_4_.refs_1_), channel_id=1, source_target_pairs={{17,16},{18,17},{19,18},{20,19},{21,20},{22,21},{23,22},{24,23},{2... | collective-permute-start | bytes 3145736 | tf_op jit(solution)/shard_map/ppermute | solution.py:325
  81.8 3.9 %shard_map.89.refs_3_.refs_2_ = f32[512,512]{1,0:T(8,128)S(1)} custom-call(s32[15]{0:T(128)S(1)} %concatenate.12.refs_0_, f32[2,512,512]{2,1,0:T(8,128)S(1)} %copy-done.5, f32[2,64,512]{2,1,0:T(8,128)S(1)} %get-tuple-element.49.refs_2_.refs_1_), custom_call_target="tpu_custom_call" | custom-call | flops 1 | bytes 1 | tf_op jit(solution)/shard_map/pallas_call | solution.py:44
  87.3 5.2 %collective-permute-done.15.refs_3_ = f32[2,64,512]{2,1,0:T(8,128)S(1)} collective-permute-done((f32[2,64,512]{2,1,0:T(8,128)S(1)}, f32[2,64,512]{2,1,0:T(8,128)S(1)}, u32[]{:S(2)}, u32[]{:S(2)}) %collective-permute-start.15) | collective-permute-done | bytes 262176 | tf_op jit(solution)/shard_map/ppermute | solution.py:249
  96.6 4.5 %collective-permute-start.20 = (f32[2,256,512]{2,1,0:T(8,128)S(1)}, f32[2,256,512]{2,1,0:T(8,128)S(1)}, u32[]{:S(2)}, u32[]{:S(2)}) collective-permute-start(f32[2,256,512]{2,1,0:T(8,128)S(1)} %shard_map.90.refs_9_), channel_id=1, source_target_pairs={{0,16},{16,32},{32,48},{48,64},{64,80},{80,96},{96,112},{1,17},{17... | collective-permute-start | bytes 3145736 | tf_op jit(solution)/shard_map/ppermute | solution.py:309
  101.2 4.3 %collective-permute-done.18.refs_3_.refs_5_ = f32[3,16,512]{2,1,0:T(8,128)S(1)} collective-permute-done((f32[3,16,512]{2,1,0:T(8,128)S(1)}, f32[3,16,512]{2,1,0:T(8,128)S(1)}, u32[]{:S(2)}, u32[]{:S(2)}) %collective-permute-start.18) | collective-permute-done | bytes 98336 | tf_op jit(solution)/shard_map/ppermute | solution.py:255
  106.2 3.2 %collective-permute-start.21 = (f32[2,256,512]{2,1,0:T(8,128)S(1)}, f32[2,256,512]{2,1,0:T(8,128)S(1)}, u32[]{:S(2)}, u32[]{:S(2)}) collective-permute-start(f32[2,256,512]{2,1,0:T(8,128)S(1)} %shard_map.94.refs_6_), channel_id=1, source_target_pairs={{0,16},{16,32},{32,48},{48,64},{64,80},{80,96},{96,112},{1,17},{17... | collective-permute-start | bytes 3145736 | tf_op jit(solution)/shard_map/ppermute | solution.py:309
  111.6 3.3 %collective-permute-done.24.refs_4_ = f32[3,16,512]{2,1,0:T(8,128)S(1)} collective-permute-done((f32[3,16,512]{2,1,0:T(8,128)S(1)}, f32[3,16,512]{2,1,0:T(8,128)S(1)}, u32[]{:S(2)}, u32[]{:S(2)}) %collective-permute-start.24) | collective-permute-done | bytes 98336 | tf_op jit(solution)/shard_map/ppermute | solution.py:255
  116.0 2.3 %collective-permute-done.22.refs_2_ = f32[3,16,512]{2,1,0:T(8,128)S(1)} collective-permute-done((f32[3,16,512]{2,1,0:T(8,128)S(1)}, f32[3,16,512]{2,1,0:T(8,128)S(1)}, u32[]{:S(2)}, u32[]{:S(2)}) %collective-permute-start.22) | collective-permute-done | bytes 98336 | tf_op jit(solution)/shard_map/ppermute | solution.py:255
  123.0 2.7 %collective-permute-done.26.refs_3_ = f32[2,16,512]{2,1,0:T(8,128)S(1)} collective-permute-done((f32[2,16,512]{2,1,0:T(8,128)S(1)}, f32[2,16,512]{2,1,0:T(8,128)S(1)}, u32[]{:S(2)}, u32[]{:S(2)}) %collective-permute-start.26) | collective-permute-done | bytes 65568 | tf_op jit(solution)/shard_map/ppermute | solution.py:255
  129.8 2.3 %shard_map.95 = (f32[2,512,512]{2,1,0:T(8,128)}, f32[8,128]{1,0:T(8,128)}) custom-call(s32[7]{0:T(128)S(1)} %concatenate.10.refs_0_, f32[2,512,512]{2,1,0:T(8,128)S(1)} %get-tuple-element.59.refs_1_.refs_5_, f32[512,512]{1,0:T(8,128)S(1)} %get-tuple-element.60.refs_2_, f32[2,256,512]{2,1,0:T(8,128)S(1)} %collective-permute-done.20.refs_3_, ...), custom_call_target="tpu_custom_call" | custom-call | flops 1 | bytes 1 | tf_op jit(solution)/shard_map/pallas_call | solution.py:44
  135.5 7.3 %collective-permute-done.28.refs_2_ = f32[4,2,16,512]{3,2,1,0:T(8,128)S(1)} collective-permute-done((f32[4,2,16,512]{3,2,1,0:T(8,128)S(1)}, f32[4,2,16,512]{3,2,1,0:T(8,128)S(1)}, u32[]{:S(2)}, u32[]{:S(2)}) %collective-permute-start.28) | collective-permute-done | bytes 262176 | tf_op jit(solution)/shard_map/ppermute | solution.py:249
  (94 shorter events, 57.3 us)
Async XLA Ops:
  1.9 20.8 %collective-permute-start.2 = (f32[2,256,512]{2,1,0:T(8,128)S(1)}, f32[2,256,512]{2,1,0:T(8,128)}, u32[]{:S(2)}, u32[]{:S(2)}) collective-permute-start(f32[2,256,512]{2,1,0:T(8,128)S(1)} %shard_map.77.refs_1_), channel_id=1, source_target_pairs={{16,0},{32,16},{48,32},{64,48},{80,64},{96,80},{112,96},{17,1},{33... | collective-permute-start | bytes 3145736 | tf_op jit(solution)/shard_map/ppermute | solution.py:309
  5.3 6.0 %collective-permute-start = (s32[2]{0:T(128)S(1)}, s32[2]{0:T(128)S(1)}, u32[]{:S(2)}, u32[]{:S(2)}) collective-permute-start(s32[2]{0:T(128)S(1)} %add_subtract_fusion), channel_id=1, source_target_pairs={{0,1},{1,2},{2,3},{3,4},{4,5},{5,6},{6,7},{7,8},{8,9},{9,10},{10,1... | collective-permute-start | bytes 32 | tf_op jit(solution)/shard_map/ppermute | solution.py:335
  6.6 20.4 %collective-permute-start.5 = (f32[1,512,512]{2,1,0:T(8,128)}, f32[1,512,512]{2,1,0:T(8,128)}, u32[]{:S(2)}, u32[]{:S(2)}) collective-permute-start(f32[1,512,512]{2,1,0:T(8,128)} %refs_1_.5), channel_id=1, source_target_pairs={{16,17},{17,18},{18,19},{19,20},{20,21},{21,22},{22,23},{23,24},{2... | collective-permute-start | bytes 3145736 | tf_op jit(solution)/shard_map/ppermute | solution.py:321
  14.0 18.6 %collective-permute-start.4 = (f32[2,256,512]{2,1,0:T(8,128)}, f32[2,256,512]{2,1,0:T(8,128)}, u32[]{:S(2)}, u32[]{:S(2)}) collective-permute-start(f32[2,256,512]{2,1,0:T(8,128)} %copy-done.1), channel_id=1, source_target_pairs={{16,0},{32,16},{48,32},{64,48},{80,64},{96,80},{112,96},{17,1},{33... | collective-permute-start | bytes 3145736 | tf_op jit(solution)/shard_map/ppermute | solution.py:309
  25.0 27.1 %collective-permute-start.3 = (f32[2,256,512]{2,1,0:T(8,128)}, f32[2,256,512]{2,1,0:T(8,128)}, u32[]{:S(2)}, u32[]{:S(2)}) collective-permute-start(f32[2,256,512]{2,1,0:T(8,128)} %shard_map.78.refs_2_), channel_id=1, source_target_pairs={{16,17},{17,18},{18,19},{19,20},{20,21},{21,22},{22,23},{23,24},{2... | collective-permute-start | bytes 3145736 | tf_op jit(solution)/shard_map/ppermute | solution.py:321
  35.1 22.1 %collective-permute-start.7 = (f32[2,256,512]{2,1,0:T(8,128)}, f32[2,256,512]{2,1,0:T(8,128)}, u32[]{:S(2)}, u32[]{:S(2)}) collective-permute-start(f32[2,256,512]{2,1,0:T(8,128)} %shard_map.81.refs_4_), channel_id=1, source_target_pairs={{16,17},{17,18},{18,19},{19,20},{20,21},{21,22},{22,23},{23,24},{2... | collective-permute-start | bytes 3145736 | tf_op jit(solution)/shard_map/ppermute | solution.py:321
  37.0 8.3 %collective-permute-start.6 = (f32[1,256,512]{2,1,0:T(8,128)}, f32[1,256,512]{2,1,0:T(8,128)}, u32[]{:S(2)}, u32[]{:S(2)}) collective-permute-start(f32[1,256,512]{2,1,0:T(8,128)} %get-tuple-element.36), channel_id=1, source_target_pairs={{0,16},{16,0},{32,48},{48,32},{64,80},{80,64},{96,112},{112,96},{1... | collective-permute-start | bytes 1572872 | tf_op jit(solution)/shard_map/ppermute | solution.py:304
  46.5 9.7 %collective-permute-start.8 = (f32[1,64,512]{2,1,0:T(8,128)S(1)}, f32[1,64,512]{2,1,0:T(8,128)S(1)}, u32[]{:S(2)}, u32[]{:S(2)}) collective-permute-start(f32[1,64,512]{2,1,0:T(8,128)S(1)} %get-tuple-element.40), channel_id=1, source_target_pairs={{0,32},{16,48},{32,64},{48,80},{64,96},{80,112},{96,0},{112,16},{1... | collective-permute-start | bytes 393224 | tf_op jit(solution)/shard_map/ppermute | solution.py:249
  48.2 9.0 %collective-permute-start.9 = (f32[1,64,512]{2,1,0:T(8,128)S(1)}, f32[1,64,512]{2,1,0:T(8,128)S(1)}, u32[]{:S(2)}, u32[]{:S(2)}) collective-permute-start(f32[1,64,512]{2,1,0:T(8,128)S(1)} %get-tuple-element.41), channel_id=1, source_target_pairs={{0,64},{16,80},{32,96},{48,112},{64,0},{80,16},{96,32},{112,48},{1... | collective-permute-start | bytes 393224 | tf_op jit(solution)/shard_map/ppermute | solution.py:249
  65.6 11.5 %collective-permute-start.11 = (f32[2,256,512]{2,1,0:T(8,128)S(1)}, f32[2,256,512]{2,1,0:T(8,128)S(1)}, u32[]{:S(2)}, u32[]{:S(2)}) collective-permute-start(f32[2,256,512]{2,1,0:T(8,128)S(1)} %get-tuple-element.48), channel_id=1, source_target_pairs={{0,16},{16,0},{32,48},{48,32},{64,80},{80,64},{96,112},{112,96},{1... | collective-permute-start | bytes 3145736 | tf_op jit(solution)/shard_map/ppermute | solution.py:304
  67.0 19.4 %collective-permute-start.12 = (f32[2,256,512]{2,1,0:T(8,128)S(1)}, f32[2,256,512]{2,1,0:T(8,128)S(1)}, u32[]{:S(2)}, u32[]{:S(2)}) collective-permute-start(f32[2,256,512]{2,1,0:T(8,128)S(1)} %get-tuple-element.50.refs_1_.refs_3_), channel_id=1, source_target_pairs={{17,16},{18,17},{19,18},{20,19},{21,20},{22,21},{23,22},{24,23},{2... | collective-permute-start | bytes 3145736 | tf_op jit(solution)/shard_map/ppermute | solution.py:325
  74.7 26.4 %collective-permute-start.13 = (f32[2,256,512]{2,1,0:T(8,128)S(1)}, f32[2,256,512]{2,1,0:T(8,128)S(1)}, u32[]{:S(2)}, u32[]{:S(2)}) collective-permute-start(f32[2,256,512]{2,1,0:T(8,128)S(1)} %get-tuple-element.51.refs_4_.refs_1_), channel_id=1, source_target_pairs={{17,16},{18,17},{19,18},{20,19},{21,20},{22,21},{23,22},{24,23},{2... | collective-permute-start | bytes 3145736 | tf_op jit(solution)/shard_map/ppermute | solution.py:325
  77.8 9.5 %collective-permute-start.14 = (f32[2,64,512]{2,1,0:T(8,128)S(1)}, f32[2,64,512]{2,1,0:T(8,128)S(1)}, u32[]{:S(2)}, u32[]{:S(2)}) collective-permute-start(f32[2,64,512]{2,1,0:T(8,128)S(1)} %get-tuple-element.52), channel_id=1, source_target_pairs={{0,32},{16,48},{32,64},{48,80},{64,96},{80,112},{96,0},{112,16},{1... | collective-permute-start | bytes 786440 | tf_op jit(solution)/shard_map/ppermute | solution.py:249
  78.8 13.7 %collective-permute-start.15 = (f32[2,64,512]{2,1,0:T(8,128)S(1)}, f32[2,64,512]{2,1,0:T(8,128)S(1)}, u32[]{:S(2)}, u32[]{:S(2)}) collective-permute-start(f32[2,64,512]{2,1,0:T(8,128)S(1)} %get-tuple-element.53), channel_id=1, source_target_pairs={{0,64},{16,80},{32,96},{48,112},{64,0},{80,16},{96,32},{112,48},{1... | collective-permute-start | bytes 786440 | tf_op jit(solution)/shard_map/ppermute | solution.py:249
  80.9 12.1 %collective-permute-start.16 = (f32[2,64,512]{2,1,0:T(8,128)S(1)}, f32[2,64,512]{2,1,0:T(8,128)S(1)}, u32[]{:S(2)}, u32[]{:S(2)}) collective-permute-start(f32[2,64,512]{2,1,0:T(8,128)S(1)} %get-tuple-element.54), channel_id=1, source_target_pairs={{0,96},{16,112},{32,0},{48,16},{64,32},{80,48},{96,64},{112,80},{1... | collective-permute-start | bytes 786440 | tf_op jit(solution)/shard_map/ppermute | solution.py:249
  93.6 7.5 %collective-permute-start.17 = (f32[3,16,512]{2,1,0:T(8,128)S(1)}, f32[3,16,512]{2,1,0:T(8,128)S(1)}, u32[]{:S(2)}, u32[]{:S(2)}) collective-permute-start(f32[3,16,512]{2,1,0:T(8,128)S(1)} %get-tuple-element.56), channel_id=1, source_target_pairs={{0,4},{1,5},{2,6},{3,7},{4,8},{5,9},{6,10},{7,11},{8,12},{9,13},{1... | collective-permute-start | bytes 294920 | tf_op jit(solution)/shard_map/ppermute | solution.py:255
  94.2 11.3 %collective-permute-start.18 = (f32[3,16,512]{2,1,0:T(8,128)S(1)}, f32[3,16,512]{2,1,0:T(8,128)S(1)}, u32[]{:S(2)}, u32[]{:S(2)}) collective-permute-start(f32[3,16,512]{2,1,0:T(8,128)S(1)} %get-tuple-element.57), channel_id=1, source_target_pairs={{0,8},{1,9},{2,10},{3,11},{4,12},{5,13},{6,14},{7,15},{8,0},{9,1},... | collective-permute-start | bytes 294920 | tf_op jit(solution)/shard_map/ppermute | solution.py:255
  95.4 10.0 %collective-permute-start.19 = (f32[3,16,512]{2,1,0:T(8,128)S(1)}, f32[3,16,512]{2,1,0:T(8,128)S(1)}, u32[]{:S(2)}, u32[]{:S(2)}) collective-permute-start(f32[3,16,512]{2,1,0:T(8,128)S(1)} %get-tuple-element.58), channel_id=1, source_target_pairs={{0,12},{1,13},{2,14},{3,15},{4,0},{5,1},{6,2},{7,3},{8,4},{9,5},{1... | collective-permute-start | bytes 294920 | tf_op jit(solution)/shard_map/ppermute | solution.py:255
  96.6 33.2 %collective-permute-start.20 = (f32[2,256,512]{2,1,0:T(8,128)S(1)}, f32[2,256,512]{2,1,0:T(8,128)S(1)}, u32[]{:S(2)}, u32[]{:S(2)}) collective-permute-start(f32[2,256,512]{2,1,0:T(8,128)S(1)} %shard_map.90.refs_9_), channel_id=1, source_target_pairs={{0,16},{16,32},{32,48},{48,64},{64,80},{80,96},{96,112},{1,17},{17... | collective-permute-start | bytes 3145736 | tf_op jit(solution)/shard_map/ppermute | solution.py:309
  106.2 23.6 %collective-permute-start.21 = (f32[2,256,512]{2,1,0:T(8,128)S(1)}, f32[2,256,512]{2,1,0:T(8,128)S(1)}, u32[]{:S(2)}, u32[]{:S(2)}) collective-permute-start(f32[2,256,512]{2,1,0:T(8,128)S(1)} %shard_map.94.refs_6_), channel_id=1, source_target_pairs={{0,16},{16,32},{32,48},{48,64},{64,80},{80,96},{96,112},{1,17},{17... | collective-permute-start | bytes 3145736 | tf_op jit(solution)/shard_map/ppermute | solution.py:309
  110.2 8.1 %collective-permute-start.22 = (f32[3,16,512]{2,1,0:T(8,128)S(1)}, f32[3,16,512]{2,1,0:T(8,128)S(1)}, u32[]{:S(2)}, u32[]{:S(2)}) collective-permute-start(f32[3,16,512]{2,1,0:T(8,128)S(1)} %shard_map.92.refs_7_.refs_1_), channel_id=1, source_target_pairs={{0,1},{1,2},{2,3},{3,0},{4,5},{5,6},{6,7},{7,4},{8,9},{9,10},{10,1... | collective-permute-start | bytes 294920 | tf_op jit(solution)/shard_map/ppermute | solution.py:255
  127.4 6.5 %collective-permute-start.30 = (f32[4,2,16,512]{3,2,1,0:T(8,128)S(1)}, f32[4,2,16,512]{3,2,1,0:T(8,128)S(1)}, u32[]{:S(2)}, u32[]{:S(2)}) collective-permute-start(f32[4,2,16,512]{3,2,1,0:T(8,128)S(1)} %shard_map.97.refs_1_), channel_id=1, source_target_pairs={{0,96},{16,112},{32,0},{48,16},{64,32},{80,48},{96,64},{112,80},{1... | collective-permute-start | bytes 786440 | tf_op jit(solution)/shard_map/ppermute | solution.py:249
  127.5 8.1 %collective-permute-start.29 = (f32[4,2,16,512]{3,2,1,0:T(8,128)S(1)}, f32[4,2,16,512]{3,2,1,0:T(8,128)S(1)}, u32[]{:S(2)}, u32[]{:S(2)}) collective-permute-start(f32[4,2,16,512]{3,2,1,0:T(8,128)S(1)} %shard_map.97.refs_1_), channel_id=1, source_target_pairs={{0,64},{16,80},{32,96},{48,112},{64,0},{80,16},{96,32},{112,48},{1... | collective-permute-start | bytes 786440 | tf_op jit(solution)/shard_map/ppermute | solution.py:249
  129.0 13.8 %collective-permute-start.28 = (f32[4,2,16,512]{3,2,1,0:T(8,128)S(1)}, f32[4,2,16,512]{3,2,1,0:T(8,128)S(1)}, u32[]{:S(2)}, u32[]{:S(2)}) collective-permute-start(f32[4,2,16,512]{3,2,1,0:T(8,128)S(1)} %shard_map.97.refs_1_), channel_id=1, source_target_pairs={{0,32},{16,48},{32,64},{48,80},{64,96},{80,112},{96,0},{112,16},{1... | collective-permute-start | bytes 786440 | tf_op jit(solution)/shard_map/ppermute | solution.py:249
  (21 other events, 96.2 us)
